TPU v7x, 512 devices: a whole 4x4x16 slice. The times are simulated.
512 devices in a mesh: seq: 16 (over x, y_lo, core), fsdp: 16 (over z), batch: 2 (over y_hi).
Axes of the slice: x: 4, y: 4 (y_hi: 2, y_lo: 2; y = y_hi * 2 + y_lo), z: 16, core: 2. Of those that a mesh axis runs over, the one named last changes fastest.
Arguments:
- ssm_input: bfloat16 [49152, 8192], P(('batch', 'seq', 'fsdp')), parts along dimension 0, may hold values from -6 to 6
- gate_input: bfloat16 [49152, 8192], P(('batch', 'seq', 'fsdp')), parts along dimension 0, may hold values from -6 to 6
- coupling: bfloat16 [49152, 2048], P(('batch', 'seq', 'fsdp')), parts along dimension 0, may hold values from -6 to 6
- step_input: bfloat16 [49152, 128], P(('batch', 'seq', 'fsdp')), parts along dimension 0, may hold values from -4 to 4
- conv_input: bfloat16 [4, 8192], P(None, 'fsdp'), may hold values from -3 to 3
- conv_coupling: bfloat16 [4, 2048], P(None, 'fsdp'), may hold values from -3 to 3
- step_bias: float32 [128], P('fsdp'), may hold values from -8 to 1.1
- log_rate: float32 [128], P('fsdp'), may hold values from -6 to -3.2
- skip_gain: float32 [128], P('fsdp'), may hold values from 0.5 to 1.5
- norm_gain: bfloat16 [8192], replicated, may hold values from 0.5 to 1.5
Outputs:
- layer_out: bfloat16 [49152, 8192], P(('batch', 'seq', 'fsdp')), parts along dimension 0
There are 2 independent parts, one for each index of `batch`. A program takes and returns all parts, laid end to end along the dimension named above; an argument that names none is the same for every part. Nothing has to cross between parts.
All inputs are finite; a program needn't handle non-finite values.
Results may differ from a plain program's by a relative error of at most 0.0051.
Values may be sent and summed in bfloat16 or wider, within the bound.
No kernel may reach another device: no remote copies, remote signals or barrier semaphores. Data moves between devices by JAX's collectives and lax.ppermute only.
A program may use at most 64 MiB of HBM per device.

v0:
```python
import jax
import jax.numpy as jnp
from jax import lax
from jax.sharding import PartitionSpec as P

HEAD_DIM = 64
STATE = 256
GROUP_HEADS = 32
GROUPS = 4


precise = lax.Precision.HIGHEST


def shifted(block, axis, distance):
    devices = range(lax.axis_size(axis))
    route = [(i - distance, i) for i in devices if i - distance in devices]
    return lax.ppermute(block, axis, route)


def conv_block(raw_rows, tail_rows, weights):
    extended = jnp.concatenate([tail_rows, raw_rows], axis=0).astype(jnp.float32)
    weights_wide = weights.astype(jnp.float32)
    kernel_len = weights.shape[0]
    row_count = raw_rows.shape[0]
    summed = extended[0:row_count] * weights_wide[0][None, :]
    for offset in range(1, kernel_len):
        summed = summed + extended[offset : offset + row_count] * weights_wide[offset][None, :]
    return jax.nn.silu(summed).astype(jnp.bfloat16)


def scan_block(carried, inputs, read_in, read_out, step_sizes, decay_rate, skip_gain, group_span):
    log_decay = -decay_rate[None, :] * step_sizes
    cumulated = jnp.cumsum(log_decay, axis=0)
    intersection = jnp.einsum("ign,jgn->gij", read_out, read_in, precision=precise)
    intersection = jnp.repeat(intersection, group_span, axis=0)
    gap_log = cumulated.T[:, :, None] - cumulated.T[:, None, :]
    length = inputs.shape[0]
    lower_mask = (jnp.arange(length)[:, None] >= jnp.arange(length)[None, :])[None]
    decay_mat = jnp.where(lower_mask, jnp.exp(jnp.where(lower_mask, gap_log, 0.0)), 0.0)
    mixing = intersection * decay_mat * step_sizes.T[:, None, :]
    intra_out = jnp.einsum("hij,jhp->ihp", mixing, inputs, precision=precise)
    heads_out = jnp.repeat(read_out, group_span, axis=1)
    carry_out = jnp.exp(cumulated)[:, :, None] * jnp.einsum(
        "ihn,hpn->ihp", heads_out, carried, precision=precise
    )
    heads_in = jnp.repeat(read_in, group_span, axis=1)
    weight_end = jnp.exp(cumulated[-1][None, :] - cumulated) * step_sizes
    updated = jnp.exp(cumulated[-1])[:, None, None] * carried + jnp.einsum(
        "jhp,jhn->hpn", inputs * weight_end[:, :, None], heads_in, precision=precise
    )
    return (updated, intra_out + carry_out + skip_gain[None, :, None] * inputs, cumulated)


def finish_norm(mixed_rows, gate_rows, gain_row):
    gated = mixed_rows.astype(jnp.float32) * jax.nn.silu(gate_rows.astype(jnp.float32))
    row_count = gated.shape[0]
    grouped = gated.reshape(row_count, GROUPS, -1)
    inv_scale = lax.rsqrt(jnp.mean(grouped * grouped, axis=-1, keepdims=True) + 1e-05)
    normed = (grouped * inv_scale).reshape(row_count, -1)
    return (normed * gain_row.astype(jnp.float32)[None, :]).astype(jnp.bfloat16)


def local(
    ssm_input,
    gate_input,
    coupling,
    step_input,
    conv_input,
    conv_coupling,
    step_bias,
    log_rate,
    skip_gain,
    norm_gain,
):
    kernel_len = conv_input.shape[0]
    kernel_inputs, kernel_coupling = (
        lax.all_gather(conv_input, "fsdp", axis=1, tiled=True),
        lax.all_gather(conv_coupling, "fsdp", axis=1, tiled=True),
    )
    tok_rows = ssm_input.shape[0]
    tail_inputs, tail_coupling = shifted(
        (ssm_input[tok_rows - (kernel_len - 1) :], coupling[tok_rows - (kernel_len - 1) :]),
        ("seq", "fsdp"),
        1,
    )
    conv_inputs = conv_block(ssm_input, tail_inputs, kernel_inputs)
    conv_rows = conv_block(coupling, tail_coupling, kernel_coupling)
    heads_here = step_bias.shape[0]
    group_span = min(heads_here, GROUP_HEADS)
    groups_here = heads_here // group_span
    pair_width = GROUPS * STATE
    paired = jnp.concatenate(
        [
            conv_rows[:, :pair_width].reshape(tok_rows, GROUPS, STATE),
            conv_rows[:, pair_width:].reshape(tok_rows, GROUPS, STATE),
        ],
        axis=2,
    )
    local_inputs, local_steps = (
        lax.all_to_all(conv_inputs, "fsdp", split_axis=1, concat_axis=0, tiled=True),
        lax.all_to_all(step_input, "fsdp", split_axis=1, concat_axis=0, tiled=True),
    )
    whole_coupling = lax.all_gather(
        paired.reshape(tok_rows, 2 * pair_width), "fsdp", axis=0, tiled=True
    )
    section_rows = whole_coupling.shape[0]
    first_group = lax.axis_index("fsdp") * heads_here // GROUP_HEADS
    local_coupling = lax.dynamic_slice_in_dim(
        whole_coupling.reshape(section_rows, GROUPS, 2 * STATE), first_group, groups_here, 1
    )
    section_len = local_inputs.shape[0]
    block_len = min(512, section_len)
    block_count = section_len // block_len
    input_blocks = local_inputs.reshape(block_count, block_len, heads_here, HEAD_DIM)
    in_blocks = local_coupling[:, :, :STATE].reshape(block_count, block_len, groups_here, STATE)
    out_blocks = local_coupling[:, :, STATE:].reshape(block_count, block_len, groups_here, STATE)
    step_sizes = jax.nn.softplus(local_steps.astype(jnp.float32) + step_bias[None, :])
    step_blocks = step_sizes.reshape(block_count, block_len, heads_here)
    decay_rate = jnp.exp(log_rate)

    def advance(carried, pieces):
        block_inputs, block_in, block_out, block_steps = pieces
        updated, mixed_out, cumulated = scan_block(
            carried,
            block_inputs.astype(jnp.float32),
            block_in.astype(jnp.float32),
            block_out.astype(jnp.float32),
            block_steps,
            decay_rate,
            skip_gain,
            group_span,
        )
        return (updated, (mixed_out, cumulated))

    zero_state = jnp.zeros((heads_here, HEAD_DIM, STATE), jnp.float32)
    section_state, (mixed_out, cumulated) = lax.scan(
        advance, zero_state, (input_blocks, in_blocks, out_blocks, step_blocks)
    )
    block_sums = cumulated[:, -1, :]
    offsets = jnp.cumsum(block_sums, axis=0) - block_sums
    through = cumulated + offsets[:, None, :]
    section_decay = jnp.exp(jnp.sum(block_sums, axis=0))

    def relay(turn_index, incoming):
        outgoing = section_decay[:, None, None] * incoming + section_state
        return shifted(outgoing, "seq", 1)

    incoming = lax.fori_loop(0, lax.axis_size("seq") - 1, relay, zero_state)
    heads_read = jnp.repeat(out_blocks.astype(jnp.float32), group_span, axis=2)
    carried_in = jnp.exp(through)[..., None] * jnp.einsum(
        "bihn,hpn->bihp", heads_read, incoming, precision=precise
    )
    section_out = (
        (mixed_out + carried_in).reshape(section_len, heads_here * HEAD_DIM).astype(jnp.bfloat16)
    )
    token_out = lax.all_to_all(section_out, "fsdp", split_axis=0, concat_axis=1, tiled=True)
    return finish_norm(token_out, gate_input, norm_gain)


def solution(mesh):
    return jax.shard_map(
        local,
        mesh=mesh,
        in_specs=(
            P(("batch", "seq", "fsdp"), None),
            P(("batch", "seq", "fsdp"), None),
            P(("batch", "seq", "fsdp"), None),
            P(("batch", "seq", "fsdp"), None),
            P(None, "fsdp"),
            P(None, "fsdp"),
            P("fsdp"),
            P("fsdp"),
            P("fsdp"),
            P(),
        ),
        out_specs=P(("batch", "seq", "fsdp"), None),
        check_vma=False,
    )
```

profile of v0, /device:TPU:6, one launch (start us, length us, event | category | flops | bytes accessed | tf_op | source)
XLA Modules:
  0.0 568.2 jit_solution(8222290422905758179)
XLA Ops:
  7.3 3.8 collective-permute-start.2
  11.1 33.8 %all_gather.10 = bf16[4,2048]{1,0:T(4,128)(2,1)S(1)} all-gather(bf16[4,128]{1,0:T(4,128)(2,1)} %param.19), channel_id=1, replica_groups=mesh['seq'=16,'fsdp'=16,'batch'=2] {'fsdp'}, dimensions={1}, use_global_device_ids=true | all-gather | bytes 17408 | tf_op jit(solution)/shard_map/all_gather | solution.py:79
  48.0 2.7 collective-permute-start.1
  51.4 8.7 %all-to-all-start = ((bf16[96,16,8]{0,2,1:T(8,128)(2,1)}), bf16[96,16,8]{0,2,1:T(8,128)(2,1)S(1)}, u32[]{:S(2)}, u32[]{:S(2)}) async-start(bf16[96,16,8]{0,2,1:T(8,128)(2,1)} %bitcast.1), calls=%async_computation | async-start | bytes 65536 | tf_op jit(solution)/shard_map/all_to_all | solution.py:102
  60.1 30.3 %all_gather.9 = bf16[4,8192]{1,0:T(4,128)(2,1)S(1)} all-gather(bf16[4,512]{1,0:T(4,128)(2,1)S(1)} %copy-done.7), channel_id=1, replica_groups=mesh['seq'=16,'fsdp'=16,'batch'=2] {'fsdp'}, dimensions={1}, use_global_device_ids=true | all-gather | bytes 69632 | tf_op jit(solution)/shard_map/all_gather | solution.py:78
  94.3 8.8 %all-to-all-start.1 = ((bf16[96,16,512]{2,0,1:T(8,128)(2,1)}), bf16[96,16,512]{2,0,1:T(8,128)(2,1)S(1)}, u32[]{:S(2)}, u32[]{:S(2)}) async-start(bf16[96,16,512]{2,0,1:T(8,128)(2,1)} %bitcast.107), calls=%async_computation.1 | async-start | bytes 3145728 | tf_op jit(solution)/shard_map/all_to_all | solution.py:101
  103.5 82.6 %all-to-all-done.1 = bf16[96,16,512]{2,0,1:T(8,128)(2,1)S(1)} async-done(((bf16[96,16,512]{2,0,1:T(8,128)(2,1)}), bf16[96,16,512]{2,0,1:T(8,128)(2,1)S(1)}, u32[]{:S(2)}, u32[]{:S(2)}) %all-to-all-start.1) | async-done | bytes 1572896 | tf_op jit(solution)/shard_map/all_to_all | solution.py:101
  186.1 3.1 reshape.199
  189.2 3.8 copy.94
  193.0 7.3 %all-gather.2.cloned.1.call-done = bf16[1536,2048]{1,0:T(8,128)(2,1)} async-done(((bf16[96,2048]{1,0:T(8,128)(2,1)}), bf16[1536,2048]{1,0:T(8,128)(2,1)}) %all-gather.2.cloned.1.call-update) | async-done | bytes 6291472 | tf_op jit(solution)/shard_map/all_gather | solution.py:104
  200.3 8.7 %copy.89 = bf16[1536,2048]{0,1:T(8,128)(2,1)} copy(bf16[1536,2048]{1,0:T(8,128)(2,1)} %all-gather.2.cloned.1.call-done) | data formatting | bytes 12582912 | tf_op jit(solution)/shard_map/all_gather | solution.py:104
  208.9 2.4 constant_dynamic-slice_fusion.2
  211.3 2.6 copy.90
  215.0 62.3 %while.28 = (s32[]{:T(128)}, f32[8,64,256]{2,1,0:T(8,128)S(1)}, f32[3,512,8,64]{1,3,0,2:T(8,128)}, f32[3,512,8]{1,2,0:T(8,128)S(1)}, f32[1,8]{1,0:T(1,128)S(1)},...) while((s32[]{:T(128)}, f32[8,64,256]{2,1,0:T(8,128)S(1)}, ...), condition=%wide.region_3.4_spmd.clone, body=%wide.region_0.3_spmd.clone.sunk | while | flops 3369357312 | bytes 12440996 | solution.py:137
  218.0 7.7 %fusion.108 = f32[512,8,64]{0,2,1:T(8,128)} fusion(f32[8,512]{1,0:T(8,128)S(1)} %bitcast.150, f32[8,512]{1,0:T(8,128)S(1)} %add_bitcast_fusion.4, f32[512,512]{1,0:T(8,128)S(1)} %fusion.107, pred[512,512]{1,0:T(8,128)(4,1)S(1)} %iota_compare_fusion.2, bf16[3,512,8,64]{1,3,2,0:T(8,128)(2,1)S(1)} %get-tuple-element.402, s32[]{:T(128)} %get-tuple-element.383), kind=kOutput, calls=%fused_computation.24.clone.1 | convolution fusion | flops 1621098496 | bytes 2932740 | tf_op jit(solution)/shard_map/while/body/eval_jaxpr/hij,jhp->ihp/dot_general | solution.py:42
  226.8 6.2 %fusion.109 = f32[3,512,8,64]{1,3,0,2:T(8,128)} fusion(f32[3,512,8,64]{1,3,0,2:T(8,128)} %get-tuple-element.385, s32[]{:T(128)} %get-tuple-element.383, f32[512,8,64]{0,2,1:T(8,128)} %fusion.108, f32[512,256]{1,0:T(8,128)S(1)} %get-tuple-element.368, f32[8]{0:T(128)S(1)} %get-tuple-element.405, f32[512,8]{0,1:T(8,128)S(1)} %get-tuple-element.369, ...), kind=kOutput, calls=%fused_computation.23.clone.1 | convolution fusion | flops 806748160 | bytes 3686945 | tf_op jit(solution)/shard_map/while/body/eval_jaxpr/ihn,hpn->ihp/dot_general | solution.py:44
  233.3 2.4 fusion.106
  238.7 7.7 %fusion.108 = f32[512,8,64]{0,2,1:T(8,128)} fusion(f32[8,512]{1,0:T(8,128)S(1)} %bitcast.150, f32[8,512]{1,0:T(8,128)S(1)} %add_bitcast_fusion.4, f32[512,512]{1,0:T(8,128)S(1)} %fusion.107, pred[512,512]{1,0:T(8,128)(4,1)S(1)} %iota_compare_fusion.2, bf16[3,512,8,64]{1,3,2,0:T(8,128)(2,1)S(1)} %get-tuple-element.402, s32[]{:T(128)} %get-tuple-element.383), kind=kOutput, calls=%fused_computation.24.clone.1 | convolution fusion | flops 1621098496 | bytes 2932740 | tf_op jit(solution)/shard_map/while/body/eval_jaxpr/hij,jhp->ihp/dot_general | solution.py:42
  247.6 6.2 %fusion.109 = f32[3,512,8,64]{1,3,0,2:T(8,128)} fusion(f32[3,512,8,64]{1,3,0,2:T(8,128)} %get-tuple-element.385, s32[]{:T(128)} %get-tuple-element.383, f32[512,8,64]{0,2,1:T(8,128)} %fusion.108, f32[512,256]{1,0:T(8,128)S(1)} %get-tuple-element.368, f32[8]{0:T(128)S(1)} %get-tuple-element.405, f32[512,8]{0,1:T(8,128)S(1)} %get-tuple-element.369, ...), kind=kOutput, calls=%fused_computation.23.clone.1 | convolution fusion | flops 806748160 | bytes 3686945 | tf_op jit(solution)/shard_map/while/body/eval_jaxpr/ihn,hpn->ihp/dot_general | solution.py:44
  254.1 2.4 fusion.106
  259.5 7.7 %fusion.108 = f32[512,8,64]{0,2,1:T(8,128)} fusion(f32[8,512]{1,0:T(8,128)S(1)} %bitcast.150, f32[8,512]{1,0:T(8,128)S(1)} %add_bitcast_fusion.4, f32[512,512]{1,0:T(8,128)S(1)} %fusion.107, pred[512,512]{1,0:T(8,128)(4,1)S(1)} %iota_compare_fusion.2, bf16[3,512,8,64]{1,3,2,0:T(8,128)(2,1)S(1)} %get-tuple-element.402, s32[]{:T(128)} %get-tuple-element.383), kind=kOutput, calls=%fused_computation.24.clone.1 | convolution fusion | flops 1621098496 | bytes 2932740 | tf_op jit(solution)/shard_map/while/body/eval_jaxpr/hij,jhp->ihp/dot_general | solution.py:42
  268.4 6.2 %fusion.109 = f32[3,512,8,64]{1,3,0,2:T(8,128)} fusion(f32[3,512,8,64]{1,3,0,2:T(8,128)} %get-tuple-element.385, s32[]{:T(128)} %get-tuple-element.383, f32[512,8,64]{0,2,1:T(8,128)} %fusion.108, f32[512,256]{1,0:T(8,128)S(1)} %get-tuple-element.368, f32[8]{0:T(128)S(1)} %get-tuple-element.405, f32[512,8]{0,1:T(8,128)S(1)} %get-tuple-element.369, ...), kind=kOutput, calls=%fused_computation.23.clone.1 | convolution fusion | flops 806748160 | bytes 3686945 | tf_op jit(solution)/shard_map/while/body/eval_jaxpr/ihn,hpn->ihp/dot_general | solution.py:44
  274.9 2.4 fusion.106
  279.3 172.8 %while.27 = (s32[]{:T(128)}, f32[8,64,256]{2,1,0:T(8,128)S(1)}, f32[8]{0:T(128)S(1)}, f32[8,64,256]{2,1,0:T(8,128)S(1)}, s32[]{:T(128)}) while((s32[]{:T(128)}, f32[8,64,256]{2,1,0:T(8,128)S(1)}, f32[8]{0:T(128)S(1)}, f32[8,64,256]{2,1,0:T(8,128)S(1)}, s32[]{:T(128)}) %tuple.64), condition=%wide.region_7.8_spmd, body=%wide.region_6.7_spmd.sunk | while | flops 262146 | bytes 3670149 | solution.py:149
  281.3 9.5 %collective-permute-done = f32[8,64,256]{2,1,0:T(8,128)S(1)} collective-permute-done((f32[8,64,256]{2,1,0:T(8,128)S(1)}, f32[8,64,256]{2,1,0:T(8,128)S(1)}, u32[]{:S(2)}, u32[]{:S(2)}) %collective-permute-start) | collective-permute-done | bytes 524320 | tf_op jit(solution)/shard_map/while/body/eval_jaxpr/ppermute | solution.py:18
  292.9 9.5 %collective-permute-done = f32[8,64,256]{2,1,0:T(8,128)S(1)} collective-permute-done((f32[8,64,256]{2,1,0:T(8,128)S(1)}, f32[8,64,256]{2,1,0:T(8,128)S(1)}, u32[]{:S(2)}, u32[]{:S(2)}) %collective-permute-start) | collective-permute-done | bytes 524320 | tf_op jit(solution)/shard_map/while/body/eval_jaxpr/ppermute | solution.py:18
  304.4 9.5 %collective-permute-done = f32[8,64,256]{2,1,0:T(8,128)S(1)} collective-permute-done((f32[8,64,256]{2,1,0:T(8,128)S(1)}, f32[8,64,256]{2,1,0:T(8,128)S(1)}, u32[]{:S(2)}, u32[]{:S(2)}) %collective-permute-start) | collective-permute-done | bytes 524320 | tf_op jit(solution)/shard_map/while/body/eval_jaxpr/ppermute | solution.py:18
  315.9 9.5 %collective-permute-done = f32[8,64,256]{2,1,0:T(8,128)S(1)} collective-permute-done((f32[8,64,256]{2,1,0:T(8,128)S(1)}, f32[8,64,256]{2,1,0:T(8,128)S(1)}, u32[]{:S(2)}, u32[]{:S(2)}) %collective-permute-start) | collective-permute-done | bytes 524320 | tf_op jit(solution)/shard_map/while/body/eval_jaxpr/ppermute | solution.py:18
  327.4 9.5 %collective-permute-done = f32[8,64,256]{2,1,0:T(8,128)S(1)} collective-permute-done((f32[8,64,256]{2,1,0:T(8,128)S(1)}, f32[8,64,256]{2,1,0:T(8,128)S(1)}, u32[]{:S(2)}, u32[]{:S(2)}) %collective-permute-start) | collective-permute-done | bytes 524320 | tf_op jit(solution)/shard_map/while/body/eval_jaxpr/ppermute | solution.py:18
  338.9 9.5 %collective-permute-done = f32[8,64,256]{2,1,0:T(8,128)S(1)} collective-permute-done((f32[8,64,256]{2,1,0:T(8,128)S(1)}, f32[8,64,256]{2,1,0:T(8,128)S(1)}, u32[]{:S(2)}, u32[]{:S(2)}) %collective-permute-start) | collective-permute-done | bytes 524320 | tf_op jit(solution)/shard_map/while/body/eval_jaxpr/ppermute | solution.py:18
  350.5 9.5 %collective-permute-done = f32[8,64,256]{2,1,0:T(8,128)S(1)} collective-permute-done((f32[8,64,256]{2,1,0:T(8,128)S(1)}, f32[8,64,256]{2,1,0:T(8,128)S(1)}, u32[]{:S(2)}, u32[]{:S(2)}) %collective-permute-start) | collective-permute-done | bytes 524320 | tf_op jit(solution)/shard_map/while/body/eval_jaxpr/ppermute | solution.py:18
  362.0 9.5 %collective-permute-done = f32[8,64,256]{2,1,0:T(8,128)S(1)} collective-permute-done((f32[8,64,256]{2,1,0:T(8,128)S(1)}, f32[8,64,256]{2,1,0:T(8,128)S(1)}, u32[]{:S(2)}, u32[]{:S(2)}) %collective-permute-start) | collective-permute-done | bytes 524320 | tf_op jit(solution)/shard_map/while/body/eval_jaxpr/ppermute | solution.py:18
  373.5 9.5 %collective-permute-done = f32[8,64,256]{2,1,0:T(8,128)S(1)} collective-permute-done((f32[8,64,256]{2,1,0:T(8,128)S(1)}, f32[8,64,256]{2,1,0:T(8,128)S(1)}, u32[]{:S(2)}, u32[]{:S(2)}) %collective-permute-start) | collective-permute-done | bytes 524320 | tf_op jit(solution)/shard_map/while/body/eval_jaxpr/ppermute | solution.py:18
  385.0 9.5 %collective-permute-done = f32[8,64,256]{2,1,0:T(8,128)S(1)} collective-permute-done((f32[8,64,256]{2,1,0:T(8,128)S(1)}, f32[8,64,256]{2,1,0:T(8,128)S(1)}, u32[]{:S(2)}, u32[]{:S(2)}) %collective-permute-start) | collective-permute-done | bytes 524320 | tf_op jit(solution)/shard_map/while/body/eval_jaxpr/ppermute | solution.py:18
  396.5 9.5 %collective-permute-done = f32[8,64,256]{2,1,0:T(8,128)S(1)} collective-permute-done((f32[8,64,256]{2,1,0:T(8,128)S(1)}, f32[8,64,256]{2,1,0:T(8,128)S(1)}, u32[]{:S(2)}, u32[]{:S(2)}) %collective-permute-start) | collective-permute-done | bytes 524320 | tf_op jit(solution)/shard_map/while/body/eval_jaxpr/ppermute | solution.py:18
  408.1 9.5 %collective-permute-done = f32[8,64,256]{2,1,0:T(8,128)S(1)} collective-permute-done((f32[8,64,256]{2,1,0:T(8,128)S(1)}, f32[8,64,256]{2,1,0:T(8,128)S(1)}, u32[]{:S(2)}, u32[]{:S(2)}) %collective-permute-start) | collective-permute-done | bytes 524320 | tf_op jit(solution)/shard_map/while/body/eval_jaxpr/ppermute | solution.py:18
  419.6 9.5 %collective-permute-done = f32[8,64,256]{2,1,0:T(8,128)S(1)} collective-permute-done((f32[8,64,256]{2,1,0:T(8,128)S(1)}, f32[8,64,256]{2,1,0:T(8,128)S(1)}, u32[]{:S(2)}, u32[]{:S(2)}) %collective-permute-start) | collective-permute-done | bytes 524320 | tf_op jit(solution)/shard_map/while/body/eval_jaxpr/ppermute | solution.py:18
  431.1 9.5 %collective-permute-done = f32[8,64,256]{2,1,0:T(8,128)S(1)} collective-permute-done((f32[8,64,256]{2,1,0:T(8,128)S(1)}, f32[8,64,256]{2,1,0:T(8,128)S(1)}, u32[]{:S(2)}, u32[]{:S(2)}) %collective-permute-start) | collective-permute-done | bytes 524320 | tf_op jit(solution)/shard_map/while/body/eval_jaxpr/ppermute | solution.py:18
  442.6 9.5 %collective-permute-done = f32[8,64,256]{2,1,0:T(8,128)S(1)} collective-permute-done((f32[8,64,256]{2,1,0:T(8,128)S(1)}, f32[8,64,256]{2,1,0:T(8,128)S(1)}, u32[]{:S(2)}, u32[]{:S(2)}) %collective-permute-start) | collective-permute-done | bytes 524320 | tf_op jit(solution)/shard_map/while/body/eval_jaxpr/ppermute | solution.py:18
  452.1 14.0 %fusion.70 = bf16[3,512,8,64]{1,3,0,2:T(8,128)(2,1)} fusion(f32[3,512,8,64]{1,3,0,2:T(8,128)} %get-tuple-element.145, f32[3,512,256]{2,1,0:T(8,128)S(1)} %bitcast.142, f32[3,512,8]{1,0,2:T(4,128)S(1)} %copy.97, f32[8,64,256]{2,1,0:T(8,128)S(1)} %get-tuple-element.148), kind=kOutput, calls=%fused_computation.76 | convolution fusion | flops 2418278400 | bytes 6864896 | tf_op jit(solution)/shard_map/bihn,hpn->bihp/dot_general | solution.py:151
  466.1 3.7 copy.108
  469.8 2.9 reshape.200
  472.6 7.6 %all-to-all-start.2 = ((bf16[16,96,512]{2,1,0:T(8,128)(2,1)}), bf16[16,96,512]{2,1,0:T(8,128)(2,1)S(1)}, u32[]{:S(2)}, u32[]{:S(2)}) async-start(bf16[16,96,512]{2,1,0:T(8,128)(2,1)} %reshape.200), calls=%async_computation.2 | async-start | bytes 3145728 | tf_op jit(solution)/shard_map/all_to_all | solution.py:157
  480.3 64.1 %all-to-all-done.2 = bf16[16,96,512]{2,1,0:T(8,128)(2,1)S(1)} async-done(((bf16[16,96,512]{2,1,0:T(8,128)(2,1)}), bf16[16,96,512]{2,1,0:T(8,128)(2,1)S(1)}, u32[]{:S(2)}, u32[]{:S(2)}) %all-to-all-start.2) | async-done | bytes 1572896 | tf_op jit(solution)/shard_map/all_to_all | solution.py:157
  546.2 2.5 fusion.78
  548.7 5.3 mul.257
  554.0 2.4 reduce_sum.19
  556.9 2.2 copy.119
  (140 shorter events, 60.1 us)
Async XLA Ops:
  6.5 193.7 %all-gather.2.cloned.1.call-start = ((), (), s32[]{:S(2)}) async-start(), calls=%async_computation.3 | async-start | bytes 6684672 | tf_op jit(solution)/shard_map/all_gather | solution.py:104
  7.3 37.6 %collective-permute-start.2 = (bf16[3,2048]{1,0:T(4,128)(2,1)S(1)}, bf16[3,2048]{1,0:T(4,128)(2,1)S(1)}, u32[]{:S(2)}, u32[]{:S(2)}) collective-permute-start(bf16[3,2048]{1,0:T(4,128)(2,1)S(1)} %slice.94), channel_id=1, source_target_pairs={{0,2},{2,4},{4,6},{6,8},{8,10},{10,12},{12,14},{14,16},{16,18},{18... | collective-permute-start | bytes 36872 | tf_op jit(solution)/shard_map/ppermute | solution.py:18
  46.1 1.9 copy-start.3
  46.1 4.6 copy-start.4
  46.1 14.0 %copy-start.7 = (bf16[4,512]{1,0:T(4,128)(2,1)S(1)}, bf16[4,512]{1,0:T(4,128)(2,1)}, u32[]{:S(2)}) copy-start(bf16[4,512]{1,0:T(4,128)(2,1)} %param.18) | copy-start | bytes 12292
  48.0 42.5 %collective-permute-start.1 = (bf16[3,8192]{1,0:T(4,128)(2,1)S(1)}, bf16[3,8192]{1,0:T(4,128)(2,1)S(1)}, u32[]{:S(2)}, u32[]{:S(2)}) collective-permute-start(bf16[3,8192]{1,0:T(4,128)(2,1)S(1)} %slice.85), channel_id=1, source_target_pairs={{0,2},{2,4},{4,6},{6,8},{8,10},{10,12},{12,14},{14,16},{16,18},{18... | collective-permute-start | bytes 147464 | tf_op jit(solution)/shard_map/ppermute | solution.py:18
  51.4 42.9 %all-to-all-start = ((bf16[96,16,8]{0,2,1:T(8,128)(2,1)}), bf16[96,16,8]{0,2,1:T(8,128)(2,1)S(1)}, u32[]{:S(2)}, u32[]{:S(2)}) async-start(bf16[96,16,8]{0,2,1:T(8,128)(2,1)} %bitcast.1), calls=%async_computation | async-start | bytes 65536 | tf_op jit(solution)/shard_map/all_to_all | solution.py:102
  92.9 10.3 %copy-start.9 = (f32[8]{0:T(128)S(1)}, f32[8]{0:T(128)}, u32[]{:S(2)}) copy-start(f32[8]{0:T(128)} %param.21) | copy-start | bytes 100
  92.9 10.4 %copy-start.8 = (f32[8]{0:T(128)S(1)}, f32[8]{0:T(128)}, u32[]{:S(2)}) copy-start(f32[8]{0:T(128)} %param.20) | copy-start | bytes 100
  94.3 91.9 %all-to-all-start.1 = ((bf16[96,16,512]{2,0,1:T(8,128)(2,1)}), bf16[96,16,512]{2,0,1:T(8,128)(2,1)S(1)}, u32[]{:S(2)}, u32[]{:S(2)}) async-start(bf16[96,16,512]{2,0,1:T(8,128)(2,1)} %bitcast.107), calls=%async_computation.1 | async-start | bytes 3145728 | tf_op jit(solution)/shard_map/all_to_all | solution.py:101
  208.9 6.1 %copy-start.6 = (f32[8]{0:T(128)S(1)}, f32[8]{0:T(128)}, u32[]{:S(2)}) copy-start(f32[8]{0:T(128)} %param.22) | copy-start | bytes 100
  211.3 3.8 copy-start
  279.4 11.4 %collective-permute-start = (f32[8,64,256]{2,1,0:T(8,128)S(1)}, f32[8,64,256]{2,1,0:T(8,128)S(1)}, u32[]{:S(2)}, u32[]{:S(2)}) collective-permute-start(f32[8,64,256]{2,1,0:T(8,128)S(1)} %multiply_add_fusion.2), channel_id=1, source_target_pairs={{0,32},{32,64},{64,96},{96,128},{128,160},{160,192},{192,224},{224... | collective-permute-start | bytes 1572872 | tf_op jit(solution)/shard_map/while/body/eval_jaxpr/ppermute | solution.py:18
  290.9 11.4 %collective-permute-start = (f32[8,64,256]{2,1,0:T(8,128)S(1)}, f32[8,64,256]{2,1,0:T(8,128)S(1)}, u32[]{:S(2)}, u32[]{:S(2)}) collective-permute-start(f32[8,64,256]{2,1,0:T(8,128)S(1)} %multiply_add_fusion.2), channel_id=1, source_target_pairs={{0,32},{32,64},{64,96},{96,128},{128,160},{160,192},{192,224},{224... | collective-permute-start | bytes 1572872 | tf_op jit(solution)/shard_map/while/body/eval_jaxpr/ppermute | solution.py:18
  302.4 11.4 %collective-permute-start = (f32[8,64,256]{2,1,0:T(8,128)S(1)}, f32[8,64,256]{2,1,0:T(8,128)S(1)}, u32[]{:S(2)}, u32[]{:S(2)}) collective-permute-start(f32[8,64,256]{2,1,0:T(8,128)S(1)} %multiply_add_fusion.2), channel_id=1, source_target_pairs={{0,32},{32,64},{64,96},{96,128},{128,160},{160,192},{192,224},{224... | collective-permute-start | bytes 1572872 | tf_op jit(solution)/shard_map/while/body/eval_jaxpr/ppermute | solution.py:18
  314.0 11.4 %collective-permute-start = (f32[8,64,256]{2,1,0:T(8,128)S(1)}, f32[8,64,256]{2,1,0:T(8,128)S(1)}, u32[]{:S(2)}, u32[]{:S(2)}) collective-permute-start(f32[8,64,256]{2,1,0:T(8,128)S(1)} %multiply_add_fusion.2), channel_id=1, source_target_pairs={{0,32},{32,64},{64,96},{96,128},{128,160},{160,192},{192,224},{224... | collective-permute-start | bytes 1572872 | tf_op jit(solution)/shard_map/while/body/eval_jaxpr/ppermute | solution.py:18
  325.5 11.4 %collective-permute-start = (f32[8,64,256]{2,1,0:T(8,128)S(1)}, f32[8,64,256]{2,1,0:T(8,128)S(1)}, u32[]{:S(2)}, u32[]{:S(2)}) collective-permute-start(f32[8,64,256]{2,1,0:T(8,128)S(1)} %multiply_add_fusion.2), channel_id=1, source_target_pairs={{0,32},{32,64},{64,96},{96,128},{128,160},{160,192},{192,224},{224... | collective-permute-start | bytes 1572872 | tf_op jit(solution)/shard_map/while/body/eval_jaxpr/ppermute | solution.py:18
  337.0 11.4 %collective-permute-start = (f32[8,64,256]{2,1,0:T(8,128)S(1)}, f32[8,64,256]{2,1,0:T(8,128)S(1)}, u32[]{:S(2)}, u32[]{:S(2)}) collective-permute-start(f32[8,64,256]{2,1,0:T(8,128)S(1)} %multiply_add_fusion.2), channel_id=1, source_target_pairs={{0,32},{32,64},{64,96},{96,128},{128,160},{160,192},{192,224},{224... | collective-permute-start | bytes 1572872 | tf_op jit(solution)/shard_map/while/body/eval_jaxpr/ppermute | solution.py:18
  348.5 11.4 %collective-permute-start = (f32[8,64,256]{2,1,0:T(8,128)S(1)}, f32[8,64,256]{2,1,0:T(8,128)S(1)}, u32[]{:S(2)}, u32[]{:S(2)}) collective-permute-start(f32[8,64,256]{2,1,0:T(8,128)S(1)} %multiply_add_fusion.2), channel_id=1, source_target_pairs={{0,32},{32,64},{64,96},{96,128},{128,160},{160,192},{192,224},{224... | collective-permute-start | bytes 1572872 | tf_op jit(solution)/shard_map/while/body/eval_jaxpr/ppermute | solution.py:18
  360.0 11.4 %collective-permute-start = (f32[8,64,256]{2,1,0:T(8,128)S(1)}, f32[8,64,256]{2,1,0:T(8,128)S(1)}, u32[]{:S(2)}, u32[]{:S(2)}) collective-permute-start(f32[8,64,256]{2,1,0:T(8,128)S(1)} %multiply_add_fusion.2), channel_id=1, source_target_pairs={{0,32},{32,64},{64,96},{96,128},{128,160},{160,192},{192,224},{224... | collective-permute-start | bytes 1572872 | tf_op jit(solution)/shard_map/while/body/eval_jaxpr/ppermute | solution.py:18
  371.6 11.4 %collective-permute-start = (f32[8,64,256]{2,1,0:T(8,128)S(1)}, f32[8,64,256]{2,1,0:T(8,128)S(1)}, u32[]{:S(2)}, u32[]{:S(2)}) collective-permute-start(f32[8,64,256]{2,1,0:T(8,128)S(1)} %multiply_add_fusion.2), channel_id=1, source_target_pairs={{0,32},{32,64},{64,96},{96,128},{128,160},{160,192},{192,224},{224... | collective-permute-start | bytes 1572872 | tf_op jit(solution)/shard_map/while/body/eval_jaxpr/ppermute | solution.py:18
  383.1 11.4 %collective-permute-start = (f32[8,64,256]{2,1,0:T(8,128)S(1)}, f32[8,64,256]{2,1,0:T(8,128)S(1)}, u32[]{:S(2)}, u32[]{:S(2)}) collective-permute-start(f32[8,64,256]{2,1,0:T(8,128)S(1)} %multiply_add_fusion.2), channel_id=1, source_target_pairs={{0,32},{32,64},{64,96},{96,128},{128,160},{160,192},{192,224},{224... | collective-permute-start | bytes 1572872 | tf_op jit(solution)/shard_map/while/body/eval_jaxpr/ppermute | solution.py:18
  394.6 11.4 %collective-permute-start = (f32[8,64,256]{2,1,0:T(8,128)S(1)}, f32[8,64,256]{2,1,0:T(8,128)S(1)}, u32[]{:S(2)}, u32[]{:S(2)}) collective-permute-start(f32[8,64,256]{2,1,0:T(8,128)S(1)} %multiply_add_fusion.2), channel_id=1, source_target_pairs={{0,32},{32,64},{64,96},{96,128},{128,160},{160,192},{192,224},{224... | collective-permute-start | bytes 1572872 | tf_op jit(solution)/shard_map/while/body/eval_jaxpr/ppermute | solution.py:18
  406.1 11.4 %collective-permute-start = (f32[8,64,256]{2,1,0:T(8,128)S(1)}, f32[8,64,256]{2,1,0:T(8,128)S(1)}, u32[]{:S(2)}, u32[]{:S(2)}) collective-permute-start(f32[8,64,256]{2,1,0:T(8,128)S(1)} %multiply_add_fusion.2), channel_id=1, source_target_pairs={{0,32},{32,64},{64,96},{96,128},{128,160},{160,192},{192,224},{224... | collective-permute-start | bytes 1572872 | tf_op jit(solution)/shard_map/while/body/eval_jaxpr/ppermute | solution.py:18
  417.6 11.4 %collective-permute-start = (f32[8,64,256]{2,1,0:T(8,128)S(1)}, f32[8,64,256]{2,1,0:T(8,128)S(1)}, u32[]{:S(2)}, u32[]{:S(2)}) collective-permute-start(f32[8,64,256]{2,1,0:T(8,128)S(1)} %multiply_add_fusion.2), channel_id=1, source_target_pairs={{0,32},{32,64},{64,96},{96,128},{128,160},{160,192},{192,224},{224... | collective-permute-start | bytes 1572872 | tf_op jit(solution)/shard_map/while/body/eval_jaxpr/ppermute | solution.py:18
  429.2 11.4 %collective-permute-start = (f32[8,64,256]{2,1,0:T(8,128)S(1)}, f32[8,64,256]{2,1,0:T(8,128)S(1)}, u32[]{:S(2)}, u32[]{:S(2)}) collective-permute-start(f32[8,64,256]{2,1,0:T(8,128)S(1)} %multiply_add_fusion.2), channel_id=1, source_target_pairs={{0,32},{32,64},{64,96},{96,128},{128,160},{160,192},{192,224},{224... | collective-permute-start | bytes 1572872 | tf_op jit(solution)/shard_map/while/body/eval_jaxpr/ppermute | solution.py:18
  440.7 11.4 %collective-permute-start = (f32[8,64,256]{2,1,0:T(8,128)S(1)}, f32[8,64,256]{2,1,0:T(8,128)S(1)}, u32[]{:S(2)}, u32[]{:S(2)}) collective-permute-start(f32[8,64,256]{2,1,0:T(8,128)S(1)} %multiply_add_fusion.2), channel_id=1, source_target_pairs={{0,32},{32,64},{64,96},{96,128},{128,160},{160,192},{192,224},{224... | collective-permute-start | bytes 1572872 | tf_op jit(solution)/shard_map/while/body/eval_jaxpr/ppermute | solution.py:18
  469.7 10.5 %copy-start.5 = (bf16[8192]{0:T(1024)(128)(2,1)S(1)}, bf16[8192]{0:T(1024)(128)(2,1)}, u32[]{:S(2)}) copy-start(bf16[8192]{0:T(1024)(128)(2,1)} %param.23) | copy-start | bytes 49156
  472.6 71.8 %all-to-all-start.2 = ((bf16[16,96,512]{2,1,0:T(8,128)(2,1)}), bf16[16,96,512]{2,1,0:T(8,128)(2,1)S(1)}, u32[]{:S(2)}, u32[]{:S(2)}) async-start(bf16[16,96,512]{2,1,0:T(8,128)(2,1)} %reshape.200), calls=%async_computation.2 | async-start | bytes 3145728 | tf_op jit(solution)/shard_map/all_to_all | solution.py:157
  544.8 1.4 copy-start.1
  556.9 2.2 copy-start.2
Sparse Core Ops, SparseCore 0:
  48.0 152.1 all-gather.1
where the time goes:
time: 570 us; the launch traced here: 568 us
  waiting for transfers between devices  296 us (52%)
  matrix products  66.8 us (12%)
  blocking collectives  64 us (11%)
  starting transfers between devices  60.5 us (11%)
  local copies, waits for them, and re-layouts  44.3 us (8%)
  other arithmetic  22.2 us (4%)
  between operations  13.8 us (2%)
    ppermute x17, waiting for transfers between devices, shifted(): return lax.ppermute(block, axis, route)  142 us
    all_to_all x1, waiting for transfers between devices, local(): lax.all_to_all(conv_inputs, 'fsdp', split_axis=1, concat_axis=0, tiled=True)  82.6 us
    all_to_all x1, waiting for transfers between devices, local(): lax.all_to_all(section_out, 'fsdp', split_axis=0, concat_axis=1, tiled=True)  64.1 us
    ppermute x17, starting transfers between devices, shifted(): return lax.ppermute(block, axis, route)  35.3 us
    all_gather x1, blocking collectives, local(): lax.all_gather(conv_coupling, 'fsdp', axis=1, tiled=True)  33.8 us
    all_gather x1, blocking collectives, local(): lax.all_gather(conv_input, 'fsdp', axis=1, tiled=True)  30.3 us
    dot_general x3, matrix products, scan_block(): intra_out = jnp.einsum('hij,jhp->ihp', mixing, inputs, precision=precise)  23 us
    dot_general x3, matrix products, scan_block(): jnp.einsum('ihn,hpn->ihp', heads_out, carried, precision=precise)  18.6 us
  transfers between devices with their start and end apart: 21, of which 18 were waited for; matrix products, arithmetic and copies ran while one was open for 2% of the time, Pallas kernels for 0%

commit v1 on v0

v1 whole, which is shorter than its diff:
```python
import functools

import jax
import jax.numpy as jnp
from jax import lax
from jax.experimental import pallas as pl
from jax.experimental.pallas import tpu as pltpu
from jax.sharding import PartitionSpec as P

HEAD_DIM = 64
STATE = 256
GROUPS = 4
LANES = 128
PARTS = 1
LOG2E = 1.4426950408889634

F32 = jnp.float32
BF16 = jnp.bfloat16
exact = lax.Precision.HIGHEST
params = pltpu.CompilerParams(vmem_limit_bytes=48 * 2**20)


def iota(shape, dim):
    return lax.broadcasted_iota(jnp.int32, shape, dim)


def filtered(scratch, tail, block, taps):
    rows = block.shape[0]
    scratch[0:8] = tail
    scratch[8 : 8 + rows] = block
    total = scratch[5 : 5 + rows] * taps[0:1]
    total = total + scratch[6 : 6 + rows] * taps[1:2]
    total = total + scratch[7 : 7 + rows] * taps[2:3]
    total = total + block * taps[3:4]
    return jax.nn.silu(total).astype(BF16)


def coupling_kernel(raw_ref, tail_ref, taps_ref, out_ref, scratch):
    count, rows, _ = raw_ref.shape
    taps = taps_ref[...].astype(F32)
    scratch[rows : rows + 8] = tail_ref[...]

    def body(c, _):
        out_ref[c] = filtered(scratch, scratch[rows : rows + 8], raw_ref[c].astype(F32), taps)
        return 0

    lax.fori_loop(0, count, body, 0)


def decay_tables(steps_ref, bias_ref, log_rate_ref, rows):
    count, heads, lanes = steps_ref.shape
    dt = jax.nn.softplus(steps_ref[...] + bias_ref[...][None])
    log_decay = -jnp.exp(log_rate_ref[...])[None] * dt
    size = (lanes, lanes)
    upper = jnp.where(iota(size, 0) <= iota(size, 1), 1.0, 0.0).astype(F32)
    flat = log_decay.reshape(count * heads, lanes)
    cum = jnp.dot(flat, upper, precision=exact, preferred_element_type=F32)
    return dt.reshape(count * heads, lanes), cum, cum[:, rows - 1 : rows]


def high_low(table):
    high = table.astype(BF16).astype(F32)
    return high, table - high


def spread_matrix(heads, width, first, copies):
    shape = (copies * heads, width)
    return jnp.where(iota(shape, 0) % heads == first + iota(shape, 1) // HEAD_DIM, 1.0, 0.0).astype(BF16)


def pick(sel_ref, pieces, read_in, read_out):
    half = LANES

    @pl.when(sel_ref[0] == 0)
    def _():
        for k in range(2):
            if read_in is not None:
                read_in[:, :, k * half : (k + 1) * half] = pieces[k][...]
            if read_out is not None:
                read_out[:, :, k * half : (k + 1) * half] = pieces[2 + k][...]

    @pl.when(sel_ref[0] != 0)
    def _():
        for k in range(2):
            if read_in is not None:
                read_in[:, :, k * half : (k + 1) * half] = pieces[2 + k][...]
            if read_out is not None:
                read_out[:, :, k * half : (k + 1) * half] = pieces[k][...]


def state_kernel(first, sel_ref, x_ref, tail_ref, taps_ref, p0, p1, p2, p3, steps_ref, bias_ref, log_rate_ref,
                 xf_ref, state_ref, total_ref, scratch, weighted, read_in, table):
    count, rows, width = x_ref.shape
    heads = steps_ref.shape[1]
    dt, cum, tot = decay_tables(steps_ref, bias_ref, log_rate_ref, rows)
    size = (count * heads, count * heads)
    later_mat = jnp.where(
        (iota(size, 0) % heads == iota(size, 1) % heads) & (iota(size, 1) // heads > iota(size, 0) // heads), 1.0, 0.0
    ).astype(F32)
    later = jnp.dot(later_mat, jnp.broadcast_to(tot, cum.shape), precision=exact, preferred_element_type=F32)
    weight = jnp.exp(later + (tot - cum)) * dt
    high, low = high_low(weight)
    table[:, 0:heads] = high.reshape(count, heads, -1)
    table[:, heads : 2 * heads] = low.reshape(count, heads, -1)
    own = iota((heads, width), 0) == first + iota((heads, width), 1) // HEAD_DIM
    section = tot[0:heads] + later[0:heads, 0:1]
    logs = jnp.sum(jnp.where(own, jnp.broadcast_to(section, own.shape), 0.0), axis=0, keepdims=True)
    high, low = high_low(jnp.broadcast_to(logs, total_ref.shape))
    total_ref[...] = jnp.where(iota(total_ref.shape, 0) == 0, high, low).astype(BF16)
    pick(sel_ref, (p0, p1, p2, p3), read_in, None)
    taps = taps_ref[...].astype(F32)
    spread = spread_matrix(heads, width, first, 2)
    scratch[rows : rows + 8] = tail_ref[...]

    def body(c, _):
        xf = filtered(scratch, scratch[rows : rows + 8], x_ref[c].astype(F32), taps)
        xf_ref[c] = xf
        columns = jnp.transpose(table[c])[:rows].astype(BF16)
        scale = jnp.dot(columns, spread, preferred_element_type=F32)
        weighted[c] = (xf.astype(F32) * scale).astype(BF16)
        return 0

    lax.fori_loop(0, count, body, 0)
    state = lax.dot_general(
        read_in[...].reshape(count * rows, STATE),
        weighted[...].reshape(count * rows, width),
        (((0,), (0,)), ((), ())),
        preferred_element_type=F32,
    )
    state_ref[...] = state.reshape(state_ref.shape).astype(BF16)


def relay_kernel(state_ref, log_ref, out_ref):
    sections = state_ref.shape[0]
    carried = jnp.zeros(state_ref.shape[1:], F32)
    for s in range(sections):
        out_ref[s] = carried.astype(BF16)
        carried = jnp.exp(log_ref[s : s + 1]) * carried + state_ref[s].astype(F32)


def output_kernel(first, sel_ref, xf_ref, p0, p1, p2, p3, steps_ref, bias_ref, log_rate_ref, skip_ref, in_ref,
                  y_ref, state, read_in, read_out, table, column_logs, row_logs):
    count, rows, width = xf_ref.shape
    heads = steps_ref.shape[1]
    dt, cum, tot = decay_tables(steps_ref, bias_ref, log_rate_ref, rows)
    blocked = (count, heads, dt.shape[1])
    w_high, w_low = high_low(jnp.exp(tot - cum) * dt)
    e_high, e_low = high_low(jnp.exp(cum))
    for k, part in enumerate((w_high, w_low, e_high, e_low)):
        table[:, k * heads : (k + 1) * heads] = part.reshape(blocked)
    column_logs[...] = (cum * LOG2E).reshape(blocked)
    row_logs[...] = ((jnp.log(dt) - cum) * LOG2E).reshape(blocked)
    pick(sel_ref, (p0, p1, p2, p3), read_in, read_out)
    spread = spread_matrix(heads, width, first, 2)
    skip = skip_ref[...]
    state[...] = in_ref[...].astype(F32)
    causal = iota((rows, rows), 0) >= iota((rows, rows), 1)
    left = iota((rows, LANES), 1) < HEAD_DIM

    def body(c, _):
        b, q, x = read_in[c], read_out[c], xf_ref[c]
        meet = lax.dot_general(q, b, (((1,), (1,)), ((), ())), preferred_element_type=F32)
        meet = jnp.where(causal, meet, 0.0)
        columns = jnp.transpose(table[c])[:rows].astype(BF16)
        scale_in = jnp.dot(columns[:, : 2 * heads], spread, preferred_element_type=F32)
        scale_out = jnp.dot(columns[:, 2 * heads :], spread, preferred_element_type=F32)
        logs = jnp.transpose(column_logs[c])[:rows]
        rows_c = row_logs[c]
        carried = jnp.dot(q, state[...].astype(BF16), preferred_element_type=F32) * scale_out
        x32 = x.astype(F32)
        for pair in range(width // LANES):
            lanes = slice(pair * LANES, (pair + 1) * LANES)
            both = []
            for k in range(2):
                h = first + 2 * pair + k
                mix = jnp.exp2(logs[:, h : h + 1] + rows_c[h : h + 1, :rows]) * meet
                both.append(jnp.dot(mix.astype(BF16), x[:, lanes], preferred_element_type=F32))
            mixed = jnp.where(left, both[0], both[1])
            y_ref[c, :, lanes] = (mixed + carried[:, lanes] + skip[:, lanes] * x32[:, lanes]).astype(BF16)
        state[...] = state[...] * scale_out[rows - 1 : rows] + lax.dot_general(
            b, (x32 * scale_in).astype(BF16), (((0,), (0,)), ((), ())), preferred_element_type=F32
        )
        return 0

    lax.fori_loop(0, count, body, 0)


def finish_kernel(*refs):
    parts, (gate_ref, gain_ref, out_ref, gated_ref) = refs[:-4], refs[-4:]
    blocks, rows, width = parts[0].shape
    total = jnp.zeros((rows, 1), F32)
    pieces = [(z, p) for z in range(blocks) for p in range(len(parts))]
    for i, (z, p) in enumerate(pieces):
        lanes = slice(i * width, (i + 1) * width)
        gated = parts[p][z].astype(F32) * jax.nn.silu(gate_ref[:, lanes].astype(F32))
        gated_ref[:, lanes] = gated
        total = total + jnp.sum(gated * gated, axis=1, keepdims=True)
    scale = lax.rsqrt(total / (len(pieces) * width) + 1e-05)
    for i in range(len(pieces)):
        lanes = slice(i * width, (i + 1) * width)
        out_ref[:, lanes] = (gated_ref[:, lanes] * scale * gain_ref[:, lanes].astype(F32)).astype(BF16)


def call(kernel, outs, scratch, args, cost=(0, 0), smem_first=False):
    specs = [pl.BlockSpec(memory_space=pltpu.VMEM)] * len(args)
    if smem_first:
        specs[0] = pl.BlockSpec(memory_space=pltpu.SMEM)
    return pl.pallas_call(
        kernel,
        out_shape=outs,
        in_specs=specs,
        out_specs=jax.tree.map(lambda _: pl.BlockSpec(memory_space=pltpu.VMEM), outs),
        scratch_shapes=scratch,
        compiler_params=params,
        cost_estimate=pl.CostEstimate(flops=cost[0], bytes_accessed=cost[1], transcendentals=0),
    )(*args)


def local(
    ssm_input,
    gate_input,
    coupling,
    step_input,
    conv_input,
    conv_coupling,
    step_bias,
    log_rate,
    skip_gain,
    norm_gain,
):
    rows = ssm_input.shape[0]
    ring = lax.axis_size("fsdp")
    heads = step_bias.shape[0]
    width = conv_input.shape[1]
    part_width = width // PARTS
    part_heads = heads // PARTS
    struct = jax.ShapeDtypeStruct

    seq, whole = lax.axis_size("seq"), lax.axis_size("seq") * ring
    last_rows = jnp.concatenate([ssm_input[rows - 3 :], coupling[rows - 3 :]], axis=1)
    tails = lax.ppermute(last_rows, ("seq", "fsdp"), [(i, i + 1) for i in range(whole - 1)])
    taps_route = [(8 * r + 2 * g + k, 4 * g + 2 * r + k) for g in range(GROUPS) for r in range(2) for k in range(2)]
    taps_coupling = lax.ppermute(conv_coupling, "fsdp", taps_route)

    def by_owner(block):
        count = block.shape[0]
        split = block.reshape(count, 2, GROUPS, 2, LANES)
        return split.transpose(2, 1, 3, 0, 4).reshape(ring, count, LANES)

    steps_t = jnp.pad(step_input.T.reshape(ring, heads, rows), ((0, 0), (0, 0), (0, LANES - rows)))
    x_tails = tails[:, : ssm_input.shape[1]].reshape(3, ring, width // LANES, LANES).transpose(1, 2, 0, 3)
    x_tail_rows = 3 * width // LANES
    small = jnp.concatenate(
        [
            by_owner(coupling),
            steps_t,
            x_tails.reshape(ring, x_tail_rows, LANES),
            by_owner(tails[:, ssm_input.shape[1] :]),
            jnp.zeros((ring, 1, LANES), BF16),
        ],
        axis=1,
    )
    small = lax.all_to_all(small, "fsdp", 0, 0)
    x_blocks = ssm_input.reshape(rows, ring, PARTS, part_width)
    x_parts = [lax.all_to_all(x_blocks[:, :, p].transpose(1, 0, 2), "fsdp", 0, 0) for p in range(PARTS)]

    at = rows
    steps = small[:, at : at + heads].astype(F32)
    at += heads
    x_tail = small[0, at : at + x_tail_rows].reshape(width // LANES, 3, LANES).transpose(1, 0, 2).reshape(3, width)
    x_tail = jnp.pad(x_tail.astype(F32), ((5, 0), (0, 0)))
    at += x_tail_rows
    c_tail = jnp.pad(small[0, at : at + 3].astype(F32), ((5, 0), (0, 0)))

    own = call(
        coupling_kernel,
        struct((ring, rows, LANES), BF16),
        [pltpu.VMEM((rows + 8, LANES), F32)],
        (small[:, :rows], c_tail, taps_coupling),
        (4000000, 800000),
    )
    pieces = [own]
    for d in range(1, 4):
        pieces.append(lax.ppermute(own, "fsdp", [(i, i ^ d) for i in range(ring)]))
    select = (lax.axis_index("fsdp") // 2 % 2).astype(jnp.int32).reshape(1)
    bias, rate = step_bias.reshape(heads, 1), log_rate.reshape(heads, 1)
    skip = jnp.repeat(skip_gain, HEAD_DIM).reshape(1, width)

    outs = []
    for p in range(PARTS):
        first = p * part_heads
        lanes = slice(p * part_width, (p + 1) * part_width)
        share = STATE // seq
        xf, state, total = call(
            functools.partial(state_kernel, first),
            (
                struct((ring, rows, part_width), BF16),
                struct((seq, share, part_width), BF16),
                struct((16, part_width), BF16),
            ),
            [
                pltpu.VMEM((rows + 8, part_width), F32),
                pltpu.VMEM((ring, rows, part_width), BF16),
                pltpu.VMEM((ring, rows, STATE), BF16),
                pltpu.VMEM((ring, 2 * heads, LANES), F32),
            ],
            (select, x_parts[p], x_tail[:, lanes], conv_input[:, lanes], *pieces, steps, bias, rate),
            (400000000, 5000000),
            True,
        )
        message = jnp.concatenate([state, jnp.broadcast_to(total[:8], (seq, 8, part_width))], axis=1)
        message = lax.all_to_all(message, "seq", 0, 0)
        section_logs = message[:, share].astype(F32) + message[:, share + 1].astype(F32)
        incoming = call(
            relay_kernel,
            struct((seq, share, part_width), BF16),
            [],
            (message[:, :share], section_logs),
            (1000000, 600000),
        )
        incoming = lax.all_to_all(incoming, "seq", 0, 0).reshape(STATE, part_width)
        y = call(
            functools.partial(output_kernel, first),
            struct((ring, rows, part_width), BF16),
            [
                pltpu.VMEM((STATE, part_width), F32),
                pltpu.VMEM((ring, rows, STATE), BF16),
                pltpu.VMEM((ring, rows, STATE), BF16),
                pltpu.VMEM((ring, 4 * heads, LANES), F32),
                pltpu.VMEM((ring, heads, LANES), F32),
                pltpu.VMEM((ring, heads, LANES), F32),
            ],
            (select, xf, *pieces, steps, bias, rate, skip[:, lanes], incoming),
            (1600000000, 5000000),
            True,
        )
        outs.append(lax.all_to_all(y, "fsdp", 0, 0))

    group_width = ssm_input.shape[1] // GROUPS
    blocks = ring // GROUPS
    return pl.pallas_call(
        finish_kernel,
        grid=(GROUPS,),
        out_shape=struct(ssm_input.shape, BF16),
        in_specs=[pl.BlockSpec((blocks, rows, part_width), lambda g: (g, 0, 0))] * PARTS
        + [
            pl.BlockSpec((rows, group_width), lambda g: (0, g)),
            pl.BlockSpec((1, group_width), lambda g: (0, g)),
        ],
        out_specs=pl.BlockSpec((rows, group_width), lambda g: (0, g)),
        scratch_shapes=[pltpu.VMEM((rows, group_width), F32)],
        compiler_params=params,
    )(*outs, gate_input, norm_gain.reshape(1, -1))


def solution(mesh):
    return jax.shard_map(
        local,
        mesh=mesh,
        in_specs=(
            P(("batch", "seq", "fsdp"), None),
            P(("batch", "seq", "fsdp"), None),
            P(("batch", "seq", "fsdp"), None),
            P(("batch", "seq", "fsdp"), None),
            P(None, "fsdp"),
            P(None, "fsdp"),
            P("fsdp"),
            P("fsdp"),
            P("fsdp"),
            P(),
        ),
        out_specs=P(("batch", "seq", "fsdp"), None),
        check_vma=False,
    )
```

time: 570 us -> 306 us (0.54)
  waiting for transfers between devices: 296 us -> 135 us
  matrix products: 66.8 us -> 0 us
  starting transfers between devices: 60.5 us -> 122 us
  blocking collectives: 64 us -> 12.8 us
  local copies, waits for them, and re-layouts: 44.3 us -> 11.4 us
  Pallas kernels: 0 us -> 21.6 us
  other arithmetic: 22.2 us -> 0.86 us
  between operations: 13.8 us -> 0.39 us
    ppermute x17 -> x5, waiting for transfers between devices: 142 us -> 31.2 us  [the longest x3 22.3 us: local(): pieces.append(lax.ppermute(own, 'fsdp', [(i, i ^ d) for i in range(ring)]))]
    dot_general x13 -> x0, matrix products: 66.8 us -> none  [the longest x3 23 us: scan_block(): intra_out = jnp.einsum('hij,jhp->ihp', mixing, inputs, precision=precise)]
    all_gather x2 -> x0, blocking collectives: 64 us -> none  [the longest x1 33.8 us: local(): lax.all_gather(conv_coupling, 'fsdp', axis=1, tiled=True)]
    ppermute x17 -> x5, starting transfers between devices: 35.3 us -> 89.4 us  [the longest x3 84.7 us: local(): pieces.append(lax.ppermute(own, 'fsdp', [(i, i ^ d) for i in range(ring)]))]
    all_to_all x3 -> x4, waiting for transfers between devices: 147 us -> 104 us  [the longest x1 74.2 us: local(): outs.append(lax.all_to_all(y, 'fsdp', 0, 0))]
    pallas_call x0 -> x5, Pallas kernels: none -> 21.6 us  [the longest x4 18.9 us: call(): pl.pallas_call(kernel, out_shape=outs, in_specs=specs, out_specs=jax.tree...]
    all_to_all x0 -> x1, blocking collectives: none -> 12.8 us  [local(): message = lax.all_to_all(message, 'seq', 0, 0)]
    convert_element_type x10 -> x1, other arithmetic: 9.5 us -> 0.76 us  [local(): steps = small[:, at:at + heads].astype(F32)]
  transfers between devices with their start and end apart: 21 -> 9, of which waited for: 18 -> 5; matrix products, arithmetic and copies ran while one was open for 2% -> 2% of each run, Pallas kernels for 0% -> 0%
where the time goes in v1:
time: 306 us; the launch traced here: 304 us
  waiting for transfers between devices  135 us (44%)
  starting transfers between devices  122 us (40%)
  Pallas kernels  21.6 us (7%)
  blocking collectives  12.8 us (4%)
  local copies, waits for them, and re-layouts  11.4 us (4%)
    ppermute x3, starting transfers between devices, local(): pieces.append(lax.ppermute(own, 'fsdp', [(i, i ^ d) for i in range(ring)]))  84.7 us
    all_to_all x1, waiting for transfers between devices, local(): outs.append(lax.all_to_all(y, 'fsdp', 0, 0))  74.2 us
    all_to_all x1, waiting for transfers between devices, local(): small = lax.all_to_all(small, 'fsdp', 0, 0)  24.3 us
    ppermute x3, waiting for transfers between devices, local(): pieces.append(lax.ppermute(own, 'fsdp', [(i, i ^ d) for i in range(ring)]))  22.3 us
    pallas_call x4, Pallas kernels, call(): pl.pallas_call(kernel, out_shape=outs, in_specs=specs, out_specs=jax.tree...  18.9 us
    all_to_all x1, blocking collectives, local(): message = lax.all_to_all(message, 'seq', 0, 0)  12.8 us
    all_to_all x1, starting transfers between devices, local(): outs.append(lax.all_to_all(y, 'fsdp', 0, 0))  11 us
    ppermute x1, waiting for transfers between devices, local(): lax.ppermute(last_rows, ('seq', 'fsdp'), [(i, i + 1) for i in range(whole...  8.91 us
  transfers between devices with their start and end apart: 9, of which 5 were waited for; matrix products, arithmetic and copies ran while one was open for 2% of the time, Pallas kernels for 0%

profile of v1, /device:TPU:6, one launch (start us, length us, event | category | flops | bytes accessed | tf_op | source)
XLA Modules:
  0.0 304.1 jit_solution(9941926540688670169)
XLA Ops:
  0.0 0.9 slice.36
  1.0 0.8 slice.37
  1.8 3.8 %collective-permute-start = (bf16[3,10240]{1,0:T(4,128)(2,1)S(1)}, bf16[3,10240]{1,0:T(4,128)(2,1)S(1)}, u32[]{:S(2)}, u32[]{:S(2)}) collective-permute-start(bf16[3,10240]{1,0:T(4,128)(2,1)S(1)} %pad_maximum_fusion.1), channel_id=1, source_target_pairs={{0,2},{2,4},{4,6},{6,8},{8,10},{10,12},{12,14},{14,16},{16,18},{18... | collective-permute-start | bytes 184328 | tf_op jit(solution)/shard_map/ppermute | solution.py:241
  5.6 1.3 reshape.47
  6.9 0.0 copy-start.5
  6.9 0.1 copy.45
  7.0 0.1 copy.46
  7.1 8.9 %collective-permute-done = bf16[3,10240]{1,0:T(4,128)(2,1)S(1)} collective-permute-done((bf16[3,10240]{1,0:T(4,128)(2,1)S(1)}, bf16[3,10240]{1,0:T(4,128)(2,1)S(1)}, u32[]{:S(2)}, u32[]{:S(2)}) %collective-permute-start) | collective-permute-done | bytes 61472 | tf_op jit(solution)/shard_map/ppermute | solution.py:241
  16.1 0.1 reshape.50
  16.3 4.1 %concatenate.10 = bf16[16,120,128]{2,1,0:T(8,128)(2,1)} concatenate(bf16[16,96,128]{2,1,0:T(8,128)(2,1)S(1)} %bitcast.30, bf16[16,8,128]{2,1,0:T(8,128)(2,1)S(1)} %pad.16, bf16[16,12,128]{2,1,0:T(8,128)(2,1)S(1)} %copy.49, bf16[16,3,128]{2,1,0:T(4,128)(2,1)S(1)} %bitcast.34, bf16[16,1,128]{2,1,0:T(2,128)(2,1)S(1)} %broadcast_in_dim.9), dimensions={1} | concatenate | bytes 983040 | tf_op jit(solution)/shard_map/concatenate | solution.py:253
  20.4 8.5 %all-to-all-start.1 = ((bf16[16,120,128]{2,1,0:T(8,128)(2,1)}), bf16[16,120,128]{2,1,0:T(8,128)(2,1)S(1)}, u32[]{:S(2)}, u32[]{:S(2)}) async-start(bf16[16,120,128]{2,1,0:T(8,128)(2,1)} %concatenate.10), calls=%async_computation.1 | async-start | bytes 983040 | tf_op jit(solution)/shard_map/all_to_all | solution.py:263
  28.9 1.3 copy.62
  30.2 24.3 %all-to-all-done.1 = bf16[16,120,128]{2,1,0:T(8,128)(2,1)S(1)} async-done(((bf16[16,120,128]{2,1,0:T(8,128)(2,1)}), bf16[16,120,128]{2,1,0:T(8,128)(2,1)S(1)}, u32[]{:S(2)}, u32[]{:S(2)}) %all-to-all-start.1) | async-done | bytes 491552 | tf_op jit(solution)/shard_map/all_to_all | solution.py:263
  54.4 7.4 %all-to-all-start = ((bf16[16,96,512]{2,1,0:T(8,128)(2,1)}), bf16[16,96,512]{2,1,0:T(8,128)(2,1)S(1)}, u32[]{:S(2)}, u32[]{:S(2)}) async-start(bf16[16,96,512]{2,1,0:T(8,128)(2,1)} %bitcast.27), calls=%async_computation | async-start | bytes 3145728 | tf_op jit(solution)/shard_map/all_to_all | solution.py:265
  61.8 0.0 copy-done.11
  61.8 0.0 copy-start.8
  61.8 0.0 copy-start.9
  61.9 0.0 copy-start.1
  61.9 0.8 collective-permute-start.1
  62.7 0.0 collective-permute-done.1.taps_ref
  62.7 0.5 shard_map.100.p0
  63.3 3.8 %collective-permute-start.2 = (bf16[16,96,128]{2,1,0:T(8,128)(2,1)S(1)}, bf16[16,96,128]{2,1,0:T(8,128)(2,1)S(1)}, u32[]{:S(2)}, u32[]{:S(2)}) collective-permute-start(bf16[16,96,128]{2,1,0:T(8,128)(2,1)S(1)} %shard_map.100.p0), channel_id=1, source_target_pairs={{0,2},{2,0},{4,6},{6,4},{8,10},{10,8},{12,14},{14,12},{16,18},{18,... | collective-permute-start | bytes 1179656 | tf_op jit(solution)/shard_map/ppermute | solution.py:284
  67.1 78.0 %collective-permute-start.3 = (bf16[16,96,128]{2,1,0:T(8,128)(2,1)S(1)}, bf16[16,96,128]{2,1,0:T(8,128)(2,1)S(1)}, u32[]{:S(2)}, u32[]{:S(2)}) collective-permute-start(bf16[16,96,128]{2,1,0:T(8,128)(2,1)S(1)} %shard_map.100.p0), channel_id=1, source_target_pairs={{0,4},{2,6},{4,0},{6,2},{8,12},{10,14},{12,8},{14,10},{16,20},{18,... | collective-permute-start | bytes 1179656 | tf_op jit(solution)/shard_map/ppermute | solution.py:284
  145.1 2.9 collective-permute-start.4
  148.1 0.0 copy-done.8
  148.1 0.1 copy.50.bias_ref
  148.2 0.1 copy.51.log_rate_ref
  148.2 0.7 slice.50
  149.0 0.8 slice_convert_fusion.steps_ref
  149.7 0.0 collective-permute-done.2.p1
  149.7 22.3 %collective-permute-done.3.p2 = bf16[16,96,128]{2,1,0:T(8,128)(2,1)S(1)} collective-permute-done((bf16[16,96,128]{2,1,0:T(8,128)(2,1)S(1)}, bf16[16,96,128]{2,1,0:T(8,128)(2,1)S(1)}, u32[]{:S(2)}, u32[]{:S(2)}) %collective-permute-start.3) | collective-permute-done | bytes 393248 | tf_op jit(solution)/shard_map/ppermute | solution.py:284
  172.0 0.0 collective-permute-done.4.p3
  172.0 0.0 all-to-all-done.x_ref
  172.0 6.8 %shard_map.101 = (bf16[16,96,512]{2,1,0:T(8,128)(2,1)S(1)}, bf16[16,16,512]{2,1,0:T(8,128)(2,1)S(1)}, bf16[16,512]{1,0:T(8,128)(2,1)S(1)}) custom-call(s32[1]{0:T(128)} %bitcast.sel_ref, bf16[16,96,512]{2,1,0:T(8,128)(2,1)S(1)} %all-to-all-done.x_ref, f32[8,512]{1,0:T(8,128)S(1)} %pad_convert_fusion.tail_ref, bf16[4,512]{1,0:T(4,128)(2,1)S(1)} %copy-done.1, ...), custom_call_target="tpu_custom_call" | custom-call | flops 400000000 | bytes 5000000 | tf_op jit(solution)/shard_map/pallas_call | solution.py:208
  178.8 0.0 copy-start.2
  178.8 0.0 copy-start.10
  178.9 12.8 %all_to_all.25 = bf16[16,24,512]{2,1,0:T(8,128)(2,1)S(1)} all-to-all(bf16[16,24,512]{2,1,0:T(8,128)(2,1)S(1)} %pad_maximum_fusion), channel_id=1, replica_groups=mesh['seq'=16,'fsdp'=16,'batch'=2] {'seq'}, dimensions={0} | all-to-all | bytes 786432 | tf_op jit(solution)/shard_map/all_to_all | solution.py:312
  191.8 0.8 shard_map.102
  192.5 5.5 %all-to-all-start.3 = ((bf16[16,16,512]{2,1,0:T(8,128)(2,1)}), bf16[16,16,512]{2,1,0:T(8,128)(2,1)S(1)}, u32[]{:S(2)}, u32[]{:S(2)}) async-start(bf16[16,16,512]{2,1,0:T(8,128)(2,1)} %shard_map.102), calls=%async_computation.3 | async-start | bytes 524288 | tf_op jit(solution)/shard_map/all_to_all | solution.py:321
  198.1 0.1 broadcast_in_dim.10
  198.1 0.1 reshape_reshape.3.skip_ref
  198.2 5.7 %all-to-all-done.3 = bf16[16,16,512]{2,1,0:T(8,128)(2,1)S(1)} async-done(((bf16[16,16,512]{2,1,0:T(8,128)(2,1)}), bf16[16,16,512]{2,1,0:T(8,128)(2,1)S(1)}, u32[]{:S(2)}, u32[]{:S(2)}) %all-to-all-start.3) | async-done | bytes 262176 | tf_op jit(solution)/shard_map/all_to_all | solution.py:321
  203.9 1.4 copy-done.3
  205.3 10.8 %shard_map.103 = bf16[16,96,512]{2,1,0:T(8,128)(2,1)} custom-call(s32[1]{0:T(128)} %bitcast.sel_ref, bf16[16,96,512]{2,1,0:T(8,128)(2,1)S(1)} %copy-done.3, bf16[16,96,128]{2,1,0:T(8,128)(2,1)S(1)} %shard_map.100.p0, bf16[16,96,128]{2,1,0:T(8,128)(2,1)S(1)} %collective-permute-done.2.p1, bf16[16,96,128]{2,1,0:T(8,128)(2,1)S(1)} %collective-permute-done.3.p2, ...), custom_call_target="tpu_custom_call" | custom-call | flops 1600000000 | bytes 5000000 | tf_op jit(solution)/shard_map/pallas_call | solution.py:208
  216.1 11.0 %all-to-all-start.4 = ((bf16[16,96,512]{2,1,0:T(8,128)(2,1)}), bf16[16,96,512]{2,1,0:T(8,128)(2,1)S(1)}, u32[]{:S(2)}, u32[]{:S(2)}) async-start(bf16[16,96,512]{2,1,0:T(8,128)(2,1)} %shard_map.103), calls=%async_computation.4 | async-start | bytes 3145728 | tf_op jit(solution)/shard_map/all_to_all | solution.py:337
  227.1 0.0 copy-done.7
  227.2 74.2 %all-to-all-done.4.refs_0_ = bf16[16,96,512]{2,1,0:T(8,128)(2,1)S(1)} async-done(((bf16[16,96,512]{2,1,0:T(8,128)(2,1)}), bf16[16,96,512]{2,1,0:T(8,128)(2,1)S(1)}, u32[]{:S(2)}, u32[]{:S(2)}) %all-to-all-start.4) | async-done | bytes 1572896 | tf_op jit(solution)/shard_map/all_to_all | solution.py:337
  301.4 2.7 shard_map.104
  (35 shorter events, 0.4 us)
Async XLA Ops:
  0.0 7.0 %copy-start.6 = (bf16[96,128]{1,0:T(8,128)(2,1)S(1)}, bf16[96,128]{1,0:T(8,128)(2,1)}, u32[]{:S(2)}) copy-start(bf16[96,128]{1,0:T(8,128)(2,1)} %param.13) | copy-start | bytes 73732
  1.8 14.3 %collective-permute-start = (bf16[3,10240]{1,0:T(4,128)(2,1)S(1)}, bf16[3,10240]{1,0:T(4,128)(2,1)S(1)}, u32[]{:S(2)}, u32[]{:S(2)}) collective-permute-start(bf16[3,10240]{1,0:T(4,128)(2,1)S(1)} %pad_maximum_fusion.1), channel_id=1, source_target_pairs={{0,2},{2,4},{4,6},{6,8},{8,10},{10,12},{12,14},{14,16},{16,18},{18... | collective-permute-start | bytes 184328 | tf_op jit(solution)/shard_map/ppermute | solution.py:241
  6.9 22.0 %copy-start.5 = (bf16[96,8192]{1,0:T(8,128)(2,1)S(1)}, bf16[96,8192]{1,0:T(8,128)(2,1)}, u32[]{:S(2)}) copy-start(bf16[96,8192]{1,0:T(8,128)(2,1)} %param.10) | copy-start | bytes 4718596
  20.4 34.0 %all-to-all-start.1 = ((bf16[16,120,128]{2,1,0:T(8,128)(2,1)}), bf16[16,120,128]{2,1,0:T(8,128)(2,1)S(1)}, u32[]{:S(2)}, u32[]{:S(2)}) async-start(bf16[16,120,128]{2,1,0:T(8,128)(2,1)} %concatenate.10), calls=%async_computation.1 | async-start | bytes 983040 | tf_op jit(solution)/shard_map/all_to_all | solution.py:263
  54.4 8.3 %copy-start.4 = (bf16[16,120,128]{2,1,0:T(8,128)(2,1)}, bf16[16,120,128]{2,1,0:T(8,128)(2,1)S(1)}, u32[]{:S(2)}) copy-start(bf16[16,120,128]{2,1,0:T(8,128)(2,1)S(1)} %all-to-all-done.1) | copy-start | bytes 1474564
  54.4 7.4 %copy-start.11 = (bf16[4,128]{1,0:T(4,128)(2,1)S(1)}, bf16[4,128]{1,0:T(4,128)(2,1)}, u32[]{:S(2)}) copy-start(bf16[4,128]{1,0:T(4,128)(2,1)} %param.15) | copy-start | bytes 3076
  54.4 117.6 %all-to-all-start = ((bf16[16,96,512]{2,1,0:T(8,128)(2,1)}), bf16[16,96,512]{2,1,0:T(8,128)(2,1)S(1)}, u32[]{:S(2)}, u32[]{:S(2)}) async-start(bf16[16,96,512]{2,1,0:T(8,128)(2,1)} %bitcast.27), calls=%async_computation | async-start | bytes 3145728 | tf_op jit(solution)/shard_map/all_to_all | solution.py:265
  61.8 86.2 %copy-start.8 = (f32[8]{0:T(128)S(1)}, f32[8]{0:T(128)}, u32[]{:S(2)}) copy-start(f32[8]{0:T(128)} %param.16) | copy-start | bytes 100
  61.8 86.3 %copy-start.9 = (f32[8]{0:T(128)S(1)}, f32[8]{0:T(128)}, u32[]{:S(2)}) copy-start(f32[8]{0:T(128)} %param.17) | copy-start | bytes 100
  61.9 110.1 %copy-start.1 = (bf16[4,512]{1,0:T(4,128)(2,1)S(1)}, bf16[4,512]{1,0:T(4,128)(2,1)}, u32[]{:S(2)}) copy-start(bf16[4,512]{1,0:T(4,128)(2,1)} %taps_ref.1) | copy-start | bytes 12292
  61.9 0.9 collective-permute-start.1
  63.3 86.4 %collective-permute-start.2 = (bf16[16,96,128]{2,1,0:T(8,128)(2,1)S(1)}, bf16[16,96,128]{2,1,0:T(8,128)(2,1)S(1)}, u32[]{:S(2)}, u32[]{:S(2)}) collective-permute-start(bf16[16,96,128]{2,1,0:T(8,128)(2,1)S(1)} %shard_map.100.p0), channel_id=1, source_target_pairs={{0,2},{2,0},{4,6},{6,4},{8,10},{10,8},{12,14},{14,12},{16,18},{18,... | collective-permute-start | bytes 1179656 | tf_op jit(solution)/shard_map/ppermute | solution.py:284
  67.1 104.9 %collective-permute-start.3 = (bf16[16,96,128]{2,1,0:T(8,128)(2,1)S(1)}, bf16[16,96,128]{2,1,0:T(8,128)(2,1)S(1)}, u32[]{:S(2)}, u32[]{:S(2)}) collective-permute-start(bf16[16,96,128]{2,1,0:T(8,128)(2,1)S(1)} %shard_map.100.p0), channel_id=1, source_target_pairs={{0,4},{2,6},{4,0},{6,2},{8,12},{10,14},{12,8},{14,10},{16,20},{18,... | collective-permute-start | bytes 1179656 | tf_op jit(solution)/shard_map/ppermute | solution.py:284
  145.1 26.9 %collective-permute-start.4 = (bf16[16,96,128]{2,1,0:T(8,128)(2,1)S(1)}, bf16[16,96,128]{2,1,0:T(8,128)(2,1)S(1)}, u32[]{:S(2)}, u32[]{:S(2)}) collective-permute-start(bf16[16,96,128]{2,1,0:T(8,128)(2,1)S(1)} %shard_map.100.p0), channel_id=1, source_target_pairs={{0,6},{2,4},{4,2},{6,0},{8,14},{10,12},{12,10},{14,8},{16,22},{18,... | collective-permute-start | bytes 1179656 | tf_op jit(solution)/shard_map/ppermute | solution.py:284
  178.8 12.9 %copy-start.2 = (bf16[16,96,512]{2,1,0:T(8,128)(2,1)}, bf16[16,96,512]{2,1,0:T(8,128)(2,1)S(1)}, u32[]{:S(2)}) copy-start(bf16[16,96,512]{2,1,0:T(8,128)(2,1)S(1)} %get-tuple-element.8.xf_ref) | copy-start | bytes 4718596
  178.8 19.2 %copy-start.10 = (f32[8]{0:T(128)S(1)}, f32[8]{0:T(128)}, u32[]{:S(2)}) copy-start(f32[8]{0:T(128)} %param.18) | copy-start | bytes 100
  192.5 11.4 %all-to-all-start.3 = ((bf16[16,16,512]{2,1,0:T(8,128)(2,1)}), bf16[16,16,512]{2,1,0:T(8,128)(2,1)S(1)}, u32[]{:S(2)}, u32[]{:S(2)}) async-start(bf16[16,16,512]{2,1,0:T(8,128)(2,1)} %shard_map.102), calls=%async_computation.3 | async-start | bytes 524288 | tf_op jit(solution)/shard_map/all_to_all | solution.py:321
  203.9 1.4 copy-start.3
  216.1 11.0 %copy-start.7 = (bf16[8192]{0:T(1024)(128)(2,1)S(1)}, bf16[8192]{0:T(1024)(128)(2,1)}, u32[]{:S(2)}) copy-start(bf16[8192]{0:T(1024)(128)(2,1)} %param.19) | copy-start | bytes 49156
  216.1 85.3 %copy-start = (bf16[96,8192]{1,0:T(8,128)(2,1)S(1)}, bf16[96,8192]{1,0:T(8,128)(2,1)}, u32[]{:S(2)}) copy-start(bf16[96,8192]{1,0:T(8,128)(2,1)} %refs_1_.1) | copy-start | bytes 4718596
  216.1 85.3 %all-to-all-start.4 = ((bf16[16,96,512]{2,1,0:T(8,128)(2,1)}), bf16[16,96,512]{2,1,0:T(8,128)(2,1)S(1)}, u32[]{:S(2)}, u32[]{:S(2)}) async-start(bf16[16,96,512]{2,1,0:T(8,128)(2,1)} %shard_map.103), calls=%async_computation.4 | async-start | bytes 3145728 | tf_op jit(solution)/shard_map/all_to_all | solution.py:337

commit v2 on v1

v2 whole, which is shorter than its diff:
```python
import jax
import jax.numpy as jnp
from jax import lax
from jax.experimental import pallas as pl
from jax.experimental.pallas import tpu as pltpu
from jax.sharding import PartitionSpec as P

HEAD_DIM = 64
STATE = 256
GROUPS = 4
LANES = 128
HALO = 8
LOG2E = 1.4426950408889634

F32 = jnp.float32
BF16 = jnp.bfloat16
exact = lax.Precision.HIGHEST
params = pltpu.CompilerParams(vmem_limit_bytes=48 * 2**20)


def iota(shape, dim):
    return lax.broadcasted_iota(jnp.int32, shape, dim)


def decay_tables(steps_ref, bias_ref, log_rate_ref, rows):
    count, heads, lanes = steps_ref.shape
    dt = jax.nn.softplus(steps_ref[...] + bias_ref[...][None])
    log_decay = -jnp.exp(log_rate_ref[...])[None] * dt
    size = (lanes, lanes)
    upper = jnp.where(iota(size, 0) <= iota(size, 1), 1.0, 0.0).astype(F32)
    flat = log_decay.reshape(count * heads, lanes)
    cum = jnp.dot(flat, upper, precision=exact, preferred_element_type=F32)
    return dt.reshape(count * heads, lanes), cum, cum[:, rows - 1 : rows]


def high_low(table):
    high = table.astype(BF16).astype(F32)
    return high, table - high


def spread_matrix(heads, width, copy):
    shape = (LANES, width)
    row, lane = iota(shape, 0), iota(shape, 1)
    ours = (row >= copy * heads) & (row < (copy + 2) * heads) & (row % heads == lane // HEAD_DIM)
    return jnp.where(ours, 1.0, 0.0).astype(BF16)


def fill(table, parts):
    table[...] = jnp.zeros(table.shape, F32)
    count, _, lanes = table.shape
    for k, part in enumerate(parts):
        heads = part.shape[0] // count
        table[:, k * heads : (k + 1) * heads] = part.reshape(count, heads, lanes)


def silu_conv(scratch, block, taps):
    rows = block.shape[0] - HALO
    scratch[...] = block
    total = scratch[HALO - 3 : HALO - 3 + rows] * taps[0:1]
    for k in range(1, 4):
        total = total + scratch[HALO - 3 + k : HALO - 3 + k + rows] * taps[k : k + 1]
    return jax.nn.silu(total)


def turned(block):
    return pltpu.roll(block, HEAD_DIM, 1)


def pack_kernel(x_ref, coupling_ref, steps_ref, x_tail_ref, c_tail_ref, taps_ref, out_ref):
    count, _, lanes = out_ref.shape
    width = lanes - LANES
    rows = x_ref.shape[0]
    heads = steps_ref.shape[1] // count
    left = iota((HALO + rows, LANES), 1) < HEAD_DIM
    below = iota((HALO, width), 0) >= HALO - 3
    below_c = iota((HALO, LANES), 0) >= HALO - 3
    steps = steps_ref[...].astype(F32)
    steps = jnp.transpose(jnp.concatenate([steps, jnp.zeros((LANES - rows, steps.shape[1]), F32)], axis=0))
    own_taps = taps_ref[...].astype(F32)
    pair_width = GROUPS * STATE
    for d in range(count):
        g, j = d // 4, d % 4
        own = steps[d * heads : (d + 1) * heads]
        top = jnp.concatenate([own[:4], own[4:], jnp.zeros((4, width - 2 * LANES), F32)], axis=1)
        top = jnp.concatenate([top, jnp.zeros((HALO - 4, width), F32)], axis=0)
        lanes_d = slice(d * width, (d + 1) * width)
        top = jnp.where(below, x_tail_ref[:, lanes_d].astype(F32), top)
        out_ref[d, :, :width] = jnp.concatenate([top, x_ref[:, lanes_d].astype(F32)], axis=0).astype(BF16)
        taps = own_taps if j % 2 == 0 else turned(own_taps)
        taps = jnp.concatenate([taps, jnp.zeros((HALO - 4, LANES), F32)], axis=0)
        blocks = []
        for r in range(2):
            at = r * pair_width + g * STATE + j // 2 * LANES
            tail = c_tail_ref[:, at : at + LANES].astype(F32)
            blocks.append(jnp.concatenate([tail, coupling_ref[:, at : at + LANES].astype(F32)], axis=0))
        b, c = blocks
        both = jnp.where(left, b, turned(c)) if j % 2 == 0 else jnp.where(left, turned(b), c)
        both = jnp.concatenate([jnp.where(below_c, both[:HALO], taps), both[HALO:]], axis=0)
        out_ref[d, :, width:] = both.astype(BF16)


def coupling_kernel(from_ref, m_ref, b_ref, c_ref, steps_ref, scratch):
    count, _, lanes = m_ref.shape
    width = lanes - LANES
    rows = m_ref.shape[1] - HALO
    taps_b = m_ref[from_ref[0], :, width:].astype(F32)[:4]
    taps_c = turned(m_ref[from_ref[1], :, width:].astype(F32)[:4])
    taps = jnp.where(iota((4, LANES), 1) < HEAD_DIM, taps_b, taps_c)
    left = iota((rows // 2, LANES), 1) < HEAD_DIM

    def body(c, _):
        steps = m_ref[c, :, : 2 * LANES].astype(F32)
        steps_ref[c] = jnp.concatenate([steps[:4, :LANES], steps[:4, LANES:]], axis=0)
        both = silu_conv(scratch, m_ref[c, :, width:].astype(F32), taps)
        early, late = both[: rows // 2], both[rows // 2 :]
        b_ref[c] = jnp.where(left, early, turned(late)).astype(BF16)
        c_ref[c] = jnp.where(left, turned(early), late).astype(BF16)
        return 0

    lax.fori_loop(0, count, body, 0)


def unpacked(pieces):
    early, late = [], []
    for k in range(0, 4, 2):
        a, b = pieces[k].astype(F32), pieces[k + 1].astype(F32)
        left = iota(a.shape, 1) < HEAD_DIM
        early.append(jnp.where(left, a, turned(b)))
        late.append(jnp.where(left, turned(a), b))
    whole = jnp.concatenate([jnp.concatenate(early, axis=1), jnp.concatenate(late, axis=1)], axis=0)
    return whole.astype(BF16)


def input_kernel(m_ref, taps_ref, steps_ref, bias_ref, log_rate_ref, x_ref, weighted_ref, total_ref, scratch, table):
    count, rows, width = x_ref.shape
    heads = steps_ref.shape[1]
    dt, cum, tot = decay_tables(steps_ref, bias_ref, log_rate_ref, rows)
    size = (count * heads, count * heads)
    later_mat = jnp.where(
        (iota(size, 0) % heads == iota(size, 1) % heads) & (iota(size, 1) // heads > iota(size, 0) // heads), 1.0, 0.0
    ).astype(F32)
    later = jnp.dot(later_mat, cum, precision=exact, preferred_element_type=F32)[:, rows - 1 : rows]
    fill(table, high_low(jnp.exp(later + (tot - cum)) * dt))
    total_ref[...] = jnp.broadcast_to((tot[0:heads] + later[0:heads, 0:1])[None], total_ref.shape)
    taps = taps_ref[...].astype(F32)
    spread = spread_matrix(heads, width, 0)

    def body(c, _):
        x = silu_conv(scratch, m_ref[c, :, :width].astype(F32), taps).astype(BF16)
        x_ref[c] = x
        columns = jnp.transpose(table[c])[:rows].astype(BF16)
        scale = jnp.dot(columns, spread, preferred_element_type=F32)
        weighted_ref[c] = (x.astype(F32) * scale).astype(BF16)
        return 0

    lax.fori_loop(0, count, body, 0)


def state_kernel(p0, p1, p2, p3, weighted_ref, totals_ref, state_ref, in_ref, decay_ref):
    count, rows, width = weighted_ref.shape
    heads = totals_ref.shape[1]

    def body(c, _):
        in_ref[c] = unpacked([p[c] for p in (p0, p1, p2, p3)])
        return 0

    lax.fori_loop(0, count, body, 0)
    own = iota((heads, width), 0) == iota((heads, width), 1) // HEAD_DIM
    for s in range(totals_ref.shape[0]):
        logs = jnp.where(own, jnp.broadcast_to(totals_ref[s][:, :1], own.shape), 0.0)
        decay_ref[s : s + 1] = jnp.exp(jnp.sum(logs, axis=0, keepdims=True))
    state = lax.dot_general(
        in_ref[...].reshape(count * rows, STATE),
        weighted_ref[...].reshape(count * rows, width),
        (((0,), (0,)), ((), ())),
        preferred_element_type=F32,
    )
    state_ref[...] = state.reshape(state_ref.shape).astype(BF16)


def relay_kernel(state_ref, decay_ref, out_ref):
    carried = jnp.zeros(state_ref.shape[1:], F32)
    for s in range(state_ref.shape[0]):
        out_ref[s] = carried.astype(BF16)
        carried = decay_ref[s : s + 1] * carried + state_ref[s].astype(F32)


def scan_kernel(j_ref, x_ref, in_ref, c_ref, steps_ref, bias_ref, log_rate_ref, skip_ref,
                y_ref, out_ref, state, table, column_logs, row_logs):
    count, rows, width = x_ref.shape
    heads = steps_ref.shape[1]
    dt, cum, tot = decay_tables(steps_ref, bias_ref, log_rate_ref, rows)
    blocked = (count, heads, dt.shape[1])
    fill(table, high_low(jnp.exp(tot - cum) * dt) + high_low(jnp.exp(cum)))
    column_logs[...] = (cum * LOG2E).reshape(blocked)
    row_logs[...] = ((jnp.log(dt) - cum) * LOG2E).reshape(blocked)
    spread_in, spread_out = spread_matrix(heads, width, 0), spread_matrix(heads, width, 2)
    skip = skip_ref[...]
    state[...] = jnp.zeros(state.shape, F32)
    causal = iota((rows, rows), 0) >= iota((rows, rows), 1)
    left = iota((rows, LANES), 1) < HEAD_DIM
    order = [lax.bitwise_xor(j_ref[0], d) for d in range(4)]

    def body(c, _):
        q = unpacked([c_ref[k, c] for k in order])
        out_ref[c] = q
        b, x = in_ref[c], x_ref[c]
        meet = lax.dot_general(q, b, (((1,), (1,)), ((), ())), preferred_element_type=F32)
        meet = jnp.where(causal, meet, 0.0)
        columns = jnp.transpose(table[c])[:rows].astype(BF16)
        scale_in = jnp.dot(columns, spread_in, preferred_element_type=F32)
        scale_out = jnp.dot(columns, spread_out, preferred_element_type=F32)
        logs = jnp.transpose(column_logs[c])[:rows]
        rows_c = row_logs[c]
        carried = jnp.dot(q, state[...].astype(BF16), preferred_element_type=F32) * scale_out
        x32 = x.astype(F32)
        for pair in range(width // LANES):
            lanes = slice(pair * LANES, (pair + 1) * LANES)
            both = []
            for k in range(2):
                h = 2 * pair + k
                mix = jnp.exp2(logs[:, h : h + 1] + rows_c[h : h + 1, :rows]) * meet
                both.append(jnp.dot(mix.astype(BF16), x[:, lanes], preferred_element_type=F32))
            mixed = jnp.where(left, both[0], both[1])
            y_ref[c, :, lanes] = mixed + carried[:, lanes] + skip[:, lanes] * x32[:, lanes]
        state[...] = state[...] * scale_out[rows - 1 : rows] + lax.dot_general(
            b, (x32 * scale_in).astype(BF16), (((0,), (0,)), ((), ())), preferred_element_type=F32
        )
        return 0

    lax.fori_loop(0, count, body, 0)


def carry_kernel(y_ref, out_ref, incoming_ref, steps_ref, bias_ref, log_rate_ref, sum_ref, table):
    count, rows, width = y_ref.shape
    heads = steps_ref.shape[1]
    _, cum, tot = decay_tables(steps_ref, bias_ref, log_rate_ref, rows)
    size = (count * heads, count * heads)
    earlier_mat = jnp.where(
        (iota(size, 0) % heads == iota(size, 1) % heads) & (iota(size, 1) // heads < iota(size, 0) // heads), 1.0, 0.0
    ).astype(F32)
    earlier = jnp.dot(earlier_mat, cum, precision=exact, preferred_element_type=F32)[:, rows - 1 : rows]
    fill(table, high_low(jnp.exp(earlier + cum)))
    spread = spread_matrix(heads, width, 0)
    incoming = incoming_ref[...]

    def body(c, _):
        columns = jnp.transpose(table[c])[:rows].astype(BF16)
        scale = jnp.dot(columns, spread, preferred_element_type=F32)
        carried = jnp.dot(out_ref[c], incoming, preferred_element_type=F32)
        sum_ref[c] = (y_ref[c] + carried * scale).astype(BF16)
        return 0

    lax.fori_loop(0, count, body, 0)


def finish_kernel(*refs):
    parts, (gate_ref, gain_ref, out_ref, gated_ref) = refs[:-4], refs[-4:]
    blocks, rows, width = parts[0].shape
    total = jnp.zeros((rows, 1), F32)
    pieces = [(z, p) for z in range(blocks) for p in range(len(parts))]
    for i, (z, p) in enumerate(pieces):
        lanes = slice(i * width, (i + 1) * width)
        gated = parts[p][z].astype(F32) * jax.nn.silu(gate_ref[:, lanes].astype(F32))
        gated_ref[:, lanes] = gated
        total = total + jnp.sum(gated * gated, axis=1, keepdims=True)
    scale = lax.rsqrt(total / (len(pieces) * width) + 1e-05)
    for i in range(len(pieces)):
        lanes = slice(i * width, (i + 1) * width)
        out_ref[:, lanes] = (gated_ref[:, lanes] * scale * gain_ref[:, lanes].astype(F32)).astype(BF16)


def call(kernel, outs, scratch, args, cost=(0, 0), smem_first=False):
    specs = [pl.BlockSpec(memory_space=pltpu.VMEM)] * len(args)
    if smem_first:
        specs[0] = pl.BlockSpec(memory_space=pltpu.SMEM)
    return pl.pallas_call(
        kernel,
        out_shape=outs,
        in_specs=specs,
        out_specs=jax.tree.map(lambda _: pl.BlockSpec(memory_space=pltpu.VMEM), outs),
        scratch_shapes=scratch,
        compiler_params=params,
        cost_estimate=pl.CostEstimate(flops=cost[0], bytes_accessed=cost[1], transcendentals=0),
    )(*args)


def local(
    ssm_input,
    gate_input,
    coupling,
    step_input,
    conv_input,
    conv_coupling,
    step_bias,
    log_rate,
    skip_gain,
    norm_gain,
):
    rows, channels = ssm_input.shape
    ring = lax.axis_size("fsdp")
    seq = lax.axis_size("seq")
    heads = step_bias.shape[0]
    width = conv_input.shape[1]
    struct = jax.ShapeDtypeStruct
    place = lax.axis_index("fsdp").astype(jnp.int32)
    bias, rate = step_bias.reshape(heads, 1), log_rate.reshape(heads, 1)

    route = [(i, i + 1) for i in range(seq * ring - 1)]
    x_tail, c_tail = lax.ppermute((ssm_input[rows - HALO :], coupling[rows - HALO :]), ("seq", "fsdp"), route)
    message = call(
        pack_kernel,
        struct((ring, HALO + rows, width + LANES), BF16),
        [],
        (ssm_input, coupling, step_input, x_tail, c_tail, conv_coupling),
        (0, 4000000),
    )
    message = lax.all_to_all(message, "fsdp", 0, 0)

    senders = 2 * (place // 4) + place % 4 // 2 + jnp.array([0, 2 * GROUPS], jnp.int32)
    packed = struct((ring, rows // 2, LANES), BF16)
    own_in, own_out, steps = call(
        coupling_kernel,
        (packed, packed, struct((ring, heads, LANES), F32)),
        [pltpu.VMEM((HALO + rows, LANES), F32)],
        (senders, message),
        (4000000, 3000000),
        True,
    )
    pieces = [own_in] + [lax.ppermute(own_in, "fsdp", [(i, i ^ d) for i in range(ring)]) for d in range(1, 4)]
    blocks = (ring, rows, width)
    x, weighted, totals = call(
        input_kernel,
        (struct(blocks, BF16), struct(blocks, BF16), struct((seq, heads, LANES), F32)),
        [pltpu.VMEM((HALO + rows, width), F32), pltpu.VMEM((ring, LANES, LANES), F32)],
        (message, conv_input, steps, bias, rate),
        (20000000, 6000000),
    )
    totals = lax.all_to_all(totals, "seq", 0, 0)
    share = STATE // seq
    state, read_in, decay = call(
        state_kernel,
        (struct((seq, share, width), BF16), struct((ring, rows, STATE), BF16), struct((seq, width), F32)),
        [],
        (*pieces, weighted, totals),
        (400000000, 5000000),
    )
    fours = [[4 * g + j for j in range(4)] for g in range(ring // 4)]
    own_out, _ = lax.optimization_barrier((own_out, read_in))
    all_out = lax.all_gather(own_out, "fsdp", axis=0, axis_index_groups=fours)
    state = lax.all_to_all(state, "seq", 0, 0)
    incoming = call(relay_kernel, struct((seq, share, width), BF16), [], (state, decay), (1000000, 600000))
    incoming = lax.all_to_all(incoming, "seq", 0, 0).reshape(STATE, width)
    table = pltpu.VMEM((ring, heads, LANES), F32)
    y, read_out = call(
        scan_kernel,
        (struct(blocks, F32), struct((ring, rows, STATE), BF16)),
        [pltpu.VMEM((STATE, width), F32), pltpu.VMEM((ring, LANES, LANES), F32), table, table],
        ((place % 4).reshape(1), x, read_in, all_out, steps, bias, rate, jnp.repeat(skip_gain, HEAD_DIM).reshape(1, width)),
        (1600000000, 8000000),
        True,
    )
    y = call(
        carry_kernel,
        struct(blocks, BF16),
        [pltpu.VMEM((ring, LANES, LANES), F32)],
        (y, read_out, incoming, steps, bias, rate),
        (400000000, 6000000),
    )
    y = lax.all_to_all(y, "fsdp", 0, 0)

    group_width = channels // GROUPS
    return pl.pallas_call(
        finish_kernel,
        grid=(GROUPS,),
        out_shape=struct(ssm_input.shape, BF16),
        in_specs=[
            pl.BlockSpec((ring // GROUPS, rows, width), lambda g: (g, 0, 0)),
            pl.BlockSpec((rows, group_width), lambda g: (0, g)),
            pl.BlockSpec((1, group_width), lambda g: (0, g)),
        ],
        out_specs=pl.BlockSpec((rows, group_width), lambda g: (0, g)),
        scratch_shapes=[pltpu.VMEM((rows, group_width), F32)],
        compiler_params=params,
    )(y, gate_input, norm_gain.reshape(1, -1))


def solution(mesh):
    return jax.shard_map(
        local,
        mesh=mesh,
        in_specs=(
            P(("batch", "seq", "fsdp"), None),
            P(("batch", "seq", "fsdp"), None),
            P(("batch", "seq", "fsdp"), None),
            P(("batch", "seq", "fsdp"), None),
            P(None, "fsdp"),
            P(None, "fsdp"),
            P("fsdp"),
            P("fsdp"),
            P("fsdp"),
            P(),
        ),
        out_specs=P(("batch", "seq", "fsdp"), None),
        check_vma=False,
    )
```

time: 306 us -> 299 us (0.977)
  starting transfers between devices: 122 us -> 46.6 us
  waiting for transfers between devices: 135 us -> 179 us
  blocking collectives: 12.8 us -> 29.9 us
  Pallas kernels: 21.6 us -> 31.8 us
    ppermute x5, starting transfers between devices: 89.4 us -> 18.4 us  [the longest x3 10.7 us: local(): lax.ppermute(own_in, 'fsdp', [(i, i ^ d) for i in range(ring)])]
    all_to_all x4, waiting for transfers between devices: 104 us -> 171 us  [the longest x1 92.2 us: local(): message = lax.all_to_all(message, 'fsdp', 0, 0)]
    ppermute x5, waiting for transfers between devices: 31.2 us -> 8.11 us  [the longest x2 8.1 us: local(): lax.ppermute((ssm_input[rows - HALO:], coupling[rows - HALO:]), ('seq', '...]
    all_gather x0 -> x1, blocking collectives: none -> 20 us  [local(): all_out = lax.all_gather(own_out, 'fsdp', axis=0, axis_index_groups=fours)]
    pallas_call x4 -> x7, Pallas kernels: 18.9 us -> 29.2 us  [call(): pl.pallas_call(kernel, out_shape=outs, in_specs=specs, out_specs=jax.tree...]
    unnamed x24 -> x28, local copies, waits for them, and re-layouts: 1.46 us -> 8.52 us
    all_to_all x4, starting transfers between devices: 32.4 us -> 28.2 us  [the longest x1 9.38 us: local(): message = lax.all_to_all(message, 'fsdp', 0, 0)]
    concatenate x1 -> x0, local copies, waits for them, and re-layouts: 4.09 us -> none  [local(): jnp.concatenate([by_owner(coupling), steps_t, x_tails.reshape(ring, x_tai...]
  transfers between devices with their start and end apart: 9 -> 9, of which waited for: 5 -> 4; matrix products, arithmetic and copies ran while one was open for 2% -> 0% of each run, Pallas kernels for 0% -> 6%
where the time goes in v2:
time: 299 us; the launch traced here: 298 us
  waiting for transfers between devices  179 us (60%)
  starting transfers between devices  46.6 us (16%)
  Pallas kernels  31.8 us (11%)
  blocking collectives  29.9 us (10%)
  local copies, waits for them, and re-layouts  10.5 us (4%)
    all_to_all x1, waiting for transfers between devices, local(): message = lax.all_to_all(message, 'fsdp', 0, 0)  92.2 us
    all_to_all x1, waiting for transfers between devices, local(): y = lax.all_to_all(y, 'fsdp', 0, 0)  73.3 us
    pallas_call x7, Pallas kernels, call(): pl.pallas_call(kernel, out_shape=outs, in_specs=specs, out_specs=jax.tree...  29.2 us
    all_gather x1, blocking collectives, local(): all_out = lax.all_gather(own_out, 'fsdp', axis=0, axis_index_groups=fours)  20 us
    ppermute x3, starting transfers between devices, local(): lax.ppermute(own_in, 'fsdp', [(i, i ^ d) for i in range(ring)])  10.7 us
    all_to_all x1, blocking collectives, local(): totals = lax.all_to_all(totals, 'seq', 0, 0)  9.88 us
    all_to_all x1, starting transfers between devices, local(): message = lax.all_to_all(message, 'fsdp', 0, 0)  9.38 us
    unnamed x28, local copies, waits for them, and re-layouts  8.52 us
  transfers between devices with their start and end apart: 9, of which 4 were waited for; matrix products, arithmetic and copies ran while one was open for 0% of the time, Pallas kernels for 6%

profile of v2, /device:TPU:6, one launch (start us, length us, event | category | flops | bytes accessed | tf_op | source)
XLA Modules:
  0.0 298.4 jit_solution(18381907620544431041)
XLA Ops:
  0.0 0.9 slice.6
  0.9 3.8 %collective-permute-start = (bf16[8,8192]{1,0:T(8,128)(2,1)S(1)}, bf16[8,8192]{1,0:T(8,128)(2,1)S(1)}, u32[]{:S(2)}, u32[]{:S(2)}) collective-permute-start(bf16[8,8192]{1,0:T(8,128)(2,1)S(1)} %slice.6), channel_id=1, source_target_pairs={{0,2},{2,4},{4,6},{6,8},{8,10},{10,12},{12,14},{14,16},{16,18},{18... | collective-permute-start | bytes 393224 | tf_op jit(solution)/shard_map/ppermute | solution.py:310
  4.8 0.8 slice.7
  5.5 3.8 %collective-permute-start.1 = (bf16[8,2048]{1,0:T(8,128)(2,1)S(1)}, bf16[8,2048]{1,0:T(8,128)(2,1)S(1)}, u32[]{:S(2)}, u32[]{:S(2)}) collective-permute-start(bf16[8,2048]{1,0:T(8,128)(2,1)S(1)} %slice.7), channel_id=1, source_target_pairs={{0,2},{2,4},{4,6},{6,8},{8,10},{10,12},{12,14},{14,16},{16,18},{18... | collective-permute-start | bytes 98312 | tf_op jit(solution)/shard_map/ppermute | solution.py:310
  9.3 8.1 %collective-permute-done.1.c_tail_ref = bf16[8,2048]{1,0:T(8,128)(2,1)S(1)} collective-permute-done((bf16[8,2048]{1,0:T(8,128)(2,1)S(1)}, bf16[8,2048]{1,0:T(8,128)(2,1)S(1)}, u32[]{:S(2)}, u32[]{:S(2)}) %collective-permute-start.1) | collective-permute-done | bytes 32800 | tf_op jit(solution)/shard_map/ppermute | solution.py:310
  17.4 0.0 collective-permute-done.x_tail_ref
  17.4 1.4 copy-done.2
  18.9 1.0 copy-done.4
  19.8 0.7 copy-done.5
  20.6 0.7 copy-done.7
  21.3 0.3 shard_map.109
  21.6 0.0 copy-start
  21.6 1.4 copy-done
  22.9 9.4 %all-to-all-start = ((bf16[16,104,640]{2,1,0:T(8,128)(2,1)}), bf16[16,104,640]{2,1,0:T(8,128)(2,1)S(1)}, u32[]{:S(2)}, u32[]{:S(2)}) async-start(bf16[16,104,640]{2,1,0:T(8,128)(2,1)} %copy-done), calls=%async_computation | async-start | bytes 4259840 | tf_op jit(solution)/shard_map/all_to_all | solution.py:318
  32.3 0.0 copy-start.11
  32.3 0.0 copy-start.12
  32.3 0.0 copy-start.6
  32.4 92.2 %all-to-all-done.m_ref = bf16[16,104,640]{2,1,0:T(8,128)(2,1)S(1)} async-done(((bf16[16,104,640]{2,1,0:T(8,128)(2,1)}), bf16[16,104,640]{2,1,0:T(8,128)(2,1)S(1)}, u32[]{:S(2)}, u32[]{:S(2)}) %all-to-all-start) | async-done | bytes 2129952 | tf_op jit(solution)/shard_map/all_to_all | solution.py:318
  124.6 2.2 shard_map.110
  126.9 4.5 %collective-permute-start.2 = (bf16[16,48,128]{2,1,0:T(8,128)(2,1)S(1)}, bf16[16,48,128]{2,1,0:T(8,128)(2,1)S(1)}, u32[]{:S(2)}, u32[]{:S(2)}) collective-permute-start(bf16[16,48,128]{2,1,0:T(8,128)(2,1)S(1)} %get-tuple-element.19.p0), channel_id=1, source_target_pairs={{0,2},{2,0},{4,6},{6,4},{8,10},{10,8},{12,14},{14,12},{16,18},{18,... | collective-permute-start | bytes 589832 | tf_op jit(solution)/shard_map/ppermute | solution.py:330
  131.4 4.3 %collective-permute-start.3 = (bf16[16,48,128]{2,1,0:T(8,128)(2,1)S(1)}, bf16[16,48,128]{2,1,0:T(8,128)(2,1)S(1)}, u32[]{:S(2)}, u32[]{:S(2)}) collective-permute-start(bf16[16,48,128]{2,1,0:T(8,128)(2,1)S(1)} %get-tuple-element.19.p0), channel_id=1, source_target_pairs={{0,4},{2,6},{4,0},{6,2},{8,12},{10,14},{12,8},{14,10},{16,20},{18,... | collective-permute-start | bytes 589832 | tf_op jit(solution)/shard_map/ppermute | solution.py:330
  135.7 1.9 collective-permute-start.4
  137.7 0.0 copy-done.11
  137.7 0.1 copy.18.bias_ref
  137.7 0.1 copy.19.log_rate_ref
  137.8 6.1 %shard_map.111 = (bf16[16,96,512]{2,1,0:T(8,128)(2,1)S(1)}, bf16[16,96,512]{2,1,0:T(8,128)(2,1)S(1)}, f32[16,8,128]{2,1,0:T(8,128)S(1)}) custom-call(bf16[16,104,640]{2,1,0:T(8,128)(2,1)S(1)} %all-to-all-done.m_ref, bf16[4,512]{1,0:T(4,128)(2,1)S(1)} %copy-done.6, f32[16,8,128]{2,1,0:T(8,128)S(1)} %get-tuple-element.17.steps_ref, f32[8,1]{1,0:T(8,128)S(1)} %copy.18.bias_ref, ...), custom_call_target="tpu_custom_call" | custom-call | flops 20000000 | bytes 6000000 | tf_op jit(solution)/shard_map/pallas_call | solution.py:277
  143.9 0.0 copy-start.8
  143.9 0.0 copy-start.13
  143.9 9.9 %all_to_all.25.totals_ref = f32[16,8,128]{2,1,0:T(8,128)S(1)} all-to-all(f32[16,8,128]{2,1,0:T(8,128)S(1)} %get-tuple-element.21), channel_id=1, replica_groups=mesh['seq'=16,'fsdp'=16,'batch'=2] {'seq'}, dimensions={0} | all-to-all | bytes 131072 | tf_op jit(solution)/shard_map/all_to_all | solution.py:339
  153.8 0.0 collective-permute-done.2.p1
  153.8 0.0 collective-permute-done.3.p2
  153.8 0.0 collective-permute-done.4.p3
  153.8 2.7 shard_map.112
  156.5 5.5 %all-to-all-start.2 = ((bf16[16,16,512]{2,1,0:T(8,128)(2,1)}), bf16[16,16,512]{2,1,0:T(8,128)(2,1)S(1)}, u32[]{:S(2)}, u32[]{:S(2)}) async-start(bf16[16,16,512]{2,1,0:T(8,128)(2,1)} %get-tuple-element.27), calls=%async_computation.2 | async-start | bytes 524288 | tf_op jit(solution)/shard_map/all_to_all | solution.py:351
  162.0 0.1 broadcast_in_dim.3
  162.1 0.1 reshape_reshape.3.skip_ref
  162.2 5.7 %all-to-all-done.2.state_ref = bf16[16,16,512]{2,1,0:T(8,128)(2,1)S(1)} async-done(((bf16[16,16,512]{2,1,0:T(8,128)(2,1)}), bf16[16,16,512]{2,1,0:T(8,128)(2,1)S(1)}, u32[]{:S(2)}, u32[]{:S(2)}) %all-to-all-start.2) | async-done | bytes 262176 | tf_op jit(solution)/shard_map/all_to_all | solution.py:351
  167.9 0.8 shard_map.114
  168.6 5.4 %all-to-all-start.3 = ((bf16[16,16,512]{2,1,0:T(8,128)(2,1)}), bf16[16,16,512]{2,1,0:T(8,128)(2,1)S(1)}, u32[]{:S(2)}, u32[]{:S(2)}) async-start(bf16[16,16,512]{2,1,0:T(8,128)(2,1)} %shard_map.114), calls=%async_computation.3 | async-start | bytes 524288 | tf_op jit(solution)/shard_map/all_to_all | solution.py:353
  174.0 20.0 %all-gather = bf16[64,48,128]{2,1,0:T(8,128)(2,1)S(1)} all-gather(bf16[16,48,128]{2,1,0:T(8,128)(2,1)S(1)} %get-tuple-element.24), channel_id=2, replica_groups={{0,2,4,6},{8,10,12,14},{16,18,20,22},{24,26,28,30},{1,3,5,7},{9,11,13,1..., dimensions={0}, use_global_device_ids=true | all-gather | bytes 983040 | tf_op jit(solution)/shard_map/all_gather | solution.py:350
  194.0 1.4 copy-done.9
  195.4 11.0 %shard_map.113 = (f32[16,96,512]{2,1,0:T(8,128)}, bf16[16,96,256]{2,1,0:T(8,128)(2,1)S(1)}) custom-call(s32[1]{0:T(128)} %bitcast.j_ref, bf16[16,96,512]{2,1,0:T(8,128)(2,1)S(1)} %copy-done.9, bf16[16,96,256]{2,1,0:T(8,128)(2,1)S(1)} %get-tuple-element.22.in_ref, bf16[4,16,48,128]{3,2,1,0:T(8,128)(2,1)S(1)} %bitcast.6, ...), custom_call_target="tpu_custom_call" | custom-call | flops 1600000000 | bytes 8000000 | tf_op jit(solution)/shard_map/pallas_call | solution.py:277
  206.4 0.0 all-to-all-done.3
  206.4 1.9 copy-done.1
  208.3 6.1 %shard_map.115 = bf16[16,96,512]{2,1,0:T(8,128)(2,1)} custom-call(f32[16,96,512]{2,1,0:T(8,128)S(1)} %copy-done.1, bf16[16,96,256]{2,1,0:T(8,128)(2,1)S(1)} %get-tuple-element.26.out_ref, bf16[256,512]{1,0:T(8,128)(2,1)S(1)} %bitcast.5, f32[16,8,128]{2,1,0:T(8,128)S(1)} %get-tuple-element.17.steps_ref, f32[8,1]{1,0:T(8,128)S(1)} %copy.18.bias_ref, ...), custom_call_target="tpu_custom_call" | custom-call | flops 400000000 | bytes 6000000 | tf_op jit(solution)/shard_map/pallas_call | solution.py:277
  214.4 8.0 %all-to-all-start.4 = ((bf16[16,96,512]{2,1,0:T(8,128)(2,1)}), bf16[16,96,512]{2,1,0:T(8,128)(2,1)S(1)}, u32[]{:S(2)}, u32[]{:S(2)}) async-start(bf16[16,96,512]{2,1,0:T(8,128)(2,1)} %shard_map.115), calls=%async_computation.4 | async-start | bytes 3145728 | tf_op jit(solution)/shard_map/all_to_all | solution.py:370
  222.4 73.3 %all-to-all-done.4.refs_0_ = bf16[16,96,512]{2,1,0:T(8,128)(2,1)S(1)} async-done(((bf16[16,96,512]{2,1,0:T(8,128)(2,1)}), bf16[16,96,512]{2,1,0:T(8,128)(2,1)S(1)}, u32[]{:S(2)}, u32[]{:S(2)}) %all-to-all-start.4) | async-done | bytes 1572896 | tf_op jit(solution)/shard_map/all_to_all | solution.py:370
  295.8 2.7 shard_map.116
  (16 shorter events, 0.0 us)
Async XLA Ops:
  0.9 16.5 %collective-permute-start = (bf16[8,8192]{1,0:T(8,128)(2,1)S(1)}, bf16[8,8192]{1,0:T(8,128)(2,1)S(1)}, u32[]{:S(2)}, u32[]{:S(2)}) collective-permute-start(bf16[8,8192]{1,0:T(8,128)(2,1)S(1)} %slice.6), channel_id=1, source_target_pairs={{0,2},{2,4},{4,6},{6,8},{8,10},{10,12},{12,14},{14,16},{16,18},{18... | collective-permute-start | bytes 393224 | tf_op jit(solution)/shard_map/ppermute | solution.py:310
  5.5 11.9 %collective-permute-start.1 = (bf16[8,2048]{1,0:T(8,128)(2,1)S(1)}, bf16[8,2048]{1,0:T(8,128)(2,1)S(1)}, u32[]{:S(2)}, u32[]{:S(2)}) collective-permute-start(bf16[8,2048]{1,0:T(8,128)(2,1)S(1)} %slice.7), channel_id=1, source_target_pairs={{0,2},{2,4},{4,6},{6,8},{8,10},{10,12},{12,14},{14,16},{16,18},{18... | collective-permute-start | bytes 98312 | tf_op jit(solution)/shard_map/ppermute | solution.py:310
  17.4 1.4 copy-start.2
  18.9 1.0 copy-start.4
  19.8 0.7 copy-start.5
  20.6 0.7 copy-start.7
  21.6 1.4 copy-start
  22.9 101.7 %all-to-all-start = ((bf16[16,104,640]{2,1,0:T(8,128)(2,1)}), bf16[16,104,640]{2,1,0:T(8,128)(2,1)S(1)}, u32[]{:S(2)}, u32[]{:S(2)}) async-start(bf16[16,104,640]{2,1,0:T(8,128)(2,1)} %copy-done), calls=%async_computation | async-start | bytes 4259840 | tf_op jit(solution)/shard_map/all_to_all | solution.py:318
  32.3 105.3 %copy-start.11 = (f32[8]{0:T(128)S(1)}, f32[8]{0:T(128)}, u32[]{:S(2)}) copy-start(f32[8]{0:T(128)} %param.17) | copy-start | bytes 100
  32.3 105.4 %copy-start.12 = (f32[8]{0:T(128)S(1)}, f32[8]{0:T(128)}, u32[]{:S(2)}) copy-start(f32[8]{0:T(128)} %param.18) | copy-start | bytes 100
  32.3 105.5 %copy-start.6 = (bf16[4,512]{1,0:T(4,128)(2,1)S(1)}, bf16[4,512]{1,0:T(4,128)(2,1)}, u32[]{:S(2)}) copy-start(bf16[4,512]{1,0:T(4,128)(2,1)} %taps_ref.3) | copy-start | bytes 12292
  126.9 26.9 %collective-permute-start.2 = (bf16[16,48,128]{2,1,0:T(8,128)(2,1)S(1)}, bf16[16,48,128]{2,1,0:T(8,128)(2,1)S(1)}, u32[]{:S(2)}, u32[]{:S(2)}) collective-permute-start(bf16[16,48,128]{2,1,0:T(8,128)(2,1)S(1)} %get-tuple-element.19.p0), channel_id=1, source_target_pairs={{0,2},{2,0},{4,6},{6,4},{8,10},{10,8},{12,14},{14,12},{16,18},{18,... | collective-permute-start | bytes 589832 | tf_op jit(solution)/shard_map/ppermute | solution.py:330
  131.4 22.4 %collective-permute-start.3 = (bf16[16,48,128]{2,1,0:T(8,128)(2,1)S(1)}, bf16[16,48,128]{2,1,0:T(8,128)(2,1)S(1)}, u32[]{:S(2)}, u32[]{:S(2)}) collective-permute-start(bf16[16,48,128]{2,1,0:T(8,128)(2,1)S(1)} %get-tuple-element.19.p0), channel_id=1, source_target_pairs={{0,4},{2,6},{4,0},{6,2},{8,12},{10,14},{12,8},{14,10},{16,20},{18,... | collective-permute-start | bytes 589832 | tf_op jit(solution)/shard_map/ppermute | solution.py:330
  135.7 18.1 %collective-permute-start.4 = (bf16[16,48,128]{2,1,0:T(8,128)(2,1)S(1)}, bf16[16,48,128]{2,1,0:T(8,128)(2,1)S(1)}, u32[]{:S(2)}, u32[]{:S(2)}) collective-permute-start(bf16[16,48,128]{2,1,0:T(8,128)(2,1)S(1)} %get-tuple-element.19.p0), channel_id=1, source_target_pairs={{0,6},{2,4},{4,2},{6,0},{8,14},{10,12},{12,10},{14,8},{16,22},{18,... | collective-permute-start | bytes 589832 | tf_op jit(solution)/shard_map/ppermute | solution.py:330
  143.9 12.6 %copy-start.8 = (bf16[16,96,512]{2,1,0:T(8,128)(2,1)}, bf16[16,96,512]{2,1,0:T(8,128)(2,1)S(1)}, u32[]{:S(2)}) copy-start(bf16[16,96,512]{2,1,0:T(8,128)(2,1)S(1)} %get-tuple-element.18.x_ref) | copy-start | bytes 4718596
  143.9 18.1 %copy-start.13 = (f32[8]{0:T(128)S(1)}, f32[8]{0:T(128)}, u32[]{:S(2)}) copy-start(f32[8]{0:T(128)} %param.19) | copy-start | bytes 100
  156.5 11.4 %all-to-all-start.2 = ((bf16[16,16,512]{2,1,0:T(8,128)(2,1)}), bf16[16,16,512]{2,1,0:T(8,128)(2,1)S(1)}, u32[]{:S(2)}, u32[]{:S(2)}) async-start(bf16[16,16,512]{2,1,0:T(8,128)(2,1)} %get-tuple-element.27), calls=%async_computation.2 | async-start | bytes 524288 | tf_op jit(solution)/shard_map/all_to_all | solution.py:351
  168.6 37.8 %all-to-all-start.3 = ((bf16[16,16,512]{2,1,0:T(8,128)(2,1)}), bf16[16,16,512]{2,1,0:T(8,128)(2,1)S(1)}, u32[]{:S(2)}, u32[]{:S(2)}) async-start(bf16[16,16,512]{2,1,0:T(8,128)(2,1)} %shard_map.114), calls=%async_computation.3 | async-start | bytes 524288 | tf_op jit(solution)/shard_map/all_to_all | solution.py:353
  194.0 1.4 copy-start.9
  206.4 1.9 copy-start.1
  214.4 8.0 %copy-start.10 = (bf16[8192]{0:T(1024)(128)(2,1)S(1)}, bf16[8192]{0:T(1024)(128)(2,1)}, u32[]{:S(2)}) copy-start(bf16[8192]{0:T(1024)(128)(2,1)} %param.20) | copy-start | bytes 49156
  214.4 81.4 %copy-start.3 = (bf16[96,8192]{1,0:T(8,128)(2,1)S(1)}, bf16[96,8192]{1,0:T(8,128)(2,1)}, u32[]{:S(2)}) copy-start(bf16[96,8192]{1,0:T(8,128)(2,1)} %refs_1_.1) | copy-start | bytes 4718596
  214.4 81.4 %all-to-all-start.4 = ((bf16[16,96,512]{2,1,0:T(8,128)(2,1)}), bf16[16,96,512]{2,1,0:T(8,128)(2,1)S(1)}, u32[]{:S(2)}, u32[]{:S(2)}) async-start(bf16[16,96,512]{2,1,0:T(8,128)(2,1)} %shard_map.115), calls=%async_computation.4 | async-start | bytes 3145728 | tf_op jit(solution)/shard_map/all_to_all | solution.py:370

commit v3 on v2

--- a/solution.py
+++ b/solution.py
@@ -16,6 +16,7 @@
 BF16 = jnp.bfloat16
 exact = lax.Precision.HIGHEST
 params = pltpu.CompilerParams(vmem_limit_bytes=48 * 2**20)
+wide = pltpu.CompilerParams(vmem_limit_bytes=60 * 2**20)
 
 
 def iota(shape, dim):
@@ -33,6 +34,14 @@
     return dt.reshape(count * heads, lanes), cum, cum[:, rows - 1 : rows]
 
 
+def sums_of_others(cum, rows, heads, later):
+    size = (cum.shape[0], cum.shape[0])
+    mine, other = iota(size, 0), iota(size, 1)
+    beyond = other // heads > mine // heads if later else other // heads < mine // heads
+    chosen = jnp.where((mine % heads == other % heads) & beyond, 1.0, 0.0).astype(F32)
+    return jnp.dot(chosen, cum, precision=exact, preferred_element_type=F32)[:, rows - 1 : rows]
+
+
 def high_low(table):
     high = table.astype(BF16).astype(F32)
     return high, table - high
@@ -66,37 +75,39 @@
     return pltpu.roll(block, HEAD_DIM, 1)
 
 
-def pack_kernel(x_ref, coupling_ref, steps_ref, x_tail_ref, c_tail_ref, taps_ref, out_ref):
+def pack_kernel(x_ref, b_ref, c_ref, steps_ref, x_tail_ref, b_tail_ref, c_tail_ref, taps_ref, out_ref, turned_steps):
     count, _, lanes = out_ref.shape
     width = lanes - LANES
     rows = x_ref.shape[0]
-    heads = steps_ref.shape[1] // count
+    g = pl.program_id(0)
+    heads = steps_ref.shape[1] // GROUPS // count
     left = iota((HALO + rows, LANES), 1) < HEAD_DIM
     below = iota((HALO, width), 0) >= HALO - 3
     below_c = iota((HALO, LANES), 0) >= HALO - 3
-    steps = steps_ref[...].astype(F32)
-    steps = jnp.transpose(jnp.concatenate([steps, jnp.zeros((LANES - rows, steps.shape[1]), F32)], axis=0))
+
+    @pl.when(g == 0)
+    def _():
+        steps = steps_ref[...].astype(F32)
+        turned_steps[...] = jnp.transpose(
+            jnp.concatenate([steps, jnp.zeros((LANES - rows, steps.shape[1]), F32)], axis=0)
+        )
+
     own_taps = taps_ref[...].astype(F32)
-    pair_width = GROUPS * STATE
-    for d in range(count):
-        g, j = d // 4, d % 4
-        own = steps[d * heads : (d + 1) * heads]
+    for j in range(count):
+        own = turned_steps[pl.ds(pl.multiple_of((g * count + j) * heads, heads), heads)]
         top = jnp.concatenate([own[:4], own[4:], jnp.zeros((4, width - 2 * LANES), F32)], axis=1)
         top = jnp.concatenate([top, jnp.zeros((HALO - 4, width), F32)], axis=0)
-        lanes_d = slice(d * width, (d + 1) * width)
-        top = jnp.where(below, x_tail_ref[:, lanes_d].astype(F32), top)
-        out_ref[d, :, :width] = jnp.concatenate([top, x_ref[:, lanes_d].astype(F32)], axis=0).astype(BF16)
+        lanes_j = slice(j * width, (j + 1) * width)
+        top = jnp.where(below, x_tail_ref[:, lanes_j].astype(F32), top)
+        out_ref[j, :, :width] = jnp.concatenate([top, x_ref[:, lanes_j].astype(F32)], axis=0).astype(BF16)
         taps = own_taps if j % 2 == 0 else turned(own_taps)
         taps = jnp.concatenate([taps, jnp.zeros((HALO - 4, LANES), F32)], axis=0)
-        blocks = []
-        for r in range(2):
-            at = r * pair_width + g * STATE + j // 2 * LANES
-            tail = c_tail_ref[:, at : at + LANES].astype(F32)
-            blocks.append(jnp.concatenate([tail, coupling_ref[:, at : at + LANES].astype(F32)], axis=0))
-        b, c = blocks
+        half = slice(j // 2 * LANES, (j // 2 + 1) * LANES)
+        b = jnp.concatenate([b_tail_ref[:, half].astype(F32), b_ref[:, half].astype(F32)], axis=0)
+        c = jnp.concatenate([c_tail_ref[:, half].astype(F32), c_ref[:, half].astype(F32)], axis=0)
         both = jnp.where(left, b, turned(c)) if j % 2 == 0 else jnp.where(left, turned(b), c)
         both = jnp.concatenate([jnp.where(below_c, both[:HALO], taps), both[HALO:]], axis=0)
-        out_ref[d, :, width:] = both.astype(BF16)
+        out_ref[j, :, width:] = both.astype(BF16)
 
 
 def coupling_kernel(from_ref, m_ref, b_ref, c_ref, steps_ref, scratch):
@@ -135,13 +146,12 @@
     count, rows, width = x_ref.shape
     heads = steps_ref.shape[1]
     dt, cum, tot = decay_tables(steps_ref, bias_ref, log_rate_ref, rows)
-    size = (count * heads, count * heads)
-    later_mat = jnp.where(
-        (iota(size, 0) % heads == iota(size, 1) % heads) & (iota(size, 1) // heads > iota(size, 0) // heads), 1.0, 0.0
-    ).astype(F32)
-    later = jnp.dot(later_mat, cum, precision=exact, preferred_element_type=F32)[:, rows - 1 : rows]
+    later = sums_of_others(cum, rows, heads, True)
     fill(table, high_low(jnp.exp(later + (tot - cum)) * dt))
-    total_ref[...] = jnp.broadcast_to((tot[0:heads] + later[0:heads, 0:1])[None], total_ref.shape)
+    own = iota((heads, width), 0) == iota((heads, width), 1) // HEAD_DIM
+    section = jnp.broadcast_to(tot[0:heads] + later[0:heads, 0:1], own.shape)
+    logs = jnp.sum(jnp.where(own, section, 0.0), axis=0, keepdims=True)
+    total_ref[...] = jnp.broadcast_to(logs, total_ref.shape)
     taps = taps_ref[...].astype(F32)
     spread = spread_matrix(heads, width, 0)
 
@@ -156,53 +166,57 @@
     lax.fori_loop(0, count, body, 0)
 
 
-def state_kernel(p0, p1, p2, p3, weighted_ref, totals_ref, state_ref, in_ref, decay_ref):
+def state_kernel(p0, p1, p2, p3, weighted_ref, logs_ref, state_ref, in_ref):
     count, rows, width = weighted_ref.shape
-    heads = totals_ref.shape[1]
+    sections, share_rows, _ = state_ref.shape
 
     def body(c, _):
         in_ref[c] = unpacked([p[c] for p in (p0, p1, p2, p3)])
         return 0
 
-    lax.fori_loop(0, count, body, 0)
-    own = iota((heads, width), 0) == iota((heads, width), 1) // HEAD_DIM
-    for s in range(totals_ref.shape[0]):
-        logs = jnp.where(own, jnp.broadcast_to(totals_ref[s][:, :1], own.shape), 0.0)
-        decay_ref[s : s + 1] = jnp.exp(jnp.sum(logs, axis=0, keepdims=True))
+    lax.fori_loop(0, count, body, 0, unroll=4)
     state = lax.dot_general(
         in_ref[...].reshape(count * rows, STATE),
         weighted_ref[...].reshape(count * rows, width),
         (((0,), (0,)), ((), ())),
         preferred_element_type=F32,
     )
-    state_ref[...] = state.reshape(state_ref.shape).astype(BF16)
-
-
-def relay_kernel(state_ref, decay_ref, out_ref):
-    carried = jnp.zeros(state_ref.shape[1:], F32)
+    high, low = high_low(logs_ref[...])
+    logs = jnp.where(iota(high.shape, 0) == 0, high, low)
+    share = STATE // sections
+    for s in range(sections):
+        block = jnp.concatenate([state[s * share : (s + 1) * share], logs], axis=0)
+        state_ref[s] = block.astype(BF16)
+
+
+def relay_kernel(state_ref, out_ref):
+    share = out_ref.shape[1]
+    carried = jnp.zeros(out_ref.shape[1:], F32)
     for s in range(state_ref.shape[0]):
         out_ref[s] = carried.astype(BF16)
-        carried = decay_ref[s : s + 1] * carried + state_ref[s].astype(F32)
-
-
-def scan_kernel(j_ref, x_ref, in_ref, c_ref, steps_ref, bias_ref, log_rate_ref, skip_ref,
-                y_ref, out_ref, state, table, column_logs, row_logs):
+        block = state_ref[s].astype(F32)
+        decay = jnp.exp(block[share : share + 1] + block[share + 1 : share + 2])
+        carried = decay * carried + block[:share]
+
+
+def scan_kernel(x_ref, in_ref, p0, p1, p2, p3, steps_ref, bias_ref, log_rate_ref, skip_ref,
+                y_ref, out_ref, scale_ref, state, table, column_logs, row_logs):
     count, rows, width = x_ref.shape
     heads = steps_ref.shape[1]
     dt, cum, tot = decay_tables(steps_ref, bias_ref, log_rate_ref, rows)
     blocked = (count, heads, dt.shape[1])
-    fill(table, high_low(jnp.exp(tot - cum) * dt) + high_low(jnp.exp(cum)))
+    earlier = sums_of_others(cum, rows, heads, False)
+    fill(table, high_low(jnp.exp(tot - cum) * dt) + high_low(jnp.exp(cum)) + high_low(jnp.exp(earlier + cum)))
     column_logs[...] = (cum * LOG2E).reshape(blocked)
     row_logs[...] = ((jnp.log(dt) - cum) * LOG2E).reshape(blocked)
-    spread_in, spread_out = spread_matrix(heads, width, 0), spread_matrix(heads, width, 2)
+    spread_in, spread_out, spread_all = (spread_matrix(heads, width, k) for k in (0, 2, 4))
     skip = skip_ref[...]
     state[...] = jnp.zeros(state.shape, F32)
     causal = iota((rows, rows), 0) >= iota((rows, rows), 1)
     left = iota((rows, LANES), 1) < HEAD_DIM
-    order = [lax.bitwise_xor(j_ref[0], d) for d in range(4)]
 
     def body(c, _):
-        q = unpacked([c_ref[k, c] for k in order])
+        q = unpacked([p[c] for p in (p0, p1, p2, p3)])
         out_ref[c] = q
         b, x = in_ref[c], x_ref[c]
         meet = lax.dot_general(q, b, (((1,), (1,)), ((), ())), preferred_element_type=F32)
@@ -210,6 +224,7 @@
         columns = jnp.transpose(table[c])[:rows].astype(BF16)
         scale_in = jnp.dot(columns, spread_in, preferred_element_type=F32)
         scale_out = jnp.dot(columns, spread_out, preferred_element_type=F32)
+        scale_ref[c] = jnp.dot(columns, spread_all, preferred_element_type=F32)
         logs = jnp.transpose(column_logs[c])[:rows]
         rows_c = row_logs[c]
         carried = jnp.dot(q, state[...].astype(BF16), preferred_element_type=F32) * scale_out
@@ -231,27 +246,15 @@
     lax.fori_loop(0, count, body, 0)
 
 
-def carry_kernel(y_ref, out_ref, incoming_ref, steps_ref, bias_ref, log_rate_ref, sum_ref, table):
-    count, rows, width = y_ref.shape
-    heads = steps_ref.shape[1]
-    _, cum, tot = decay_tables(steps_ref, bias_ref, log_rate_ref, rows)
-    size = (count * heads, count * heads)
-    earlier_mat = jnp.where(
-        (iota(size, 0) % heads == iota(size, 1) % heads) & (iota(size, 1) // heads < iota(size, 0) // heads), 1.0, 0.0
-    ).astype(F32)
-    earlier = jnp.dot(earlier_mat, cum, precision=exact, preferred_element_type=F32)[:, rows - 1 : rows]
-    fill(table, high_low(jnp.exp(earlier + cum)))
-    spread = spread_matrix(heads, width, 0)
+def carry_kernel(y_ref, out_ref, scale_ref, incoming_ref, sum_ref):
     incoming = incoming_ref[...]
 
     def body(c, _):
-        columns = jnp.transpose(table[c])[:rows].astype(BF16)
-        scale = jnp.dot(columns, spread, preferred_element_type=F32)
         carried = jnp.dot(out_ref[c], incoming, preferred_element_type=F32)
-        sum_ref[c] = (y_ref[c] + carried * scale).astype(BF16)
+        sum_ref[c] = (y_ref[c] + carried * scale_ref[c]).astype(BF16)
         return 0
 
-    lax.fori_loop(0, count, body, 0)
+    lax.fori_loop(0, y_ref.shape[0], body, 0, unroll=4)
 
 
 def finish_kernel(*refs):
@@ -308,13 +311,32 @@
 
     route = [(i, i + 1) for i in range(seq * ring - 1)]
     x_tail, c_tail = lax.ppermute((ssm_input[rows - HALO :], coupling[rows - HALO :]), ("seq", "fsdp"), route)
-    message = call(
+    group_width = channels // GROUPS
+
+    def columns_of(count, size, first):
+        return pl.BlockSpec((count, size), lambda g: (0, first + g))
+
+    def same(*shape):
+        return pl.BlockSpec(shape, lambda g: (0,) * len(shape))
+
+    message = pl.pallas_call(
         pack_kernel,
-        struct((ring, HALO + rows, width + LANES), BF16),
-        [],
-        (ssm_input, coupling, step_input, x_tail, c_tail, conv_coupling),
-        (0, 4000000),
-    )
+        grid=(GROUPS,),
+        out_shape=struct((ring, HALO + rows, width + LANES), BF16),
+        in_specs=[
+            columns_of(rows, group_width, 0),
+            columns_of(rows, STATE, 0),
+            columns_of(rows, STATE, GROUPS),
+            same(*step_input.shape),
+            columns_of(HALO, group_width, 0),
+            columns_of(HALO, STATE, 0),
+            columns_of(HALO, STATE, GROUPS),
+            same(*conv_coupling.shape),
+        ],
+        out_specs=pl.BlockSpec((ring // GROUPS, HALO + rows, width + LANES), lambda g: (g, 0, 0)),
+        scratch_shapes=[pltpu.VMEM((LANES, LANES), F32)],
+        compiler_params=wide,
+    )(ssm_input, coupling, coupling, step_input, x_tail, c_tail, c_tail, conv_coupling)
     message = lax.all_to_all(message, "fsdp", 0, 0)
 
     senders = 2 * (place // 4) + place % 4 // 2 + jnp.array([0, 2 * GROUPS], jnp.int32)
@@ -329,47 +351,37 @@
     )
     pieces = [own_in] + [lax.ppermute(own_in, "fsdp", [(i, i ^ d) for i in range(ring)]) for d in range(1, 4)]
     blocks = (ring, rows, width)
-    x, weighted, totals = call(
+    x, weighted, logs = call(
         input_kernel,
-        (struct(blocks, BF16), struct(blocks, BF16), struct((seq, heads, LANES), F32)),
+        (struct(blocks, BF16), struct(blocks, BF16), struct((8, width), F32)),
         [pltpu.VMEM((HALO + rows, width), F32), pltpu.VMEM((ring, LANES, LANES), F32)],
         (message, conv_input, steps, bias, rate),
-        (20000000, 6000000),
-    )
-    totals = lax.all_to_all(totals, "seq", 0, 0)
+        (6000000000, 6000000),
+    )
+    own_out, weighted = lax.optimization_barrier((own_out, weighted))
+    out_pieces = [own_out] + [lax.ppermute(own_out, "fsdp", [(i, i ^ d) for i in range(ring)]) for d in range(1, 4)]
     share = STATE // seq
-    state, read_in, decay = call(
+    state, read_in = call(
         state_kernel,
-        (struct((seq, share, width), BF16), struct((ring, rows, STATE), BF16), struct((seq, width), F32)),
+        (struct((seq, share + 8, width), BF16), struct((ring, rows, STATE), BF16)),
         [],
-        (*pieces, weighted, totals),
-        (400000000, 5000000),
-    )
-    fours = [[4 * g + j for j in range(4)] for g in range(ring // 4)]
-    own_out, _ = lax.optimization_barrier((own_out, read_in))
-    all_out = lax.all_gather(own_out, "fsdp", axis=0, axis_index_groups=fours)
+        (*pieces, weighted, logs),
+        (2000000000, 5000000),
+    )
     state = lax.all_to_all(state, "seq", 0, 0)
-    incoming = call(relay_kernel, struct((seq, share, width), BF16), [], (state, decay), (1000000, 600000))
+    incoming = call(relay_kernel, struct((seq, share, width), BF16), [], (state,), (500000000, 600000))
     incoming = lax.all_to_all(incoming, "seq", 0, 0).reshape(STATE, width)
     table = pltpu.VMEM((ring, heads, LANES), F32)
-    y, read_out = call(
+    y, read_out, scale = call(
         scan_kernel,
-        (struct(blocks, F32), struct((ring, rows, STATE), BF16)),
+        (struct(blocks, F32), struct((ring, rows, STATE), BF16), struct(blocks, F32)),
         [pltpu.VMEM((STATE, width), F32), pltpu.VMEM((ring, LANES, LANES), F32), table, table],
-        ((place % 4).reshape(1), x, read_in, all_out, steps, bias, rate, jnp.repeat(skip_gain, HEAD_DIM).reshape(1, width)),
-        (1600000000, 8000000),
-        True,
-    )
-    y = call(
-        carry_kernel,
-        struct(blocks, BF16),
-        [pltpu.VMEM((ring, LANES, LANES), F32)],
-        (y, read_out, incoming, steps, bias, rate),
-        (400000000, 6000000),
-    )
+        (x, read_in, *out_pieces, steps, bias, rate, jnp.repeat(skip_gain, HEAD_DIM).reshape(1, width)),
+        (10000000000, 8000000),
+    )
+    y = call(carry_kernel, struct(blocks, BF16), [], (y, read_out, scale, incoming), (3000000000, 6000000))
     y = lax.all_to_all(y, "fsdp", 0, 0)
 
-    group_width = channels // GROUPS
     return pl.pallas_call(
         finish_kernel,
         grid=(GROUPS,),
@@ -381,7 +393,7 @@
         ],
         out_specs=pl.BlockSpec((rows, group_width), lambda g: (0, g)),
         scratch_shapes=[pltpu.VMEM((rows, group_width), F32)],
-        compiler_params=params,
+        compiler_params=wide,
     )(y, gate_input, norm_gain.reshape(1, -1))
 
 

time: 299 us -> 286 us (0.957)
  blocking collectives: 29.9 us -> 0 us
  starting transfers between devices: 46.6 us -> 59.3 us
  Pallas kernels: 31.8 us -> 35.9 us
    all_gather x1 -> x0, blocking collectives: 20 us -> none  [local(): all_out = lax.all_gather(own_out, 'fsdp', axis=0, axis_index_groups=fours)]
    ppermute x0 -> x3, starting transfers between devices: none -> 10.1 us  [local(): lax.ppermute(own_out, 'fsdp', [(i, i ^ d) for i in range(ring)])]
    all_to_all x1 -> x0, blocking collectives: 9.88 us -> none  [local(): totals = lax.all_to_all(totals, 'seq', 0, 0)]
    all_to_all x1, waiting for transfers between devices: 5.68 us -> 0.01 us  [local(): state = lax.all_to_all(state, 'seq', 0, 0)]
    ppermute x3, waiting for transfers between devices: 0.01 us -> 4.22 us  [local(): lax.ppermute(own_in, 'fsdp', [(i, i ^ d) for i in range(ring)])]
    pallas_call x0 -> x1, Pallas kernels: none -> 4.07 us  [local(): pl.pallas_call(pack_kernel, grid=(GROUPS,), out_shape=struct((ring, HALO...]
    pallas_call x7 -> x6, Pallas kernels: 29.2 us -> 27.3 us  [call(): pl.pallas_call(kernel, out_shape=outs, in_specs=specs, out_specs=jax.tree...]
    unnamed x28 -> x22, local copies, waits for them, and re-layouts: 8.52 us -> 6.92 us
  transfers between devices with their start and end apart: 9 -> 12, of which waited for: 4 -> 5; matrix products, arithmetic and copies ran while one was open for 0% -> 1% of each run, Pallas kernels for 6% -> 7%
where the time goes in v3:
time: 286 us; the launch traced here: 285 us
  waiting for transfers between devices  180 us (63%)
  starting transfers between devices  59.3 us (21%)
  Pallas kernels  35.9 us (13%)
  local copies, waits for them, and re-layouts  9.53 us (3%)
    all_to_all x1, waiting for transfers between devices, local(): message = lax.all_to_all(message, 'fsdp', 0, 0)  92.1 us
    all_to_all x1, waiting for transfers between devices, local(): y = lax.all_to_all(y, 'fsdp', 0, 0)  73 us
    pallas_call x6, Pallas kernels, call(): pl.pallas_call(kernel, out_shape=outs, in_specs=specs, out_specs=jax.tree...  27.3 us
    ppermute x3, starting transfers between devices, local(): lax.ppermute(own_in, 'fsdp', [(i, i ^ d) for i in range(ring)])  10.7 us
    ppermute x3, starting transfers between devices, local(): lax.ppermute(own_out, 'fsdp', [(i, i ^ d) for i in range(ring)])  10.1 us
    all_to_all x1, starting transfers between devices, local(): y = lax.all_to_all(y, 'fsdp', 0, 0)  9.78 us
    all_to_all x1, starting transfers between devices, local(): message = lax.all_to_all(message, 'fsdp', 0, 0)  9.52 us
    ppermute x2, waiting for transfers between devices, local(): lax.ppermute((ssm_input[rows - HALO:], coupling[rows - HALO:]), ('seq', '...  8.1 us
  transfers between devices with their start and end apart: 12, of which 5 were waited for; matrix products, arithmetic and copies ran while one was open for 1% of the time, Pallas kernels for 7%

profile of v3, /device:TPU:6, one launch (start us, length us, event | category | flops | bytes accessed | tf_op | source)
XLA Modules:
  0.0 285.4 jit_solution(14351279920112163792)
XLA Ops:
  0.0 0.9 slice.6
  0.9 3.8 %collective-permute-start = (bf16[8,8192]{1,0:T(8,128)(2,1)S(1)}, bf16[8,8192]{1,0:T(8,128)(2,1)S(1)}, u32[]{:S(2)}, u32[]{:S(2)}) collective-permute-start(bf16[8,8192]{1,0:T(8,128)(2,1)S(1)} %slice.6), channel_id=1, source_target_pairs={{0,2},{2,4},{4,6},{6,8},{8,10},{10,12},{12,14},{14,16},{16,18},{18... | collective-permute-start | bytes 393224 | tf_op jit(solution)/shard_map/ppermute | solution.py:313
  4.8 0.8 slice.7
  5.5 3.8 %collective-permute-start.1 = (bf16[8,2048]{1,0:T(8,128)(2,1)S(1)}, bf16[8,2048]{1,0:T(8,128)(2,1)S(1)}, u32[]{:S(2)}, u32[]{:S(2)}) collective-permute-start(bf16[8,2048]{1,0:T(8,128)(2,1)S(1)} %slice.7), channel_id=1, source_target_pairs={{0,2},{2,4},{4,6},{6,8},{8,10},{10,12},{12,14},{14,16},{16,18},{18... | collective-permute-start | bytes 98312 | tf_op jit(solution)/shard_map/ppermute | solution.py:313
  9.3 8.1 %collective-permute-done.1.b_tail_ref.c_tail_ref = bf16[8,2048]{1,0:T(8,128)(2,1)S(1)} collective-permute-done((bf16[8,2048]{1,0:T(8,128)(2,1)S(1)}, bf16[8,2048]{1,0:T(8,128)(2,1)S(1)}, u32[]{:S(2)}, u32[]{:S(2)}) %collective-permute-start.1) | collective-permute-done | bytes 32800 | tf_op jit(solution)/shard_map/ppermute | solution.py:313
  17.4 0.0 collective-permute-done.x_tail_ref
  17.4 0.6 copy-done.5
  18.0 0.7 copy-done.6
  18.7 4.1 %shard_map.109 = bf16[16,104,640]{2,1,0:T(8,128)(2,1)} custom-call(bf16[96,8192]{1,0:T(8,128)(2,1)} %x_ref.1, bf16[96,2048]{1,0:T(8,128)(2,1)} %c_ref.1, bf16[96,2048]{1,0:T(8,128)(2,1)} %c_ref.1, bf16[96,128]{1,0:T(8,128)(2,1)} %steps_ref.1, bf16[8,8192]{1,0:T(8,128)(2,1)} %copy-done.6, bf16[8,2048]{1,0:T(8,128)(2,1)} %copy-done.5, ...), custom_call_target="tpu_custom_call" | custom-call | tf_op jit(solution)/shard_map/pallas_call | solution.py:322
  22.8 9.5 %all-to-all-start = ((bf16[16,104,640]{2,1,0:T(8,128)(2,1)}), bf16[16,104,640]{2,1,0:T(8,128)(2,1)S(1)}, u32[]{:S(2)}, u32[]{:S(2)}) async-start(bf16[16,104,640]{2,1,0:T(8,128)(2,1)} %shard_map.109), calls=%async_computation | async-start | bytes 4259840 | tf_op jit(solution)/shard_map/all_to_all | solution.py:340
  32.3 0.0 copy-start
  32.4 0.0 copy-done.8
  32.4 0.1 copy.12.bias_ref
  32.5 0.1 copy.13.log_rate_ref
  32.5 92.1 %all-to-all-done.m_ref = bf16[16,104,640]{2,1,0:T(8,128)(2,1)S(1)} async-done(((bf16[16,104,640]{2,1,0:T(8,128)(2,1)}), bf16[16,104,640]{2,1,0:T(8,128)(2,1)S(1)}, u32[]{:S(2)}, u32[]{:S(2)}) %all-to-all-start) | async-done | bytes 2129952 | tf_op jit(solution)/shard_map/all_to_all | solution.py:340
  124.6 2.2 shard_map.110
  126.9 6.3 %collective-permute-start.4 = (bf16[16,48,128]{2,1,0:T(8,128)(2,1)S(1)}, bf16[16,48,128]{2,1,0:T(8,128)(2,1)S(1)}, u32[]{:S(2)}, u32[]{:S(2)}) collective-permute-start(bf16[16,48,128]{2,1,0:T(8,128)(2,1)S(1)} %get-tuple-element.20.p0), channel_id=1, source_target_pairs={{0,6},{2,4},{4,2},{6,0},{8,14},{10,12},{12,10},{14,8},{16,22},{18,... | collective-permute-start | bytes 589832 | tf_op jit(solution)/shard_map/ppermute | solution.py:352
  133.2 1.9 collective-permute-start.3
  135.2 2.5 collective-permute-start.2
  137.7 6.0 %shard_map.111 = (bf16[16,96,512]{2,1,0:T(8,128)(2,1)S(1)}, bf16[16,96,512]{2,1,0:T(8,128)(2,1)S(1)}, f32[8,512]{1,0:T(8,128)S(1)}) custom-call(bf16[16,104,640]{2,1,0:T(8,128)(2,1)S(1)} %all-to-all-done.m_ref, bf16[4,512]{1,0:T(4,128)(2,1)S(1)} %copy-done, f32[16,8,128]{2,1,0:T(8,128)S(1)} %get-tuple-element.18.steps_ref, f32[8,1]{1,0:T(8,128)S(1)} %copy.12.bias_ref, ...), custom_call_target="tpu_custom_call" | custom-call | flops 6000000000 | bytes 6000000 | tf_op jit(solution)/shard_map/pallas_call | solution.py:280
  143.7 0.0 copy-start.2
  143.7 1.1 copy-done.2
  144.9 0.0 collective-permute-done.4.p3
  144.9 4.2 %collective-permute-done.3.p2 = bf16[16,48,128]{2,1,0:T(8,128)(2,1)S(1)} collective-permute-done((bf16[16,48,128]{2,1,0:T(8,128)(2,1)S(1)}, bf16[16,48,128]{2,1,0:T(8,128)(2,1)S(1)}, u32[]{:S(2)}, u32[]{:S(2)}) %collective-permute-start.3) | collective-permute-done | bytes 196640 | tf_op jit(solution)/shard_map/ppermute | solution.py:352
  149.1 0.0 collective-permute-done.2.p1
  149.1 1.9 shard_map.112
  150.9 5.8 %all-to-all-start.1 = ((bf16[16,24,512]{2,1,0:T(8,128)(2,1)}), bf16[16,24,512]{2,1,0:T(8,128)(2,1)S(1)}, u32[]{:S(2)}, u32[]{:S(2)}) async-start(bf16[16,24,512]{2,1,0:T(8,128)(2,1)} %get-tuple-element.30), calls=%async_computation.1 | async-start | bytes 786432 | tf_op jit(solution)/shard_map/all_to_all | solution.py:371
  156.7 3.6 %collective-permute-start.7 = (bf16[16,48,128]{2,1,0:T(8,128)(2,1)S(1)}, bf16[16,48,128]{2,1,0:T(8,128)(2,1)S(1)}, u32[]{:S(2)}, u32[]{:S(2)}) collective-permute-start(bf16[16,48,128]{2,1,0:T(8,128)(2,1)S(1)} %get-tuple-element.26.p0), channel_id=1, source_target_pairs={{0,6},{2,4},{4,2},{6,0},{8,14},{10,12},{12,10},{14,8},{16,22},{18,... | collective-permute-start | bytes 589832 | tf_op jit(solution)/shard_map/ppermute | solution.py:362
  160.4 1.9 collective-permute-start.6
  162.3 4.6 %collective-permute-start.5 = (bf16[16,48,128]{2,1,0:T(8,128)(2,1)S(1)}, bf16[16,48,128]{2,1,0:T(8,128)(2,1)S(1)}, u32[]{:S(2)}, u32[]{:S(2)}) collective-permute-start(bf16[16,48,128]{2,1,0:T(8,128)(2,1)S(1)} %get-tuple-element.26.p0), channel_id=1, source_target_pairs={{0,2},{2,0},{4,6},{6,4},{8,10},{10,8},{12,14},{14,12},{16,18},{18,... | collective-permute-start | bytes 589832 | tf_op jit(solution)/shard_map/ppermute | solution.py:362
  166.9 0.1 broadcast_in_dim.3
  166.9 0.1 reshape_reshape.3.skip_ref
  167.0 0.0 all-to-all-done.1.state_ref
  167.0 0.8 shard_map.114
  167.8 5.7 %all-to-all-start.2 = ((bf16[16,16,512]{2,1,0:T(8,128)(2,1)}), bf16[16,16,512]{2,1,0:T(8,128)(2,1)S(1)}, u32[]{:S(2)}, u32[]{:S(2)}) async-start(bf16[16,16,512]{2,1,0:T(8,128)(2,1)} %shard_map.114), calls=%async_computation.2 | async-start | bytes 524288 | tf_op jit(solution)/shard_map/all_to_all | solution.py:373
  173.6 0.0 collective-permute-done.7.p3
  173.6 3.0 %collective-permute-done.6.p2 = bf16[16,48,128]{2,1,0:T(8,128)(2,1)S(1)} collective-permute-done((bf16[16,48,128]{2,1,0:T(8,128)(2,1)S(1)}, bf16[16,48,128]{2,1,0:T(8,128)(2,1)S(1)}, u32[]{:S(2)}, u32[]{:S(2)}) %collective-permute-start.6) | collective-permute-done | bytes 196640 | tf_op jit(solution)/shard_map/ppermute | solution.py:362
  176.5 0.0 collective-permute-done.5.p1
  176.5 1.4 copy-done.3
  178.0 12.0 %shard_map.113 = (f32[16,96,512]{2,1,0:T(8,128)}, bf16[16,96,256]{2,1,0:T(8,128)(2,1)S(1)}, f32[16,96,512]{2,1,0:T(8,128)}) custom-call(bf16[16,96,512]{2,1,0:T(8,128)(2,1)S(1)} %copy-done.3, bf16[16,96,256]{2,1,0:T(8,128)(2,1)S(1)} %get-tuple-element.25.in_ref, bf16[16,48,128]{2,1,0:T(8,128)(2,1)S(1)} %get-tuple-element.26.p0, ...), custom_call_target="tpu_custom_call" | custom-call | flops 10000000000 | bytes 8000000 | tf_op jit(solution)/shard_map/pallas_call | solution.py:280
  190.0 0.0 all-to-all-done.2
  190.0 1.9 copy-done.1
  191.9 4.3 %shard_map.115 = bf16[16,96,512]{2,1,0:T(8,128)(2,1)} custom-call(f32[16,96,512]{2,1,0:T(8,128)S(1)} %copy-done.1, bf16[16,96,256]{2,1,0:T(8,128)(2,1)S(1)} %get-tuple-element.28.out_ref, f32[16,96,512]{2,1,0:T(8,128)} %get-tuple-element.29.scale_ref, bf16[256,512]{1,0:T(8,128)(2,1)S(1)} %bitcast.3), custom_call_target="tpu_custom_call" | custom-call | flops 3000000000 | bytes 6000000 | tf_op jit(solution)/shard_map/pallas_call | solution.py:280
  196.2 9.8 %all-to-all-start.3 = ((bf16[16,96,512]{2,1,0:T(8,128)(2,1)}), bf16[16,96,512]{2,1,0:T(8,128)(2,1)S(1)}, u32[]{:S(2)}, u32[]{:S(2)}) async-start(bf16[16,96,512]{2,1,0:T(8,128)(2,1)} %shard_map.115), calls=%async_computation.3 | async-start | bytes 3145728 | tf_op jit(solution)/shard_map/all_to_all | solution.py:383
  206.0 0.6 reshape.15.refs_2_
  206.7 73.0 %all-to-all-done.3.refs_0_ = bf16[16,96,512]{2,1,0:T(8,128)(2,1)S(1)} async-done(((bf16[16,96,512]{2,1,0:T(8,128)(2,1)}), bf16[16,96,512]{2,1,0:T(8,128)(2,1)S(1)}, u32[]{:S(2)}, u32[]{:S(2)}) %all-to-all-start.3) | async-done | bytes 1572896 | tf_op jit(solution)/shard_map/all_to_all | solution.py:383
  279.7 1.2 copy-done.4
  280.9 4.5 %shard_map.116 = bf16[96,8192]{1,0:T(8,128)(2,1)} custom-call(bf16[16,96,512]{2,1,0:T(8,128)(2,1)} %copy-done.4, bf16[96,8192]{1,0:T(8,128)(2,1)} %refs_1_.1, bf16[1,8192]{1,0:T(2,128)(2,1)} %reshape.15.refs_2_), custom_call_target="tpu_custom_call" | custom-call | tf_op jit(solution)/shard_map/pallas_call | solution.py:385
  (14 shorter events, 0.0 us)
Async XLA Ops:
  0.9 16.5 %collective-permute-start = (bf16[8,8192]{1,0:T(8,128)(2,1)S(1)}, bf16[8,8192]{1,0:T(8,128)(2,1)S(1)}, u32[]{:S(2)}, u32[]{:S(2)}) collective-permute-start(bf16[8,8192]{1,0:T(8,128)(2,1)S(1)} %slice.6), channel_id=1, source_target_pairs={{0,2},{2,4},{4,6},{6,8},{8,10},{10,12},{12,14},{14,16},{16,18},{18... | collective-permute-start | bytes 393224 | tf_op jit(solution)/shard_map/ppermute | solution.py:313
  5.5 11.9 %collective-permute-start.1 = (bf16[8,2048]{1,0:T(8,128)(2,1)S(1)}, bf16[8,2048]{1,0:T(8,128)(2,1)S(1)}, u32[]{:S(2)}, u32[]{:S(2)}) collective-permute-start(bf16[8,2048]{1,0:T(8,128)(2,1)S(1)} %slice.7), channel_id=1, source_target_pairs={{0,2},{2,4},{4,6},{6,8},{8,10},{10,12},{12,14},{14,16},{16,18},{18... | collective-permute-start | bytes 98312 | tf_op jit(solution)/shard_map/ppermute | solution.py:313
  17.4 0.6 copy-start.5
  18.0 0.7 copy-start.6
  22.8 9.6 %copy-start.8 = (f32[8]{0:T(128)S(1)}, f32[8]{0:T(128)}, u32[]{:S(2)}) copy-start(f32[8]{0:T(128)} %param.17) | copy-start | bytes 100
  22.8 9.7 %copy-start.9 = (f32[8]{0:T(128)S(1)}, f32[8]{0:T(128)}, u32[]{:S(2)}) copy-start(f32[8]{0:T(128)} %param.18) | copy-start | bytes 100
  22.8 101.9 %all-to-all-start = ((bf16[16,104,640]{2,1,0:T(8,128)(2,1)}), bf16[16,104,640]{2,1,0:T(8,128)(2,1)S(1)}, u32[]{:S(2)}, u32[]{:S(2)}) async-start(bf16[16,104,640]{2,1,0:T(8,128)(2,1)} %shard_map.109), calls=%async_computation | async-start | bytes 4259840 | tf_op jit(solution)/shard_map/all_to_all | solution.py:340
  32.3 105.3 %copy-start = (bf16[4,512]{1,0:T(4,128)(2,1)S(1)}, bf16[4,512]{1,0:T(4,128)(2,1)}, u32[]{:S(2)}) copy-start(bf16[4,512]{1,0:T(4,128)(2,1)} %taps_ref.3) | copy-start | bytes 12292
  126.9 18.0 %collective-permute-start.4 = (bf16[16,48,128]{2,1,0:T(8,128)(2,1)S(1)}, bf16[16,48,128]{2,1,0:T(8,128)(2,1)S(1)}, u32[]{:S(2)}, u32[]{:S(2)}) collective-permute-start(bf16[16,48,128]{2,1,0:T(8,128)(2,1)S(1)} %get-tuple-element.20.p0), channel_id=1, source_target_pairs={{0,6},{2,4},{4,2},{6,0},{8,14},{10,12},{12,10},{14,8},{16,22},{18,... | collective-permute-start | bytes 589832 | tf_op jit(solution)/shard_map/ppermute | solution.py:352
  133.2 15.8 %collective-permute-start.3 = (bf16[16,48,128]{2,1,0:T(8,128)(2,1)S(1)}, bf16[16,48,128]{2,1,0:T(8,128)(2,1)S(1)}, u32[]{:S(2)}, u32[]{:S(2)}) collective-permute-start(bf16[16,48,128]{2,1,0:T(8,128)(2,1)S(1)} %get-tuple-element.20.p0), channel_id=1, source_target_pairs={{0,4},{2,6},{4,0},{6,2},{8,12},{10,14},{12,8},{14,10},{16,20},{18,... | collective-permute-start | bytes 589832 | tf_op jit(solution)/shard_map/ppermute | solution.py:352
  135.2 13.9 %collective-permute-start.2 = (bf16[16,48,128]{2,1,0:T(8,128)(2,1)S(1)}, bf16[16,48,128]{2,1,0:T(8,128)(2,1)S(1)}, u32[]{:S(2)}, u32[]{:S(2)}) collective-permute-start(bf16[16,48,128]{2,1,0:T(8,128)(2,1)S(1)} %get-tuple-element.20.p0), channel_id=1, source_target_pairs={{0,2},{2,0},{4,6},{6,4},{8,10},{10,8},{12,14},{14,12},{16,18},{18,... | collective-permute-start | bytes 589832 | tf_op jit(solution)/shard_map/ppermute | solution.py:352
  143.7 1.1 copy-start.2
  149.1 17.8 %copy-start.10 = (f32[8]{0:T(128)S(1)}, f32[8]{0:T(128)}, u32[]{:S(2)}) copy-start(f32[8]{0:T(128)} %param.19) | copy-start | bytes 100
  150.9 16.1 %all-to-all-start.1 = ((bf16[16,24,512]{2,1,0:T(8,128)(2,1)}), bf16[16,24,512]{2,1,0:T(8,128)(2,1)S(1)}, u32[]{:S(2)}, u32[]{:S(2)}) async-start(bf16[16,24,512]{2,1,0:T(8,128)(2,1)} %get-tuple-element.30), calls=%async_computation.1 | async-start | bytes 786432 | tf_op jit(solution)/shard_map/all_to_all | solution.py:371
  156.7 16.8 %collective-permute-start.7 = (bf16[16,48,128]{2,1,0:T(8,128)(2,1)S(1)}, bf16[16,48,128]{2,1,0:T(8,128)(2,1)S(1)}, u32[]{:S(2)}, u32[]{:S(2)}) collective-permute-start(bf16[16,48,128]{2,1,0:T(8,128)(2,1)S(1)} %get-tuple-element.26.p0), channel_id=1, source_target_pairs={{0,6},{2,4},{4,2},{6,0},{8,14},{10,12},{12,10},{14,8},{16,22},{18,... | collective-permute-start | bytes 589832 | tf_op jit(solution)/shard_map/ppermute | solution.py:362
  160.4 16.2 %collective-permute-start.6 = (bf16[16,48,128]{2,1,0:T(8,128)(2,1)S(1)}, bf16[16,48,128]{2,1,0:T(8,128)(2,1)S(1)}, u32[]{:S(2)}, u32[]{:S(2)}) collective-permute-start(bf16[16,48,128]{2,1,0:T(8,128)(2,1)S(1)} %get-tuple-element.26.p0), channel_id=1, source_target_pairs={{0,4},{2,6},{4,0},{6,2},{8,12},{10,14},{12,8},{14,10},{16,20},{18,... | collective-permute-start | bytes 589832 | tf_op jit(solution)/shard_map/ppermute | solution.py:362
  162.3 14.3 %collective-permute-start.5 = (bf16[16,48,128]{2,1,0:T(8,128)(2,1)S(1)}, bf16[16,48,128]{2,1,0:T(8,128)(2,1)S(1)}, u32[]{:S(2)}, u32[]{:S(2)}) collective-permute-start(bf16[16,48,128]{2,1,0:T(8,128)(2,1)S(1)} %get-tuple-element.26.p0), channel_id=1, source_target_pairs={{0,2},{2,0},{4,6},{6,4},{8,10},{10,8},{12,14},{14,12},{16,18},{18,... | collective-permute-start | bytes 589832 | tf_op jit(solution)/shard_map/ppermute | solution.py:362
  167.8 22.1 %all-to-all-start.2 = ((bf16[16,16,512]{2,1,0:T(8,128)(2,1)}), bf16[16,16,512]{2,1,0:T(8,128)(2,1)S(1)}, u32[]{:S(2)}, u32[]{:S(2)}) async-start(bf16[16,16,512]{2,1,0:T(8,128)(2,1)} %shard_map.114), calls=%async_computation.2 | async-start | bytes 524288 | tf_op jit(solution)/shard_map/all_to_all | solution.py:373
  176.5 1.4 copy-start.3
  190.0 1.9 copy-start.1
  196.2 9.8 %copy-start.7 = (bf16[8192]{0:T(1024)(128)(2,1)S(1)}, bf16[8192]{0:T(1024)(128)(2,1)}, u32[]{:S(2)}) copy-start(bf16[8192]{0:T(1024)(128)(2,1)} %param.20) | copy-start | bytes 49156
  196.2 83.5 %all-to-all-start.3 = ((bf16[16,96,512]{2,1,0:T(8,128)(2,1)}), bf16[16,96,512]{2,1,0:T(8,128)(2,1)S(1)}, u32[]{:S(2)}, u32[]{:S(2)}) async-start(bf16[16,96,512]{2,1,0:T(8,128)(2,1)} %shard_map.115), calls=%async_computation.3 | async-start | bytes 3145728 | tf_op jit(solution)/shard_map/all_to_all | solution.py:383
  279.7 1.2 copy-start.4

commit v4 on v3

--- a/solution.py
+++ b/solution.py
@@ -128,7 +128,7 @@
         c_ref[c] = jnp.where(left, turned(early), late).astype(BF16)
         return 0
 
-    lax.fori_loop(0, count, body, 0)
+    lax.fori_loop(0, count, body, 0, unroll=4)
 
 
 def unpacked(pieces):
@@ -163,7 +163,7 @@
         weighted_ref[c] = (x.astype(F32) * scale).astype(BF16)
         return 0
 
-    lax.fori_loop(0, count, body, 0)
+    lax.fori_loop(0, count, body, 0, unroll=4)
 
 
 def state_kernel(p0, p1, p2, p3, weighted_ref, logs_ref, state_ref, in_ref):
@@ -243,7 +243,7 @@
         )
         return 0
 
-    lax.fori_loop(0, count, body, 0)
+    lax.fori_loop(0, count, body, 0, unroll=4)
 
 
 def carry_kernel(y_ref, out_ref, scale_ref, incoming_ref, sum_ref):
@@ -310,7 +310,8 @@
     bias, rate = step_bias.reshape(heads, 1), log_rate.reshape(heads, 1)
 
     route = [(i, i + 1) for i in range(seq * ring - 1)]
-    x_tail, c_tail = lax.ppermute((ssm_input[rows - HALO :], coupling[rows - HALO :]), ("seq", "fsdp"), route)
+    last_rows = jnp.concatenate([ssm_input[rows - HALO :], coupling[rows - HALO :]], axis=1)
+    tails = lax.ppermute(last_rows, ("seq", "fsdp"), route)
     group_width = channels // GROUPS
 
     def columns_of(count, size, first):
@@ -329,14 +330,14 @@
             columns_of(rows, STATE, GROUPS),
             same(*step_input.shape),
             columns_of(HALO, group_width, 0),
-            columns_of(HALO, STATE, 0),
-            columns_of(HALO, STATE, GROUPS),
+            columns_of(HALO, STATE, channels // STATE),
+            columns_of(HALO, STATE, channels // STATE + GROUPS),
             same(*conv_coupling.shape),
         ],
         out_specs=pl.BlockSpec((ring // GROUPS, HALO + rows, width + LANES), lambda g: (g, 0, 0)),
         scratch_shapes=[pltpu.VMEM((LANES, LANES), F32)],
         compiler_params=wide,
-    )(ssm_input, coupling, coupling, step_input, x_tail, c_tail, c_tail, conv_coupling)
+    )(ssm_input, coupling, coupling, step_input, tails, tails, tails, conv_coupling)
     message = lax.all_to_all(message, "fsdp", 0, 0)
 
     senders = 2 * (place // 4) + place % 4 // 2 + jnp.array([0, 2 * GROUPS], jnp.int32)
@@ -393,7 +394,7 @@
         ],
         out_specs=pl.BlockSpec((rows, group_width), lambda g: (0, g)),
         scratch_shapes=[pltpu.VMEM((rows, group_width), F32)],
-        compiler_params=wide,
+        compiler_params=params,
     )(y, gate_input, norm_gain.reshape(1, -1))
 
 

time: 286 us -> 279 us (0.976)
  waiting for transfers between devices: 180 us -> 188 us
  Pallas kernels: 35.9 us -> 29.1 us
  starting transfers between devices: 59.3 us -> 53.3 us
    pallas_call x6, Pallas kernels: 27.3 us -> 22.3 us  [call(): pl.pallas_call(kernel, out_shape=outs, in_specs=specs, out_specs=jax.tree...]
    all_to_all x1, waiting for transfers between devices: 92.1 us -> 96.4 us  [local(): message = lax.all_to_all(message, 'fsdp', 0, 0)]
    ppermute x2 -> x1, waiting for transfers between devices: 8.1 us -> 12.2 us  [local(): tails = lax.ppermute(last_rows, ('seq', 'fsdp'), route)]
    ppermute x2 -> x1, starting transfers between devices: 7.64 us -> 3.83 us  [local(): tails = lax.ppermute(last_rows, ('seq', 'fsdp'), route)]
    unnamed x22 -> x20, local copies, waits for them, and re-layouts: 6.92 us -> 5.13 us
  transfers between devices with their start and end apart: 12 -> 11, of which waited for: 5 -> 5; matrix products, arithmetic and copies ran while one was open for 1% -> 0% of each run, Pallas kernels for 7% -> 5%
where the time goes in v4:
time: 279 us; the launch traced here: 278 us
  waiting for transfers between devices  188 us (67%)
  starting transfers between devices  53.3 us (19%)
  Pallas kernels  29.1 us (10%)
  local copies, waits for them, and re-layouts  7.13 us (3%)
    all_to_all x1, waiting for transfers between devices, local(): message = lax.all_to_all(message, 'fsdp', 0, 0)  96.4 us
    all_to_all x1, waiting for transfers between devices, local(): y = lax.all_to_all(y, 'fsdp', 0, 0)  74.3 us
    pallas_call x6, Pallas kernels, call(): pl.pallas_call(kernel, out_shape=outs, in_specs=specs, out_specs=jax.tree...  22.3 us
    ppermute x1, waiting for transfers between devices, local(): tails = lax.ppermute(last_rows, ('seq', 'fsdp'), route)  12.2 us
    ppermute x3, starting transfers between devices, local(): lax.ppermute(own_in, 'fsdp', [(i, i ^ d) for i in range(ring)])  10.1 us
    ppermute x3, starting transfers between devices, local(): lax.ppermute(own_out, 'fsdp', [(i, i ^ d) for i in range(ring)])  10.1 us
    all_to_all x1, starting transfers between devices, local(): y = lax.all_to_all(y, 'fsdp', 0, 0)  9.35 us
    all_to_all x1, starting transfers between devices, local(): message = lax.all_to_all(message, 'fsdp', 0, 0)  8.34 us
  transfers between devices with their start and end apart: 11, of which 5 were waited for; matrix products, arithmetic and copies ran while one was open for 0% of the time, Pallas kernels for 5%

profile of v4, /device:TPU:6, one launch (start us, length us, event | category | flops | bytes accessed | tf_op | source)
XLA Modules:
  0.0 278.0 jit_solution(5100591464788035044)
XLA Ops:
  0.0 0.8 slice.7
  0.8 0.9 slice.6
  1.7 3.8 %collective-permute-start = (bf16[8,10240]{1,0:T(8,128)(2,1)S(1)}, bf16[8,10240]{1,0:T(8,128)(2,1)S(1)}, u32[]{:S(2)}, u32[]{:S(2)}) collective-permute-start(bf16[8,10240]{1,0:T(8,128)(2,1)S(1)} %pad_maximum_fusion), channel_id=1, source_target_pairs={{0,2},{2,4},{4,6},{6,8},{8,10},{10,12},{12,14},{14,16},{16,18},{18... | collective-permute-start | bytes 491528 | tf_op jit(solution)/shard_map/ppermute | solution.py:314
  5.5 12.2 %collective-permute-done.x_tail_ref.b_tail_ref.c_tail_ref = bf16[8,10240]{1,0:T(8,128)(2,1)S(1)} collective-permute-done((bf16[8,10240]{1,0:T(8,128)(2,1)S(1)}, bf16[8,10240]{1,0:T(8,128)(2,1)S(1)}, u32[]{:S(2)}, u32[]{:S(2)}) %collective-permute-start) | collective-permute-done | bytes 163872 | tf_op jit(solution)/shard_map/ppermute | solution.py:314
  17.7 0.7 copy-done.5
  18.4 4.1 %shard_map.109 = bf16[16,104,640]{2,1,0:T(8,128)(2,1)} custom-call(bf16[96,8192]{1,0:T(8,128)(2,1)} %x_ref.1, bf16[96,2048]{1,0:T(8,128)(2,1)} %c_ref.1, bf16[96,2048]{1,0:T(8,128)(2,1)} %c_ref.1, bf16[96,128]{1,0:T(8,128)(2,1)} %steps_ref.1, bf16[8,10240]{1,0:T(8,128)(2,1)} %copy-done.5, bf16[8,10240]{1,0:T(8,128)(2,1)} %copy-done.5, ...), custom_call_target="tpu_custom_call" | custom-call | tf_op jit(solution)/shard_map/pallas_call | solution.py:323
  22.5 8.3 %all-to-all-start = ((bf16[16,104,640]{2,1,0:T(8,128)(2,1)}), bf16[16,104,640]{2,1,0:T(8,128)(2,1)S(1)}, u32[]{:S(2)}, u32[]{:S(2)}) async-start(bf16[16,104,640]{2,1,0:T(8,128)(2,1)} %shard_map.109), calls=%async_computation | async-start | bytes 4259840 | tf_op jit(solution)/shard_map/all_to_all | solution.py:341
  30.9 0.0 copy-start.1
  30.9 0.0 copy-done.7
  30.9 0.1 copy.12.bias_ref
  31.0 0.0 copy-done.8
  31.0 0.1 copy.13.log_rate_ref
  31.1 96.4 %all-to-all-done.m_ref = bf16[16,104,640]{2,1,0:T(8,128)(2,1)S(1)} async-done(((bf16[16,104,640]{2,1,0:T(8,128)(2,1)}), bf16[16,104,640]{2,1,0:T(8,128)(2,1)S(1)}, u32[]{:S(2)}, u32[]{:S(2)}) %all-to-all-start) | async-done | bytes 2129952 | tf_op jit(solution)/shard_map/all_to_all | solution.py:341
  127.6 1.3 shard_map.110
  128.9 2.5 collective-permute-start.3
  131.4 1.9 collective-permute-start.2
  133.3 5.7 %collective-permute-start.1 = (bf16[16,48,128]{2,1,0:T(8,128)(2,1)S(1)}, bf16[16,48,128]{2,1,0:T(8,128)(2,1)S(1)}, u32[]{:S(2)}, u32[]{:S(2)}) collective-permute-start(bf16[16,48,128]{2,1,0:T(8,128)(2,1)S(1)} %get-tuple-element.20.p0), channel_id=1, source_target_pairs={{0,2},{2,0},{4,6},{6,4},{8,10},{10,8},{12,14},{14,12},{16,18},{18,... | collective-permute-start | bytes 589832 | tf_op jit(solution)/shard_map/ppermute | solution.py:353
  139.0 0.0 copy-done.1
  139.0 4.8 %shard_map.111 = (bf16[16,96,512]{2,1,0:T(8,128)(2,1)S(1)}, bf16[16,96,512]{2,1,0:T(8,128)(2,1)S(1)}, f32[8,512]{1,0:T(8,128)S(1)}) custom-call(bf16[16,104,640]{2,1,0:T(8,128)(2,1)S(1)} %all-to-all-done.m_ref, bf16[4,512]{1,0:T(4,128)(2,1)S(1)} %copy-done.1, f32[16,8,128]{2,1,0:T(8,128)S(1)} %get-tuple-element.18.steps_ref, f32[8,1]{1,0:T(8,128)S(1)} %copy.12.bias_ref, ...), custom_call_target="tpu_custom_call" | custom-call | flops 6000000000 | bytes 6000000 | tf_op jit(solution)/shard_map/pallas_call | solution.py:280
  143.8 0.0 copy-start.3
  143.8 1.1 copy-done.3
  145.0 0.0 collective-permute-done.3.p3
  145.0 2.0 collective-permute-done.2.p2
  147.0 0.0 collective-permute-done.1.p1
  147.0 1.9 shard_map.112
  148.8 5.8 %all-to-all-start.1 = ((bf16[16,24,512]{2,1,0:T(8,128)(2,1)}), bf16[16,24,512]{2,1,0:T(8,128)(2,1)S(1)}, u32[]{:S(2)}, u32[]{:S(2)}) async-start(bf16[16,24,512]{2,1,0:T(8,128)(2,1)} %get-tuple-element.30), calls=%async_computation.1 | async-start | bytes 786432 | tf_op jit(solution)/shard_map/all_to_all | solution.py:372
  154.6 3.9 %collective-permute-start.6 = (bf16[16,48,128]{2,1,0:T(8,128)(2,1)S(1)}, bf16[16,48,128]{2,1,0:T(8,128)(2,1)S(1)}, u32[]{:S(2)}, u32[]{:S(2)}) collective-permute-start(bf16[16,48,128]{2,1,0:T(8,128)(2,1)S(1)} %get-tuple-element.26.p0), channel_id=1, source_target_pairs={{0,6},{2,4},{4,2},{6,0},{8,14},{10,12},{12,10},{14,8},{16,22},{18,... | collective-permute-start | bytes 589832 | tf_op jit(solution)/shard_map/ppermute | solution.py:363
  158.5 1.9 collective-permute-start.5
  160.5 4.3 %collective-permute-start.4 = (bf16[16,48,128]{2,1,0:T(8,128)(2,1)S(1)}, bf16[16,48,128]{2,1,0:T(8,128)(2,1)S(1)}, u32[]{:S(2)}, u32[]{:S(2)}) collective-permute-start(bf16[16,48,128]{2,1,0:T(8,128)(2,1)S(1)} %get-tuple-element.26.p0), channel_id=1, source_target_pairs={{0,2},{2,0},{4,6},{6,4},{8,10},{10,8},{12,14},{14,12},{16,18},{18,... | collective-permute-start | bytes 589832 | tf_op jit(solution)/shard_map/ppermute | solution.py:363
  164.8 0.0 copy-done.9
  164.8 0.1 broadcast_in_dim.3
  164.8 0.1 reshape_reshape.3.skip_ref
  164.9 0.0 all-to-all-done.1.state_ref
  164.9 0.8 shard_map.114
  165.7 5.7 %all-to-all-start.2 = ((bf16[16,16,512]{2,1,0:T(8,128)(2,1)}), bf16[16,16,512]{2,1,0:T(8,128)(2,1)S(1)}, u32[]{:S(2)}, u32[]{:S(2)}) async-start(bf16[16,16,512]{2,1,0:T(8,128)(2,1)} %shard_map.114), calls=%async_computation.2 | async-start | bytes 524288 | tf_op jit(solution)/shard_map/all_to_all | solution.py:374
  171.5 0.0 collective-permute-done.6.p3
  171.5 3.3 %collective-permute-done.5.p2 = bf16[16,48,128]{2,1,0:T(8,128)(2,1)S(1)} collective-permute-done((bf16[16,48,128]{2,1,0:T(8,128)(2,1)S(1)}, bf16[16,48,128]{2,1,0:T(8,128)(2,1)S(1)}, u32[]{:S(2)}, u32[]{:S(2)}) %collective-permute-start.5) | collective-permute-done | bytes 196640 | tf_op jit(solution)/shard_map/ppermute | solution.py:363
  174.7 0.0 collective-permute-done.4.p1
  174.7 1.4 copy-done.4
  176.1 9.2 %shard_map.113 = (f32[16,96,512]{2,1,0:T(8,128)}, bf16[16,96,256]{2,1,0:T(8,128)(2,1)S(1)}, f32[16,96,512]{2,1,0:T(8,128)}) custom-call(bf16[16,96,512]{2,1,0:T(8,128)(2,1)S(1)} %copy-done.4, bf16[16,96,256]{2,1,0:T(8,128)(2,1)S(1)} %get-tuple-element.25.in_ref, bf16[16,48,128]{2,1,0:T(8,128)(2,1)S(1)} %get-tuple-element.26.p0, ...), custom_call_target="tpu_custom_call" | custom-call | flops 10000000000 | bytes 8000000 | tf_op jit(solution)/shard_map/pallas_call | solution.py:280
  185.3 0.0 all-to-all-done.2
  185.3 1.9 copy-done.2
  187.2 4.3 %shard_map.115 = bf16[16,96,512]{2,1,0:T(8,128)(2,1)} custom-call(f32[16,96,512]{2,1,0:T(8,128)S(1)} %copy-done.2, bf16[16,96,256]{2,1,0:T(8,128)(2,1)S(1)} %get-tuple-element.28.out_ref, f32[16,96,512]{2,1,0:T(8,128)} %get-tuple-element.29.scale_ref, bf16[256,512]{1,0:T(8,128)(2,1)S(1)} %bitcast.3), custom_call_target="tpu_custom_call" | custom-call | flops 3000000000 | bytes 6000000 | tf_op jit(solution)/shard_map/pallas_call | solution.py:280
  191.6 9.3 %all-to-all-start.3 = ((bf16[16,96,512]{2,1,0:T(8,128)(2,1)}), bf16[16,96,512]{2,1,0:T(8,128)(2,1)S(1)}, u32[]{:S(2)}, u32[]{:S(2)}) async-start(bf16[16,96,512]{2,1,0:T(8,128)(2,1)} %shard_map.115), calls=%async_computation.3 | async-start | bytes 3145728 | tf_op jit(solution)/shard_map/all_to_all | solution.py:384
  200.9 0.0 copy-done.6
  200.9 74.3 %all-to-all-done.3.refs_0_ = bf16[16,96,512]{2,1,0:T(8,128)(2,1)S(1)} async-done(((bf16[16,96,512]{2,1,0:T(8,128)(2,1)}), bf16[16,96,512]{2,1,0:T(8,128)(2,1)S(1)}, u32[]{:S(2)}, u32[]{:S(2)}) %all-to-all-start.3) | async-done | bytes 1572896 | tf_op jit(solution)/shard_map/all_to_all | solution.py:384
  275.3 0.0 copy-done
  275.3 2.7 shard_map.116
  (11 shorter events, 0.0 us)
Async XLA Ops:
  1.7 16.0 %collective-permute-start = (bf16[8,10240]{1,0:T(8,128)(2,1)S(1)}, bf16[8,10240]{1,0:T(8,128)(2,1)S(1)}, u32[]{:S(2)}, u32[]{:S(2)}) collective-permute-start(bf16[8,10240]{1,0:T(8,128)(2,1)S(1)} %pad_maximum_fusion), channel_id=1, source_target_pairs={{0,2},{2,4},{4,6},{6,8},{8,10},{10,12},{12,14},{14,16},{16,18},{18... | collective-permute-start | bytes 491528 | tf_op jit(solution)/shard_map/ppermute | solution.py:314
  17.7 0.7 copy-start.5
  22.5 8.4 %copy-start.7 = (f32[8]{0:T(128)S(1)}, f32[8]{0:T(128)}, u32[]{:S(2)}) copy-start(f32[8]{0:T(128)} %param.17) | copy-start | bytes 100
  22.5 8.5 %copy-start.8 = (f32[8]{0:T(128)S(1)}, f32[8]{0:T(128)}, u32[]{:S(2)}) copy-start(f32[8]{0:T(128)} %param.18) | copy-start | bytes 100
  22.5 105.0 %all-to-all-start = ((bf16[16,104,640]{2,1,0:T(8,128)(2,1)}), bf16[16,104,640]{2,1,0:T(8,128)(2,1)S(1)}, u32[]{:S(2)}, u32[]{:S(2)}) async-start(bf16[16,104,640]{2,1,0:T(8,128)(2,1)} %shard_map.109), calls=%async_computation | async-start | bytes 4259840 | tf_op jit(solution)/shard_map/all_to_all | solution.py:341
  30.9 108.1 %copy-start.1 = (bf16[4,512]{1,0:T(4,128)(2,1)S(1)}, bf16[4,512]{1,0:T(4,128)(2,1)}, u32[]{:S(2)}) copy-start(bf16[4,512]{1,0:T(4,128)(2,1)} %taps_ref.3) | copy-start | bytes 12292
  128.9 16.1 %collective-permute-start.3 = (bf16[16,48,128]{2,1,0:T(8,128)(2,1)S(1)}, bf16[16,48,128]{2,1,0:T(8,128)(2,1)S(1)}, u32[]{:S(2)}, u32[]{:S(2)}) collective-permute-start(bf16[16,48,128]{2,1,0:T(8,128)(2,1)S(1)} %get-tuple-element.20.p0), channel_id=1, source_target_pairs={{0,6},{2,4},{4,2},{6,0},{8,14},{10,12},{12,10},{14,8},{16,22},{18,... | collective-permute-start | bytes 589832 | tf_op jit(solution)/shard_map/ppermute | solution.py:353
  131.4 15.6 %collective-permute-start.2 = (bf16[16,48,128]{2,1,0:T(8,128)(2,1)S(1)}, bf16[16,48,128]{2,1,0:T(8,128)(2,1)S(1)}, u32[]{:S(2)}, u32[]{:S(2)}) collective-permute-start(bf16[16,48,128]{2,1,0:T(8,128)(2,1)S(1)} %get-tuple-element.20.p0), channel_id=1, source_target_pairs={{0,4},{2,6},{4,0},{6,2},{8,12},{10,14},{12,8},{14,10},{16,20},{18,... | collective-permute-start | bytes 589832 | tf_op jit(solution)/shard_map/ppermute | solution.py:353
  133.3 13.6 %collective-permute-start.1 = (bf16[16,48,128]{2,1,0:T(8,128)(2,1)S(1)}, bf16[16,48,128]{2,1,0:T(8,128)(2,1)S(1)}, u32[]{:S(2)}, u32[]{:S(2)}) collective-permute-start(bf16[16,48,128]{2,1,0:T(8,128)(2,1)S(1)} %get-tuple-element.20.p0), channel_id=1, source_target_pairs={{0,2},{2,0},{4,6},{6,4},{8,10},{10,8},{12,14},{14,12},{16,18},{18,... | collective-permute-start | bytes 589832 | tf_op jit(solution)/shard_map/ppermute | solution.py:353
  143.8 1.1 copy-start.3
  147.0 17.8 %copy-start.9 = (f32[8]{0:T(128)S(1)}, f32[8]{0:T(128)}, u32[]{:S(2)}) copy-start(f32[8]{0:T(128)} %param.19) | copy-start | bytes 100
  148.8 16.1 %all-to-all-start.1 = ((bf16[16,24,512]{2,1,0:T(8,128)(2,1)}), bf16[16,24,512]{2,1,0:T(8,128)(2,1)S(1)}, u32[]{:S(2)}, u32[]{:S(2)}) async-start(bf16[16,24,512]{2,1,0:T(8,128)(2,1)} %get-tuple-element.30), calls=%async_computation.1 | async-start | bytes 786432 | tf_op jit(solution)/shard_map/all_to_all | solution.py:372
  154.6 16.8 %collective-permute-start.6 = (bf16[16,48,128]{2,1,0:T(8,128)(2,1)S(1)}, bf16[16,48,128]{2,1,0:T(8,128)(2,1)S(1)}, u32[]{:S(2)}, u32[]{:S(2)}) collective-permute-start(bf16[16,48,128]{2,1,0:T(8,128)(2,1)S(1)} %get-tuple-element.26.p0), channel_id=1, source_target_pairs={{0,6},{2,4},{4,2},{6,0},{8,14},{10,12},{12,10},{14,8},{16,22},{18,... | collective-permute-start | bytes 589832 | tf_op jit(solution)/shard_map/ppermute | solution.py:363
  158.5 16.2 %collective-permute-start.5 = (bf16[16,48,128]{2,1,0:T(8,128)(2,1)S(1)}, bf16[16,48,128]{2,1,0:T(8,128)(2,1)S(1)}, u32[]{:S(2)}, u32[]{:S(2)}) collective-permute-start(bf16[16,48,128]{2,1,0:T(8,128)(2,1)S(1)} %get-tuple-element.26.p0), channel_id=1, source_target_pairs={{0,4},{2,6},{4,0},{6,2},{8,12},{10,14},{12,8},{14,10},{16,20},{18,... | collective-permute-start | bytes 589832 | tf_op jit(solution)/shard_map/ppermute | solution.py:363
  160.5 14.3 %collective-permute-start.4 = (bf16[16,48,128]{2,1,0:T(8,128)(2,1)S(1)}, bf16[16,48,128]{2,1,0:T(8,128)(2,1)S(1)}, u32[]{:S(2)}, u32[]{:S(2)}) collective-permute-start(bf16[16,48,128]{2,1,0:T(8,128)(2,1)S(1)} %get-tuple-element.26.p0), channel_id=1, source_target_pairs={{0,2},{2,0},{4,6},{6,4},{8,10},{10,8},{12,14},{14,12},{16,18},{18,... | collective-permute-start | bytes 589832 | tf_op jit(solution)/shard_map/ppermute | solution.py:363
  165.7 19.6 %all-to-all-start.2 = ((bf16[16,16,512]{2,1,0:T(8,128)(2,1)}), bf16[16,16,512]{2,1,0:T(8,128)(2,1)S(1)}, u32[]{:S(2)}, u32[]{:S(2)}) async-start(bf16[16,16,512]{2,1,0:T(8,128)(2,1)} %shard_map.114), calls=%async_computation.2 | async-start | bytes 524288 | tf_op jit(solution)/shard_map/all_to_all | solution.py:374
  174.7 1.4 copy-start.4
  185.3 1.9 copy-start.2
  191.5 9.4 %copy-start.6 = (bf16[8192]{0:T(1024)(128)(2,1)S(1)}, bf16[8192]{0:T(1024)(128)(2,1)}, u32[]{:S(2)}) copy-start(bf16[8192]{0:T(1024)(128)(2,1)} %param.20) | copy-start | bytes 49156
  191.6 83.7 %copy-start = (bf16[96,8192]{1,0:T(8,128)(2,1)S(1)}, bf16[96,8192]{1,0:T(8,128)(2,1)}, u32[]{:S(2)}) copy-start(bf16[96,8192]{1,0:T(8,128)(2,1)} %refs_1_.1) | copy-start | bytes 4718596
  191.6 83.7 %all-to-all-start.3 = ((bf16[16,96,512]{2,1,0:T(8,128)(2,1)}), bf16[16,96,512]{2,1,0:T(8,128)(2,1)S(1)}, u32[]{:S(2)}, u32[]{:S(2)}) async-start(bf16[16,96,512]{2,1,0:T(8,128)(2,1)} %shard_map.115), calls=%async_computation.3 | async-start | bytes 3145728 | tf_op jit(solution)/shard_map/all_to_all | solution.py:384

commit v5 on v4

--- a/solution.py
+++ b/solution.py
@@ -359,8 +359,9 @@
         (message, conv_input, steps, bias, rate),
         (6000000000, 6000000),
     )
-    own_out, weighted = lax.optimization_barrier((own_out, weighted))
-    out_pieces = [own_out] + [lax.ppermute(own_out, "fsdp", [(i, i ^ d) for i in range(ring)]) for d in range(1, 4)]
+    nearest = lax.ppermute(own_out, "fsdp", [(i, i ^ 1) for i in range(ring)])
+    own_out, nearest, weighted = lax.optimization_barrier((own_out, nearest, weighted))
+    out_pieces = [own_out, nearest] + [lax.ppermute(own_out, "fsdp", [(i, i ^ d) for i in range(ring)]) for d in (2, 3)]
     share = STATE // seq
     state, read_in = call(
         state_kernel,
@@ -380,7 +381,20 @@
         (x, read_in, *out_pieces, steps, bias, rate, jnp.repeat(skip_gain, HEAD_DIM).reshape(1, width)),
         (10000000000, 8000000),
     )
-    y = call(carry_kernel, struct(blocks, BF16), [], (y, read_out, scale, incoming), (3000000000, 6000000))
+    some = ring // 4
+    y = pl.pallas_call(
+        carry_kernel,
+        grid=(4,),
+        out_shape=struct(blocks, BF16),
+        in_specs=[
+            pl.BlockSpec((some, rows, width), lambda i: (i, 0, 0)),
+            pl.BlockSpec((some, rows, STATE), lambda i: (i, 0, 0)),
+            pl.BlockSpec((some, rows, width), lambda i: (i, 0, 0)),
+            same(STATE, width),
+        ],
+        out_specs=pl.BlockSpec((some, rows, width), lambda i: (i, 0, 0)),
+        compiler_params=wide,
+    )(y, read_out, scale, incoming)
     y = lax.all_to_all(y, "fsdp", 0, 0)
 
     return pl.pallas_call(

time: 279 us -> 282 us (1.011)
  waiting for transfers between devices: 188 us -> 195 us
  starting transfers between devices: 53.3 us -> 49.4 us
    pallas_call x0 -> x1, Pallas kernels: none -> 5.31 us  [local(): pl.pallas_call(carry_kernel, grid=(4,), out_shape=struct(blocks, BF16), i...]
    ppermute x3 -> x2, starting transfers between devices: 10.1 us -> 5.52 us  [local(): lax.ppermute(own_out, 'fsdp', [(i, i ^ d) for i in range(ring)])]
    pallas_call x6 -> x5, Pallas kernels: 22.3 us -> 17.9 us  [call(): pl.pallas_call(kernel, out_shape=outs, in_specs=specs, out_specs=jax.tree...]
    ppermute x0 -> x1, waiting for transfers between devices: none -> 4.08 us  [local(): nearest = lax.ppermute(own_out, 'fsdp', [(i, i ^ 1) for i in range(ring)])]
    ppermute x3 -> x2, waiting for transfers between devices: 3.28 us -> 6.97 us  [local(): lax.ppermute(own_out, 'fsdp', [(i, i ^ d) for i in range(ring)])]
  transfers between devices with their start and end apart: 11 -> 11, of which waited for: 5 -> 6; matrix products, arithmetic and copies ran while one was open for 0% -> 0% of each run, Pallas kernels for 5% -> 5%
where the time goes in v5:
time: 282 us; the launch traced here: 281 us
  waiting for transfers between devices  195 us (69%)
  starting transfers between devices  49.4 us (18%)
  Pallas kernels  30 us (11%)
  local copies, waits for them, and re-layouts  6.82 us (2%)
    all_to_all x1, waiting for transfers between devices, local(): message = lax.all_to_all(message, 'fsdp', 0, 0)  96.4 us
    all_to_all x1, waiting for transfers between devices, local(): y = lax.all_to_all(y, 'fsdp', 0, 0)  73.6 us
    pallas_call x5, Pallas kernels, call(): pl.pallas_call(kernel, out_shape=outs, in_specs=specs, out_specs=jax.tree...  17.9 us
    ppermute x1, waiting for transfers between devices, local(): tails = lax.ppermute(last_rows, ('seq', 'fsdp'), route)  12.2 us
    ppermute x3, starting transfers between devices, local(): lax.ppermute(own_in, 'fsdp', [(i, i ^ d) for i in range(ring)])  10.1 us
    all_to_all x1, starting transfers between devices, local(): message = lax.all_to_all(message, 'fsdp', 0, 0)  8.34 us
    all_to_all x1, starting transfers between devices, local(): y = lax.all_to_all(y, 'fsdp', 0, 0)  8.32 us
    ppermute x2, waiting for transfers between devices, local(): lax.ppermute(own_out, 'fsdp', [(i, i ^ d) for i in range(ring)])  6.97 us
  transfers between devices with their start and end apart: 11, of which 6 were waited for; matrix products, arithmetic and copies ran while one was open for 0% of the time, Pallas kernels for 5%

profile of v5, /device:TPU:6, one launch (start us, length us, event | category | flops | bytes accessed | tf_op | source)
XLA Modules:
  0.0 281.3 jit_solution(1473634238618025784)
XLA Ops:
  0.0 0.8 slice.7
  0.8 0.9 slice.6
  1.7 3.8 %collective-permute-start = (bf16[8,10240]{1,0:T(8,128)(2,1)S(1)}, bf16[8,10240]{1,0:T(8,128)(2,1)S(1)}, u32[]{:S(2)}, u32[]{:S(2)}) collective-permute-start(bf16[8,10240]{1,0:T(8,128)(2,1)S(1)} %pad_maximum_fusion), channel_id=1, source_target_pairs={{0,2},{2,4},{4,6},{6,8},{8,10},{10,12},{12,14},{14,16},{16,18},{18... | collective-permute-start | bytes 491528 | tf_op jit(solution)/shard_map/ppermute | solution.py:314
  5.5 12.2 %collective-permute-done.x_tail_ref.b_tail_ref.c_tail_ref = bf16[8,10240]{1,0:T(8,128)(2,1)S(1)} collective-permute-done((bf16[8,10240]{1,0:T(8,128)(2,1)S(1)}, bf16[8,10240]{1,0:T(8,128)(2,1)S(1)}, u32[]{:S(2)}, u32[]{:S(2)}) %collective-permute-start) | collective-permute-done | bytes 163872 | tf_op jit(solution)/shard_map/ppermute | solution.py:314
  17.7 0.7 copy-done.5
  18.4 4.1 %shard_map.109 = bf16[16,104,640]{2,1,0:T(8,128)(2,1)} custom-call(bf16[96,8192]{1,0:T(8,128)(2,1)} %x_ref.1, bf16[96,2048]{1,0:T(8,128)(2,1)} %c_ref.1, bf16[96,2048]{1,0:T(8,128)(2,1)} %c_ref.1, bf16[96,128]{1,0:T(8,128)(2,1)} %steps_ref.1, bf16[8,10240]{1,0:T(8,128)(2,1)} %copy-done.5, bf16[8,10240]{1,0:T(8,128)(2,1)} %copy-done.5, ...), custom_call_target="tpu_custom_call" | custom-call | tf_op jit(solution)/shard_map/pallas_call | solution.py:323
  22.5 8.3 %all-to-all-start = ((bf16[16,104,640]{2,1,0:T(8,128)(2,1)}), bf16[16,104,640]{2,1,0:T(8,128)(2,1)S(1)}, u32[]{:S(2)}, u32[]{:S(2)}) async-start(bf16[16,104,640]{2,1,0:T(8,128)(2,1)} %shard_map.109), calls=%async_computation | async-start | bytes 4259840 | tf_op jit(solution)/shard_map/all_to_all | solution.py:341
  30.9 0.0 copy-start.2
  30.9 0.0 copy-done.8
  31.0 0.1 copy.12.bias_ref
  31.0 0.0 copy-done.9
  31.0 0.1 copy.13.log_rate_ref
  31.1 96.4 %all-to-all-done.m_ref = bf16[16,104,640]{2,1,0:T(8,128)(2,1)S(1)} async-done(((bf16[16,104,640]{2,1,0:T(8,128)(2,1)}), bf16[16,104,640]{2,1,0:T(8,128)(2,1)S(1)}, u32[]{:S(2)}, u32[]{:S(2)}) %all-to-all-start) | async-done | bytes 2129952 | tf_op jit(solution)/shard_map/all_to_all | solution.py:341
  127.6 1.3 shard_map.110
  128.9 2.5 collective-permute-start.3
  131.4 1.9 collective-permute-start.2
  133.4 5.7 %collective-permute-start.1 = (bf16[16,48,128]{2,1,0:T(8,128)(2,1)S(1)}, bf16[16,48,128]{2,1,0:T(8,128)(2,1)S(1)}, u32[]{:S(2)}, u32[]{:S(2)}) collective-permute-start(bf16[16,48,128]{2,1,0:T(8,128)(2,1)S(1)} %get-tuple-element.21.p0), channel_id=1, source_target_pairs={{0,2},{2,0},{4,6},{6,4},{8,10},{10,8},{12,14},{14,12},{16,18},{18,... | collective-permute-start | bytes 589832 | tf_op jit(solution)/shard_map/ppermute | solution.py:353
  139.0 1.9 collective-permute-start.4
  140.9 0.0 copy-done.2
  141.0 4.8 %shard_map.111 = (bf16[16,96,512]{2,1,0:T(8,128)(2,1)S(1)}, bf16[16,96,512]{2,1,0:T(8,128)(2,1)S(1)}, f32[8,512]{1,0:T(8,128)S(1)}) custom-call(bf16[16,104,640]{2,1,0:T(8,128)(2,1)S(1)} %all-to-all-done.m_ref, bf16[4,512]{1,0:T(4,128)(2,1)S(1)} %copy-done.2, f32[16,8,128]{2,1,0:T(8,128)S(1)} %get-tuple-element.19.steps_ref, f32[8,1]{1,0:T(8,128)S(1)} %copy.12.bias_ref, ...), custom_call_target="tpu_custom_call" | custom-call | flops 6000000000 | bytes 6000000 | tf_op jit(solution)/shard_map/pallas_call | solution.py:280
  145.8 0.0 copy-start.3
  145.8 1.1 copy-done.3
  146.9 4.1 %collective-permute-done.4.p1 = bf16[16,48,128]{2,1,0:T(8,128)(2,1)S(1)} collective-permute-done((bf16[16,48,128]{2,1,0:T(8,128)(2,1)S(1)}, bf16[16,48,128]{2,1,0:T(8,128)(2,1)S(1)}, u32[]{:S(2)}, u32[]{:S(2)}) %collective-permute-start.4) | collective-permute-done | bytes 196640 | tf_op jit(solution)/shard_map/ppermute | solution.py:362
  151.0 0.0 collective-permute-done.3.p3
  151.0 0.0 collective-permute-done.2.p2
  151.0 0.0 collective-permute-done.1.p1
  151.0 0.0 copy-start.10
  151.0 1.9 shard_map.112
  152.9 5.8 %all-to-all-start.1 = ((bf16[16,24,512]{2,1,0:T(8,128)(2,1)}), bf16[16,24,512]{2,1,0:T(8,128)(2,1)S(1)}, u32[]{:S(2)}, u32[]{:S(2)}) async-start(bf16[16,24,512]{2,1,0:T(8,128)(2,1)} %get-tuple-element.32), calls=%async_computation.1 | async-start | bytes 786432 | tf_op jit(solution)/shard_map/all_to_all | solution.py:373
  158.7 3.6 %collective-permute-start.6 = (bf16[16,48,128]{2,1,0:T(8,128)(2,1)S(1)}, bf16[16,48,128]{2,1,0:T(8,128)(2,1)S(1)}, u32[]{:S(2)}, u32[]{:S(2)}) collective-permute-start(bf16[16,48,128]{2,1,0:T(8,128)(2,1)S(1)} %get-tuple-element.27.p0), channel_id=1, source_target_pairs={{0,6},{2,4},{4,2},{6,0},{8,14},{10,12},{12,10},{14,8},{16,22},{18,... | collective-permute-start | bytes 589832 | tf_op jit(solution)/shard_map/ppermute | solution.py:364
  162.3 1.9 collective-permute-start.5
  164.2 0.0 copy-done.10
  164.2 0.1 broadcast_in_dim.3
  164.3 0.1 reshape_reshape.3.skip_ref
  164.4 1.5 all-to-all-done.1.state_ref
  165.8 0.8 shard_map.114
  166.6 5.5 %all-to-all-start.2 = ((bf16[16,16,512]{2,1,0:T(8,128)(2,1)}), bf16[16,16,512]{2,1,0:T(8,128)(2,1)S(1)}, u32[]{:S(2)}, u32[]{:S(2)}) async-start(bf16[16,16,512]{2,1,0:T(8,128)(2,1)} %shard_map.114), calls=%async_computation.2 | async-start | bytes 524288 | tf_op jit(solution)/shard_map/all_to_all | solution.py:375
  172.2 0.0 collective-permute-done.6.p3
  172.2 7.0 %collective-permute-done.5.p2 = bf16[16,48,128]{2,1,0:T(8,128)(2,1)S(1)} collective-permute-done((bf16[16,48,128]{2,1,0:T(8,128)(2,1)S(1)}, bf16[16,48,128]{2,1,0:T(8,128)(2,1)S(1)}, u32[]{:S(2)}, u32[]{:S(2)}) %collective-permute-start.5) | collective-permute-done | bytes 196640 | tf_op jit(solution)/shard_map/ppermute | solution.py:364
  179.1 1.4 copy-done.4
  180.5 9.2 %shard_map.113 = (f32[16,96,512]{2,1,0:T(8,128)}, bf16[16,96,256]{2,1,0:T(8,128)(2,1)S(1)}, f32[16,96,512]{2,1,0:T(8,128)}) custom-call(bf16[16,96,512]{2,1,0:T(8,128)(2,1)S(1)} %copy-done.4, bf16[16,96,256]{2,1,0:T(8,128)(2,1)S(1)} %get-tuple-element.26.in_ref, bf16[16,48,128]{2,1,0:T(8,128)(2,1)S(1)} %get-tuple-element.27.p0, ...), custom_call_target="tpu_custom_call" | custom-call | flops 10000000000 | bytes 8000000 | tf_op jit(solution)/shard_map/pallas_call | solution.py:280
  189.7 0.9 copy-done.1
  190.6 0.0 all-to-all-done.2
  190.6 0.7 copy-done.6
  191.3 5.3 %shard_map.115 = bf16[16,96,512]{2,1,0:T(8,128)(2,1)} custom-call(f32[16,96,512]{2,1,0:T(8,128)} %get-tuple-element.29.y_ref, bf16[16,96,256]{2,1,0:T(8,128)(2,1)} %copy-done.1, f32[16,96,512]{2,1,0:T(8,128)} %get-tuple-element.31.scale_ref, bf16[256,512]{1,0:T(8,128)(2,1)} %bitcast.3), custom_call_target="tpu_custom_call" | custom-call | tf_op jit(solution)/shard_map/pallas_call | solution.py:385
  196.6 8.3 %all-to-all-start.3 = ((bf16[16,96,512]{2,1,0:T(8,128)(2,1)}), bf16[16,96,512]{2,1,0:T(8,128)(2,1)S(1)}, u32[]{:S(2)}, u32[]{:S(2)}) async-start(bf16[16,96,512]{2,1,0:T(8,128)(2,1)} %shard_map.115), calls=%async_computation.3 | async-start | bytes 3145728 | tf_op jit(solution)/shard_map/all_to_all | solution.py:398
  205.0 73.6 %all-to-all-done.3.refs_0_ = bf16[16,96,512]{2,1,0:T(8,128)(2,1)S(1)} async-done(((bf16[16,96,512]{2,1,0:T(8,128)(2,1)}), bf16[16,96,512]{2,1,0:T(8,128)(2,1)S(1)}, u32[]{:S(2)}, u32[]{:S(2)}) %all-to-all-start.3) | async-done | bytes 1572896 | tf_op jit(solution)/shard_map/all_to_all | solution.py:398
  278.6 2.7 shard_map.116
  (13 shorter events, 0.1 us)
Async XLA Ops:
  1.7 16.0 %collective-permute-start = (bf16[8,10240]{1,0:T(8,128)(2,1)S(1)}, bf16[8,10240]{1,0:T(8,128)(2,1)S(1)}, u32[]{:S(2)}, u32[]{:S(2)}) collective-permute-start(bf16[8,10240]{1,0:T(8,128)(2,1)S(1)} %pad_maximum_fusion), channel_id=1, source_target_pairs={{0,2},{2,4},{4,6},{6,8},{8,10},{10,12},{12,14},{14,16},{16,18},{18... | collective-permute-start | bytes 491528 | tf_op jit(solution)/shard_map/ppermute | solution.py:314
  17.7 0.7 copy-start.5
  22.5 8.4 %copy-start.8 = (f32[8]{0:T(128)S(1)}, f32[8]{0:T(128)}, u32[]{:S(2)}) copy-start(f32[8]{0:T(128)} %param.17) | copy-start | bytes 100
  22.5 8.5 %copy-start.9 = (f32[8]{0:T(128)S(1)}, f32[8]{0:T(128)}, u32[]{:S(2)}) copy-start(f32[8]{0:T(128)} %param.18) | copy-start | bytes 100
  22.5 105.0 %all-to-all-start = ((bf16[16,104,640]{2,1,0:T(8,128)(2,1)}), bf16[16,104,640]{2,1,0:T(8,128)(2,1)S(1)}, u32[]{:S(2)}, u32[]{:S(2)}) async-start(bf16[16,104,640]{2,1,0:T(8,128)(2,1)} %shard_map.109), calls=%async_computation | async-start | bytes 4259840 | tf_op jit(solution)/shard_map/all_to_all | solution.py:341
  30.9 110.1 %copy-start.2 = (bf16[4,512]{1,0:T(4,128)(2,1)S(1)}, bf16[4,512]{1,0:T(4,128)(2,1)}, u32[]{:S(2)}) copy-start(bf16[4,512]{1,0:T(4,128)(2,1)} %taps_ref.3) | copy-start | bytes 12292
  128.9 22.1 %collective-permute-start.3 = (bf16[16,48,128]{2,1,0:T(8,128)(2,1)S(1)}, bf16[16,48,128]{2,1,0:T(8,128)(2,1)S(1)}, u32[]{:S(2)}, u32[]{:S(2)}) collective-permute-start(bf16[16,48,128]{2,1,0:T(8,128)(2,1)S(1)} %get-tuple-element.21.p0), channel_id=1, source_target_pairs={{0,6},{2,4},{4,2},{6,0},{8,14},{10,12},{12,10},{14,8},{16,22},{18,... | collective-permute-start | bytes 589832 | tf_op jit(solution)/shard_map/ppermute | solution.py:353
  131.4 19.6 %collective-permute-start.2 = (bf16[16,48,128]{2,1,0:T(8,128)(2,1)S(1)}, bf16[16,48,128]{2,1,0:T(8,128)(2,1)S(1)}, u32[]{:S(2)}, u32[]{:S(2)}) collective-permute-start(bf16[16,48,128]{2,1,0:T(8,128)(2,1)S(1)} %get-tuple-element.21.p0), channel_id=1, source_target_pairs={{0,4},{2,6},{4,0},{6,2},{8,12},{10,14},{12,8},{14,10},{16,20},{18,... | collective-permute-start | bytes 589832 | tf_op jit(solution)/shard_map/ppermute | solution.py:353
  133.4 17.6 %collective-permute-start.1 = (bf16[16,48,128]{2,1,0:T(8,128)(2,1)S(1)}, bf16[16,48,128]{2,1,0:T(8,128)(2,1)S(1)}, u32[]{:S(2)}, u32[]{:S(2)}) collective-permute-start(bf16[16,48,128]{2,1,0:T(8,128)(2,1)S(1)} %get-tuple-element.21.p0), channel_id=1, source_target_pairs={{0,2},{2,0},{4,6},{6,4},{8,10},{10,8},{12,14},{14,12},{16,18},{18,... | collective-permute-start | bytes 589832 | tf_op jit(solution)/shard_map/ppermute | solution.py:353
  139.0 12.0 %collective-permute-start.4 = (bf16[16,48,128]{2,1,0:T(8,128)(2,1)S(1)}, bf16[16,48,128]{2,1,0:T(8,128)(2,1)S(1)}, u32[]{:S(2)}, u32[]{:S(2)}) collective-permute-start(bf16[16,48,128]{2,1,0:T(8,128)(2,1)S(1)} %get-tuple-element.27.p0), channel_id=1, source_target_pairs={{0,2},{2,0},{4,6},{6,4},{8,10},{10,8},{12,14},{14,12},{16,18},{18,... | collective-permute-start | bytes 589832 | tf_op jit(solution)/shard_map/ppermute | solution.py:362
  145.8 1.1 copy-start.3
  151.0 13.2 %copy-start.10 = (f32[8]{0:T(128)S(1)}, f32[8]{0:T(128)}, u32[]{:S(2)}) copy-start(f32[8]{0:T(128)} %param.19) | copy-start | bytes 100
  152.9 13.0 %all-to-all-start.1 = ((bf16[16,24,512]{2,1,0:T(8,128)(2,1)}), bf16[16,24,512]{2,1,0:T(8,128)(2,1)S(1)}, u32[]{:S(2)}, u32[]{:S(2)}) async-start(bf16[16,24,512]{2,1,0:T(8,128)(2,1)} %get-tuple-element.32), calls=%async_computation.1 | async-start | bytes 786432 | tf_op jit(solution)/shard_map/all_to_all | solution.py:373
  158.7 13.5 %collective-permute-start.6 = (bf16[16,48,128]{2,1,0:T(8,128)(2,1)S(1)}, bf16[16,48,128]{2,1,0:T(8,128)(2,1)S(1)}, u32[]{:S(2)}, u32[]{:S(2)}) collective-permute-start(bf16[16,48,128]{2,1,0:T(8,128)(2,1)S(1)} %get-tuple-element.27.p0), channel_id=1, source_target_pairs={{0,6},{2,4},{4,2},{6,0},{8,14},{10,12},{12,10},{14,8},{16,22},{18,... | collective-permute-start | bytes 589832 | tf_op jit(solution)/shard_map/ppermute | solution.py:364
  162.3 16.9 %collective-permute-start.5 = (bf16[16,48,128]{2,1,0:T(8,128)(2,1)S(1)}, bf16[16,48,128]{2,1,0:T(8,128)(2,1)S(1)}, u32[]{:S(2)}, u32[]{:S(2)}) collective-permute-start(bf16[16,48,128]{2,1,0:T(8,128)(2,1)S(1)} %get-tuple-element.27.p0), channel_id=1, source_target_pairs={{0,4},{2,6},{4,0},{6,2},{8,12},{10,14},{12,8},{14,10},{16,20},{18,... | collective-permute-start | bytes 589832 | tf_op jit(solution)/shard_map/ppermute | solution.py:364
  166.6 24.0 %all-to-all-start.2 = ((bf16[16,16,512]{2,1,0:T(8,128)(2,1)}), bf16[16,16,512]{2,1,0:T(8,128)(2,1)S(1)}, u32[]{:S(2)}, u32[]{:S(2)}) async-start(bf16[16,16,512]{2,1,0:T(8,128)(2,1)} %shard_map.114), calls=%async_computation.2 | async-start | bytes 524288 | tf_op jit(solution)/shard_map/all_to_all | solution.py:375
  179.1 1.4 copy-start.4
  189.7 0.9 copy-start.1
  190.6 0.7 copy-start.6
  196.6 8.3 %copy-start.7 = (bf16[8192]{0:T(1024)(128)(2,1)S(1)}, bf16[8192]{0:T(1024)(128)(2,1)}, u32[]{:S(2)}) copy-start(bf16[8192]{0:T(1024)(128)(2,1)} %param.20) | copy-start | bytes 49156
  196.6 82.0 %copy-start = (bf16[96,8192]{1,0:T(8,128)(2,1)S(1)}, bf16[96,8192]{1,0:T(8,128)(2,1)}, u32[]{:S(2)}) copy-start(bf16[96,8192]{1,0:T(8,128)(2,1)} %refs_1_.1) | copy-start | bytes 4718596
  196.6 82.0 %all-to-all-start.3 = ((bf16[16,96,512]{2,1,0:T(8,128)(2,1)}), bf16[16,96,512]{2,1,0:T(8,128)(2,1)S(1)}, u32[]{:S(2)}, u32[]{:S(2)}) async-start(bf16[16,96,512]{2,1,0:T(8,128)(2,1)} %shard_map.115), calls=%async_computation.3 | async-start | bytes 3145728 | tf_op jit(solution)/shard_map/all_to_all | solution.py:398

commit v6 on v4

--- a/solution.py
+++ b/solution.py
@@ -15,7 +15,7 @@
 F32 = jnp.float32
 BF16 = jnp.bfloat16
 exact = lax.Precision.HIGHEST
-params = pltpu.CompilerParams(vmem_limit_bytes=48 * 2**20)
+params = pltpu.CompilerParams(vmem_limit_bytes=50 * 2**20)
 wide = pltpu.CompilerParams(vmem_limit_bytes=60 * 2**20)
 
 
@@ -243,7 +243,7 @@
         )
         return 0
 
-    lax.fori_loop(0, count, body, 0, unroll=4)
+    lax.fori_loop(0, count, body, 0, unroll=8)
 
 
 def carry_kernel(y_ref, out_ref, scale_ref, incoming_ref, sum_ref):

time: 279 us -> 277 us (level)
  local copies, waits for them, and re-layouts: 7.13 us -> 4.11 us
    unnamed x20, local copies, waits for them, and re-layouts: 5.13 us -> 2.11 us
  transfers between devices with their start and end apart: 11 -> 11, of which waited for: 5 -> 5; matrix products, arithmetic and copies ran while one was open for 0% -> 0% of each run, Pallas kernels for 5% -> 6%
where the time goes in v6:
time: 277 us
  waiting for transfers between devices  188 us (68%)
  starting transfers between devices  53.3 us (19%)
  Pallas kernels  31.1 us (11%)
  local copies, waits for them, and re-layouts  4.11 us (1%)
    all_to_all x1, waiting for transfers between devices, local(): message = lax.all_to_all(message, 'fsdp', 0, 0)  96.4 us
    all_to_all x1, waiting for transfers between devices, local(): y = lax.all_to_all(y, 'fsdp', 0, 0)  74.3 us
    pallas_call x6, Pallas kernels, call(): pl.pallas_call(kernel, out_shape=outs, in_specs=specs, out_specs=jax.tree...  24.3 us
    ppermute x1, waiting for transfers between devices, local(): tails = lax.ppermute(last_rows, ('seq', 'fsdp'), route)  12.2 us
    ppermute x3, starting transfers between devices, local(): lax.ppermute(own_in, 'fsdp', [(i, i ^ d) for i in range(ring)])  10.1 us
    ppermute x3, starting transfers between devices, local(): lax.ppermute(own_out, 'fsdp', [(i, i ^ d) for i in range(ring)])  10.1 us
    all_to_all x1, starting transfers between devices, local(): y = lax.all_to_all(y, 'fsdp', 0, 0)  9.38 us
    all_to_all x1, starting transfers between devices, local(): message = lax.all_to_all(message, 'fsdp', 0, 0)  8.34 us
  transfers between devices with their start and end apart: 11, of which 5 were waited for; matrix products, arithmetic and copies ran while one was open for 0% of the time, Pallas kernels for 6%

profile of v6, /device:TPU:6, one launch (start us, length us, event | category | flops | bytes accessed | tf_op | source)
XLA Modules:
  0.0 276.6 jit_solution(8856776116554703714)
XLA Ops:
  0.0 0.8 slice.7
  0.8 0.9 slice.6
  1.7 3.8 %collective-permute-start = (bf16[8,10240]{1,0:T(8,128)(2,1)S(1)}, bf16[8,10240]{1,0:T(8,128)(2,1)S(1)}, u32[]{:S(2)}, u32[]{:S(2)}) collective-permute-start(bf16[8,10240]{1,0:T(8,128)(2,1)S(1)} %pad_maximum_fusion), channel_id=1, source_target_pairs={{0,2},{2,4},{4,6},{6,8},{8,10},{10,12},{12,14},{14,16},{16,18},{18... | collective-permute-start | bytes 491528 | tf_op jit(solution)/shard_map/ppermute | solution.py:314
  5.5 12.2 %collective-permute-done.x_tail_ref.b_tail_ref.c_tail_ref = bf16[8,10240]{1,0:T(8,128)(2,1)S(1)} collective-permute-done((bf16[8,10240]{1,0:T(8,128)(2,1)S(1)}, bf16[8,10240]{1,0:T(8,128)(2,1)S(1)}, u32[]{:S(2)}, u32[]{:S(2)}) %collective-permute-start) | collective-permute-done | bytes 163872 | tf_op jit(solution)/shard_map/ppermute | solution.py:314
  17.7 0.7 copy-done.5
  18.4 4.1 %shard_map.109 = bf16[16,104,640]{2,1,0:T(8,128)(2,1)} custom-call(bf16[96,8192]{1,0:T(8,128)(2,1)} %x_ref.1, bf16[96,2048]{1,0:T(8,128)(2,1)} %c_ref.1, bf16[96,2048]{1,0:T(8,128)(2,1)} %c_ref.1, bf16[96,128]{1,0:T(8,128)(2,1)} %steps_ref.1, bf16[8,10240]{1,0:T(8,128)(2,1)} %copy-done.5, bf16[8,10240]{1,0:T(8,128)(2,1)} %copy-done.5, ...), custom_call_target="tpu_custom_call" | custom-call | tf_op jit(solution)/shard_map/pallas_call | solution.py:323
  22.5 8.3 %all-to-all-start = ((bf16[16,104,640]{2,1,0:T(8,128)(2,1)}), bf16[16,104,640]{2,1,0:T(8,128)(2,1)S(1)}, u32[]{:S(2)}, u32[]{:S(2)}) async-start(bf16[16,104,640]{2,1,0:T(8,128)(2,1)} %shard_map.109), calls=%async_computation | async-start | bytes 4259840 | tf_op jit(solution)/shard_map/all_to_all | solution.py:341
  30.9 0.0 copy-start.2
  30.9 0.0 copy-done.7
  30.9 0.1 copy.12.bias_ref
  31.0 0.0 copy-done.8
  31.0 0.1 copy.13.log_rate_ref
  31.1 96.4 %all-to-all-done.m_ref = bf16[16,104,640]{2,1,0:T(8,128)(2,1)S(1)} async-done(((bf16[16,104,640]{2,1,0:T(8,128)(2,1)}), bf16[16,104,640]{2,1,0:T(8,128)(2,1)S(1)}, u32[]{:S(2)}, u32[]{:S(2)}) %all-to-all-start) | async-done | bytes 2129952 | tf_op jit(solution)/shard_map/all_to_all | solution.py:341
  127.6 1.3 shard_map.110
  128.9 2.5 collective-permute-start.3
  131.4 1.9 collective-permute-start.2
  133.3 5.7 %collective-permute-start.1 = (bf16[16,48,128]{2,1,0:T(8,128)(2,1)S(1)}, bf16[16,48,128]{2,1,0:T(8,128)(2,1)S(1)}, u32[]{:S(2)}, u32[]{:S(2)}) collective-permute-start(bf16[16,48,128]{2,1,0:T(8,128)(2,1)S(1)} %get-tuple-element.20.p0), channel_id=1, source_target_pairs={{0,2},{2,0},{4,6},{6,4},{8,10},{10,8},{12,14},{14,12},{16,18},{18,... | collective-permute-start | bytes 589832 | tf_op jit(solution)/shard_map/ppermute | solution.py:353
  139.0 0.0 copy-done
  139.0 0.0 copy-done.2
  139.0 6.4 %shard_map.111 = (bf16[16,96,512]{2,1,0:T(8,128)(2,1)S(1)}, bf16[16,96,512]{2,1,0:T(8,128)(2,1)S(1)}, f32[8,512]{1,0:T(8,128)S(1)}) custom-call(bf16[16,104,640]{2,1,0:T(8,128)(2,1)} %copy-done, bf16[4,512]{1,0:T(4,128)(2,1)S(1)} %copy-done.2, f32[16,8,128]{2,1,0:T(8,128)S(1)} %get-tuple-element.18.steps_ref, f32[8,1]{1,0:T(8,128)S(1)} %copy.12.bias_ref, ...), custom_call_target="tpu_custom_call" | custom-call | flops 6000000000 | bytes 6000000 | tf_op jit(solution)/shard_map/pallas_call | solution.py:280
  145.4 0.0 copy-start.3
  145.4 0.0 collective-permute-done.3.p3
  145.5 1.5 collective-permute-done.2.p2
  147.0 0.0 collective-permute-done.1.p1
  147.0 1.9 shard_map.112
  148.8 0.0 copy-done.3
  148.8 5.8 %all-to-all-start.1 = ((bf16[16,24,512]{2,1,0:T(8,128)(2,1)}), bf16[16,24,512]{2,1,0:T(8,128)(2,1)S(1)}, u32[]{:S(2)}, u32[]{:S(2)}) async-start(bf16[16,24,512]{2,1,0:T(8,128)(2,1)} %get-tuple-element.30), calls=%async_computation.1 | async-start | bytes 786432 | tf_op jit(solution)/shard_map/all_to_all | solution.py:372
  154.6 3.9 %collective-permute-start.6 = (bf16[16,48,128]{2,1,0:T(8,128)(2,1)S(1)}, bf16[16,48,128]{2,1,0:T(8,128)(2,1)S(1)}, u32[]{:S(2)}, u32[]{:S(2)}) collective-permute-start(bf16[16,48,128]{2,1,0:T(8,128)(2,1)S(1)} %get-tuple-element.26.p0), channel_id=1, source_target_pairs={{0,6},{2,4},{4,2},{6,0},{8,14},{10,12},{12,10},{14,8},{16,22},{18,... | collective-permute-start | bytes 589832 | tf_op jit(solution)/shard_map/ppermute | solution.py:363
  158.5 1.9 collective-permute-start.5
  160.5 4.3 %collective-permute-start.4 = (bf16[16,48,128]{2,1,0:T(8,128)(2,1)S(1)}, bf16[16,48,128]{2,1,0:T(8,128)(2,1)S(1)}, u32[]{:S(2)}, u32[]{:S(2)}) collective-permute-start(bf16[16,48,128]{2,1,0:T(8,128)(2,1)S(1)} %get-tuple-element.26.p0), channel_id=1, source_target_pairs={{0,2},{2,0},{4,6},{6,4},{8,10},{10,8},{12,14},{14,12},{16,18},{18,... | collective-permute-start | bytes 589832 | tf_op jit(solution)/shard_map/ppermute | solution.py:363
  164.8 0.0 copy-done.9
  164.8 0.1 broadcast_in_dim.3
  164.8 0.1 reshape_reshape.3.skip_ref
  164.9 0.0 all-to-all-done.1.state_ref
  164.9 0.8 shard_map.114
  165.7 5.7 %all-to-all-start.2 = ((bf16[16,16,512]{2,1,0:T(8,128)(2,1)}), bf16[16,16,512]{2,1,0:T(8,128)(2,1)S(1)}, u32[]{:S(2)}, u32[]{:S(2)}) async-start(bf16[16,16,512]{2,1,0:T(8,128)(2,1)} %shard_map.114), calls=%async_computation.2 | async-start | bytes 524288 | tf_op jit(solution)/shard_map/all_to_all | solution.py:374
  171.5 0.0 collective-permute-done.6.p3
  171.5 3.3 %collective-permute-done.5.p2 = bf16[16,48,128]{2,1,0:T(8,128)(2,1)S(1)} collective-permute-done((bf16[16,48,128]{2,1,0:T(8,128)(2,1)S(1)}, bf16[16,48,128]{2,1,0:T(8,128)(2,1)S(1)}, u32[]{:S(2)}, u32[]{:S(2)}) %collective-permute-start.5) | collective-permute-done | bytes 196640 | tf_op jit(solution)/shard_map/ppermute | solution.py:363
  174.7 0.0 collective-permute-done.4.p1
  174.7 1.4 copy-done.4
  176.1 8.7 %shard_map.113 = (f32[16,96,512]{2,1,0:T(8,128)}, bf16[16,96,256]{2,1,0:T(8,128)(2,1)S(1)}, f32[16,96,512]{2,1,0:T(8,128)}) custom-call(bf16[16,96,512]{2,1,0:T(8,128)(2,1)S(1)} %copy-done.4, bf16[16,96,256]{2,1,0:T(8,128)(2,1)S(1)} %get-tuple-element.25.in_ref, bf16[16,48,128]{2,1,0:T(8,128)(2,1)S(1)} %get-tuple-element.26.p0, ...), custom_call_target="tpu_custom_call" | custom-call | flops 10000000000 | bytes 8000000 | tf_op jit(solution)/shard_map/pallas_call | solution.py:280
  184.8 0.0 all-to-all-done.2
  184.8 5.3 %shard_map.115 = bf16[16,96,512]{2,1,0:T(8,128)(2,1)} custom-call(f32[16,96,512]{2,1,0:T(8,128)} %get-tuple-element.27.y_ref, bf16[16,96,256]{2,1,0:T(8,128)(2,1)S(1)} %get-tuple-element.28.out_ref, f32[16,96,512]{2,1,0:T(8,128)} %get-tuple-element.29.scale_ref, bf16[256,512]{1,0:T(8,128)(2,1)S(1)} %bitcast.3), custom_call_target="tpu_custom_call" | custom-call | flops 3000000000 | bytes 6000000 | tf_op jit(solution)/shard_map/pallas_call | solution.py:280
  190.1 9.4 %all-to-all-start.3 = ((bf16[16,96,512]{2,1,0:T(8,128)(2,1)}), bf16[16,96,512]{2,1,0:T(8,128)(2,1)S(1)}, u32[]{:S(2)}, u32[]{:S(2)}) async-start(bf16[16,96,512]{2,1,0:T(8,128)(2,1)} %shard_map.115), calls=%async_computation.3 | async-start | bytes 3145728 | tf_op jit(solution)/shard_map/all_to_all | solution.py:384
  199.5 0.0 copy-done.6
  199.6 74.3 %all-to-all-done.3.refs_0_ = bf16[16,96,512]{2,1,0:T(8,128)(2,1)S(1)} async-done(((bf16[16,96,512]{2,1,0:T(8,128)(2,1)}), bf16[16,96,512]{2,1,0:T(8,128)(2,1)S(1)}, u32[]{:S(2)}, u32[]{:S(2)}) %all-to-all-start.3) | async-done | bytes 1572896 | tf_op jit(solution)/shard_map/all_to_all | solution.py:384
  273.9 0.0 copy-done.1
  273.9 2.7 shard_map.116
  (11 shorter events, 0.1 us)
Async XLA Ops:
  1.7 16.0 %collective-permute-start = (bf16[8,10240]{1,0:T(8,128)(2,1)S(1)}, bf16[8,10240]{1,0:T(8,128)(2,1)S(1)}, u32[]{:S(2)}, u32[]{:S(2)}) collective-permute-start(bf16[8,10240]{1,0:T(8,128)(2,1)S(1)} %pad_maximum_fusion), channel_id=1, source_target_pairs={{0,2},{2,4},{4,6},{6,8},{8,10},{10,12},{12,14},{14,16},{16,18},{18... | collective-permute-start | bytes 491528 | tf_op jit(solution)/shard_map/ppermute | solution.py:314
  17.7 0.7 copy-start.5
  22.5 8.4 %copy-start.7 = (f32[8]{0:T(128)S(1)}, f32[8]{0:T(128)}, u32[]{:S(2)}) copy-start(f32[8]{0:T(128)} %param.17) | copy-start | bytes 100
  22.5 8.5 %copy-start.8 = (f32[8]{0:T(128)S(1)}, f32[8]{0:T(128)}, u32[]{:S(2)}) copy-start(f32[8]{0:T(128)} %param.18) | copy-start | bytes 100
  22.5 105.0 %all-to-all-start = ((bf16[16,104,640]{2,1,0:T(8,128)(2,1)}), bf16[16,104,640]{2,1,0:T(8,128)(2,1)S(1)}, u32[]{:S(2)}, u32[]{:S(2)}) async-start(bf16[16,104,640]{2,1,0:T(8,128)(2,1)} %shard_map.109), calls=%async_computation | async-start | bytes 4259840 | tf_op jit(solution)/shard_map/all_to_all | solution.py:341
  30.9 108.1 %copy-start.2 = (bf16[4,512]{1,0:T(4,128)(2,1)S(1)}, bf16[4,512]{1,0:T(4,128)(2,1)}, u32[]{:S(2)}) copy-start(bf16[4,512]{1,0:T(4,128)(2,1)} %taps_ref.3) | copy-start | bytes 12292
  127.6 11.5 %copy-start = (bf16[16,104,640]{2,1,0:T(8,128)(2,1)}, bf16[16,104,640]{2,1,0:T(8,128)(2,1)S(1)}, u32[]{:S(2)}) copy-start(bf16[16,104,640]{2,1,0:T(8,128)(2,1)S(1)} %all-to-all-done.m_ref) | copy-start | bytes 6389764
  128.9 16.6 %collective-permute-start.3 = (bf16[16,48,128]{2,1,0:T(8,128)(2,1)S(1)}, bf16[16,48,128]{2,1,0:T(8,128)(2,1)S(1)}, u32[]{:S(2)}, u32[]{:S(2)}) collective-permute-start(bf16[16,48,128]{2,1,0:T(8,128)(2,1)S(1)} %get-tuple-element.20.p0), channel_id=1, source_target_pairs={{0,6},{2,4},{4,2},{6,0},{8,14},{10,12},{12,10},{14,8},{16,22},{18,... | collective-permute-start | bytes 589832 | tf_op jit(solution)/shard_map/ppermute | solution.py:353
  131.4 15.6 %collective-permute-start.2 = (bf16[16,48,128]{2,1,0:T(8,128)(2,1)S(1)}, bf16[16,48,128]{2,1,0:T(8,128)(2,1)S(1)}, u32[]{:S(2)}, u32[]{:S(2)}) collective-permute-start(bf16[16,48,128]{2,1,0:T(8,128)(2,1)S(1)} %get-tuple-element.20.p0), channel_id=1, source_target_pairs={{0,4},{2,6},{4,0},{6,2},{8,12},{10,14},{12,8},{14,10},{16,20},{18,... | collective-permute-start | bytes 589832 | tf_op jit(solution)/shard_map/ppermute | solution.py:353
  133.3 13.6 %collective-permute-start.1 = (bf16[16,48,128]{2,1,0:T(8,128)(2,1)S(1)}, bf16[16,48,128]{2,1,0:T(8,128)(2,1)S(1)}, u32[]{:S(2)}, u32[]{:S(2)}) collective-permute-start(bf16[16,48,128]{2,1,0:T(8,128)(2,1)S(1)} %get-tuple-element.20.p0), channel_id=1, source_target_pairs={{0,2},{2,0},{4,6},{6,4},{8,10},{10,8},{12,14},{14,12},{16,18},{18,... | collective-permute-start | bytes 589832 | tf_op jit(solution)/shard_map/ppermute | solution.py:353
  145.4 3.4 %copy-start.3 = (bf16[16,96,512]{2,1,0:T(8,128)(2,1)}, bf16[16,96,512]{2,1,0:T(8,128)(2,1)S(1)}, u32[]{:S(2)}) copy-start(bf16[16,96,512]{2,1,0:T(8,128)(2,1)S(1)} %get-tuple-element.19.x_ref) | copy-start | bytes 4718596
  147.0 17.8 %copy-start.9 = (f32[8]{0:T(128)S(1)}, f32[8]{0:T(128)}, u32[]{:S(2)}) copy-start(f32[8]{0:T(128)} %param.19) | copy-start | bytes 100
  148.8 16.1 %all-to-all-start.1 = ((bf16[16,24,512]{2,1,0:T(8,128)(2,1)}), bf16[16,24,512]{2,1,0:T(8,128)(2,1)S(1)}, u32[]{:S(2)}, u32[]{:S(2)}) async-start(bf16[16,24,512]{2,1,0:T(8,128)(2,1)} %get-tuple-element.30), calls=%async_computation.1 | async-start | bytes 786432 | tf_op jit(solution)/shard_map/all_to_all | solution.py:372
  154.6 16.8 %collective-permute-start.6 = (bf16[16,48,128]{2,1,0:T(8,128)(2,1)S(1)}, bf16[16,48,128]{2,1,0:T(8,128)(2,1)S(1)}, u32[]{:S(2)}, u32[]{:S(2)}) collective-permute-start(bf16[16,48,128]{2,1,0:T(8,128)(2,1)S(1)} %get-tuple-element.26.p0), channel_id=1, source_target_pairs={{0,6},{2,4},{4,2},{6,0},{8,14},{10,12},{12,10},{14,8},{16,22},{18,... | collective-permute-start | bytes 589832 | tf_op jit(solution)/shard_map/ppermute | solution.py:363
  158.5 16.2 %collective-permute-start.5 = (bf16[16,48,128]{2,1,0:T(8,128)(2,1)S(1)}, bf16[16,48,128]{2,1,0:T(8,128)(2,1)S(1)}, u32[]{:S(2)}, u32[]{:S(2)}) collective-permute-start(bf16[16,48,128]{2,1,0:T(8,128)(2,1)S(1)} %get-tuple-element.26.p0), channel_id=1, source_target_pairs={{0,4},{2,6},{4,0},{6,2},{8,12},{10,14},{12,8},{14,10},{16,20},{18,... | collective-permute-start | bytes 589832 | tf_op jit(solution)/shard_map/ppermute | solution.py:363
  160.5 14.3 %collective-permute-start.4 = (bf16[16,48,128]{2,1,0:T(8,128)(2,1)S(1)}, bf16[16,48,128]{2,1,0:T(8,128)(2,1)S(1)}, u32[]{:S(2)}, u32[]{:S(2)}) collective-permute-start(bf16[16,48,128]{2,1,0:T(8,128)(2,1)S(1)} %get-tuple-element.26.p0), channel_id=1, source_target_pairs={{0,2},{2,0},{4,6},{6,4},{8,10},{10,8},{12,14},{14,12},{16,18},{18,... | collective-permute-start | bytes 589832 | tf_op jit(solution)/shard_map/ppermute | solution.py:363
  165.7 19.1 %all-to-all-start.2 = ((bf16[16,16,512]{2,1,0:T(8,128)(2,1)}), bf16[16,16,512]{2,1,0:T(8,128)(2,1)S(1)}, u32[]{:S(2)}, u32[]{:S(2)}) async-start(bf16[16,16,512]{2,1,0:T(8,128)(2,1)} %shard_map.114), calls=%async_computation.2 | async-start | bytes 524288 | tf_op jit(solution)/shard_map/all_to_all | solution.py:374
  174.7 1.4 copy-start.4
  190.1 9.4 %copy-start.6 = (bf16[8192]{0:T(1024)(128)(2,1)S(1)}, bf16[8192]{0:T(1024)(128)(2,1)}, u32[]{:S(2)}) copy-start(bf16[8192]{0:T(1024)(128)(2,1)} %param.20) | copy-start | bytes 49156
  190.1 83.8 %copy-start.1 = (bf16[96,8192]{1,0:T(8,128)(2,1)S(1)}, bf16[96,8192]{1,0:T(8,128)(2,1)}, u32[]{:S(2)}) copy-start(bf16[96,8192]{1,0:T(8,128)(2,1)} %refs_1_.1) | copy-start | bytes 4718596
  190.1 83.8 %all-to-all-start.3 = ((bf16[16,96,512]{2,1,0:T(8,128)(2,1)}), bf16[16,96,512]{2,1,0:T(8,128)(2,1)S(1)}, u32[]{:S(2)}, u32[]{:S(2)}) async-start(bf16[16,96,512]{2,1,0:T(8,128)(2,1)} %shard_map.115), calls=%async_computation.3 | async-start | bytes 3145728 | tf_op jit(solution)/shard_map/all_to_all | solution.py:384
